TPU v7x, 128 devices: a whole 4x4x4 slice. The times are simulated.
128 devices in a mesh: sec: 8 (over z, x_lo), tp: 16 (over x_hi, y, core).
Axes of the slice: x: 4 (x_hi: 2, x_lo: 2; x = x_hi * 2 + x_lo), y: 4, z: 4, core: 2. Of those that a mesh axis runs over, the one named last changes fastest.
Arguments:
- rollout: bfloat16 [16384, 8192], P('sec', 'tp'), may hold values from -96 to 96
- lengths: int32 [8, 8], P('sec'), may hold values from 1 to 256, as said below
- target: int32 [8, 8], P('sec'), may hold values from 0 to 7, as said below
- w_query: bfloat16 [8, 8192, 8192], P('sec', None, 'tp'), may hold values from -0.0625 to 0.0625
- w_keyval: bfloat16 [8, 8192, 2048], P('sec', None, 'tp'), may hold values from -0.0625 to 0.0625
- w_out: bfloat16 [8, 8192, 8192], P('sec', 'tp'), may hold values from -0.0625 to 0.0625
Outputs:
- attended: bfloat16 [8192, 8192], P('sec', 'tp')
Inputs may be any that keep to these rules, and one draw needn't show every extreme that they name: `lengths`: rollout group s holds its responses one after another from the first row of its block in the order of r; the rest of the block is not read. Every response holds at most 256 tokens and some response exactly 256. The responses that go to one section group hold at most 1024 tokens together, and some section group exactly 1024. `target`: every rollout group sends exactly one response to each section group.
All inputs are finite; a program needn't handle non-finite values.
Results may differ from a plain program's by a relative error of at most 0.012.
The roundings to bfloat16 on the way count: a program that leaves them out, or rounds other values in their place, can miss the bound.
Values may be sent and summed in bfloat16 or wider, within the bound.
No kernel may reach another device: no remote copies, remote signals or barrier semaphores. Data moves between devices by JAX's collectives and lax.ppermute only.
A program may use at most 128 MiB of HBM per device.

v0:
```python
import math

import jax
import jax.numpy as jnp
from jax import lax
from jax.sharding import PartitionSpec as P

HQ = 64
KVH = 8
HD = 128
CAP = 1024


rope_base = 500000.0


def rotary(values, position, pair_ids, head_dim, keep):
    frequency = jnp.exp(pair_ids.astype(jnp.float32) * (-2.0 * math.log(rope_base) / head_dim))
    angles = position.astype(jnp.float32)[:, None] * frequency[None, :]
    cosine = jnp.cos(angles)
    sine_part = jnp.sin(angles)
    paired = values.reshape(values.shape[0], -1, 2)
    swapped = jnp.stack([-paired[:, :, 1], paired[:, :, 0]], axis=2).reshape(values.shape)
    turned = values * cosine + swapped * sine_part
    return jnp.where(keep[None, :], turned, values)


def packing(counts):
    end_rows = jnp.cumsum(counts)
    offsets = end_rows - counts
    row_ids = jnp.arange(CAP, dtype=jnp.int32)
    segment = jnp.sum((end_rows[None, :] <= row_ids[:, None]).astype(jnp.int32), axis=1)
    filled = row_ids < end_rows[-1]
    segment = jnp.minimum(segment, counts.shape[0] - 1)
    position = (row_ids - offsets[segment]).astype(jnp.int32)
    return (segment, position, filled)


def attend(q_head, k_head, v_head, allowed):
    scores = jnp.dot(q_head, k_head.T, preferred_element_type=jnp.float32) / math.sqrt(HD)
    scores = jnp.where(allowed, scores, jnp.float32(-1e30))
    row_max = jnp.max(scores, axis=1, keepdims=True)
    shifted = jnp.exp(scores - row_max)
    weights = (shifted / jnp.sum(shifted, axis=1, keepdims=True)).astype(jnp.bfloat16)
    return jnp.dot(weights, v_head, preferred_element_type=jnp.float32)


def body(rollout, lengths, target, w_query, w_keyval, w_out):
    sections = lax.axis_size("sec")
    member = lax.axis_index("tp")
    slot_rows = 2 * CAP // sections
    feature_cols = rollout.shape[1]
    section_ids = jnp.arange(sections, dtype=jnp.int32)
    own_lengths = lengths[0]
    chosen = target[0][None, :] == section_ids[:, None]
    before = jnp.cumsum(own_lengths) - own_lengths
    count_to = jnp.sum(jnp.where(chosen, own_lengths[None, :], 0), axis=1)
    start_to = jnp.sum(jnp.where(chosen, before[None, :], 0), axis=1)
    padded = jnp.concatenate([rollout, jnp.zeros((1, feature_cols), rollout.dtype)], axis=0)
    slot_steps = jnp.arange(slot_rows, dtype=jnp.int32)
    in_slot = slot_steps[None, :] < count_to[:, None]
    row_index = jnp.where(in_slot, start_to[:, None] + slot_steps[None, :], rollout.shape[0])
    outgoing = jnp.take(padded, row_index.reshape(-1), axis=0).reshape(
        sections, slot_rows, feature_cols
    )
    arrived, arrived_count = (
        lax.all_to_all(outgoing, "sec", split_axis=0, concat_axis=0, tiled=True),
        lax.all_to_all(count_to, "sec", split_axis=0, concat_axis=0, tiled=True),
    )
    segment, position, filled = packing(arrived_count)
    flat_index = jnp.where(filled, segment * slot_rows + position, 0)
    packed = jnp.take(arrived.reshape(sections * slot_rows, feature_cols), flat_index, axis=0)
    packed = jnp.where(filled[:, None], packed, jnp.zeros((), packed.dtype))
    query_weights = w_query[0]
    keyval_weights = w_keyval[0]
    query_width = query_weights.shape[1]
    keyval_width = keyval_weights.shape[1]
    piece = lax.all_gather(packed, "tp", axis=1, tiled=True)
    query_sum = jnp.dot(piece, query_weights, preferred_element_type=jnp.float32)
    keyval_sum = jnp.dot(piece, keyval_weights, preferred_element_type=jnp.float32)
    query = query_sum
    keyval = keyval_sum
    query_cols = member * query_width + jnp.arange(query_width, dtype=jnp.int32)
    query = rotary(query, position, query_cols % HD // 2, HD, query_cols >= 0).astype(jnp.bfloat16)
    keyval_cols = member * keyval_width + jnp.arange(keyval_width, dtype=jnp.int32)
    keyval_pairs = keyval_cols // (2 * KVH) % (HD // 2)
    keyval = rotary(keyval, position, keyval_pairs, HD, keyval_cols < KVH * HD).astype(jnp.bfloat16)
    keyval = lax.all_gather(keyval, "tp", axis=1, tiled=True)
    keyval_split = keyval.reshape(CAP, 2, HD // 2, KVH, 2)
    row_ids = jnp.arange(CAP, dtype=jnp.int32)
    allowed = (segment[:, None] == segment[None, :]) & (row_ids[None, :] <= row_ids[:, None])
    local_heads = query_width // HD
    head_blocks = []
    for head_slot in range(local_heads):
        global_head = member * local_heads + head_slot
        kv_index = global_head // (HQ // KVH)
        picked = lax.dynamic_index_in_dim(keyval_split, kv_index, 3, keepdims=False)
        k_head = picked[:, 0].reshape(CAP, HD)
        v_head = picked[:, 1].reshape(CAP, HD)
        q_head = query[:, head_slot * HD : (head_slot + 1) * HD]
        result = attend(q_head, k_head, v_head, allowed)
        head_blocks.append(
            jnp.where(filled[:, None], result, jnp.float32(0.0)).astype(jnp.bfloat16)
        )
    head_rows = jnp.concatenate(head_blocks, axis=1)
    terms = jnp.dot(head_rows, w_out[0], preferred_element_type=jnp.float32)
    summed = lax.psum_scatter(terms, "tp", scatter_dimension=1, tiled=True)
    return summed.astype(jnp.bfloat16)


def solution(mesh):
    placed = (
        P("sec", "tp"),
        P("sec", None),
        P("sec", None),
        P("sec", None, "tp"),
        P("sec", None, "tp"),
        P("sec", "tp", None),
    )
    return jax.shard_map(
        body, mesh=mesh, in_specs=placed, out_specs=P("sec", "tp"), check_vma=False
    )
```

profile of v0, /device:TPU:1, one launch (start us, length us, event | category | flops | bytes accessed | tf_op | source)
XLA Modules:
  0.0 555.7 jit_solution(7648156603387322365)
XLA Ops:
  6.5 1.0 reduce-window_1_clone.1
  7.5 0.7 subtract_bitcast_fusion
  8.2 0.8 select_reduce_fusion.1
  9.0 0.7 copy.9
  9.7 6.8 %all-to-all-start = ((s32[8,1,1]{2,1,0:T(1,128)}), s32[8,1,1]{2,1,0:T(1,128)S(1)}, u32[]{:S(2)}, u32[]{:S(2)}) async-start(s32[8,1,1]{2,1,0:T(1,128)} %copy.9), calls=%async_computation | async-start | bytes 8192 | tf_op jit(solution)/shard_map/all_to_all | solution.py:68
  16.7 3.1 concatenate.6
  19.7 11.1 %gather_fusion = bf16[2048,512]{1,0:T(8,128)(2,1)} fusion(bf16[2049,512]{1,0:T(8,128)(2,1)} %concatenate.6, s32[2048]{0:T(1024)S(1)} %broadcast_clamp_fusion), kind=kCustom, calls=%fused_computation | custom fusion | bytes 4202496 | tf_op jit(solution)/shard_map/jit(_take)/gather | solution.py:63
  30.9 2.8 broadcast_select_fusion
  33.6 5.1 all-to-all-start.1
  39.3 0.6 slice.52
  39.9 0.7 fusion.66
  40.7 4.3 compare_select_fusion.4
  45.0 0.7 fusion.48
  45.7 0.6 compare_select_fusion.1
  46.3 0.6 iota_compare_fusion.4
  47.0 17.4 %all-to-all-done.1 = bf16[8,256,512]{2,1,0:T(8,128)(2,1)} async-done(((bf16[8,256,512]{2,1,0:T(8,128)(2,1)}), bf16[8,256,512]{2,1,0:T(8,128)(2,1)}, u32[]{:S(2)}, u32[]{:S(2)}) %all-to-all-start.1) | async-done | bytes 2097184 | tf_op jit(solution)/shard_map/all_to_all | solution.py:67
  64.4 5.8 %gather_fusion.1 = bf16[1024,512]{1,0:T(8,128)(2,1)S(1)} fusion(bf16[2048,512]{1,0:T(8,128)(2,1)} %bitcast.18, s32[1024]{0:T(1024)S(1)} %broadcast_clamp_fusion.1), kind=kCustom, calls=%fused_computation.1 | custom fusion | bytes 2101248 | tf_op jit(solution)/shard_map/jit(_take)/gather | solution.py:72
  70.2 1.6 select_select_fusion
  72.0 120.6 %all-gather.3.cloned.1.call-done = bf16[1024,8192]{1,0:T(8,128)(2,1)} async-done(((bf16[1024,512]{1,0:T(8,128)(2,1)}), bf16[1024,8192]{1,0:T(8,128)(2,1)}) %all-gather.3.cloned.1.call-update) | async-done | bytes 16777232 | tf_op jit(solution)/shard_map/all_gather | solution.py:78
  192.5 11.4 %fusion.14 = f32[1024,128]{0,1:T(8,128)S(1)} fusion(bf16[1024,8192]{1,0:T(8,128)(2,1)} %all-gather.3.cloned.1.call-done, bf16[1,8192,128]{2,1,0:T(8,128)(2,1)S(1)} %copy-done), kind=kOutput, calls=%fused_computation.32 | convolution fusion | flops 2147483648 | bytes 19398656 | tf_op jit(solution)/shard_map/dot_general | solution.py:80
  204.7 0.5 pad_maximum_fusion.1
  205.5 2.9 fusion.38
  208.5 0.5 reduce-scatter.2.cloned.1.call-start
  209.1 17.2 %fusion.2 = f32[1024,512]{0,1:T(8,128)S(1)} fusion(bf16[1024,8192]{1,0:T(8,128)(2,1)} %all-gather.3.cloned.1.call-done, bf16[1,8192,512]{2,1,0:T(8,128)(2,1)} %param.9), kind=kOutput, calls=%fused_computation.4 | convolution fusion | flops 8589934592 | bytes 27262976 | tf_op jit(solution)/shard_map/dot_general | solution.py:79
  226.4 2.3 reshape.268
  228.7 4.3 slice_negate_fusion
  233.0 3.2 pad_maximum_fusion
  236.2 3.7 reshape.269
  239.9 10.0 %fusion.12 = bf16[1024,512]{0,1:T(8,128)(2,1)} fusion(f32[1024,512]{0,1:T(8,128)S(1)} %fusion.2, f32[1024,512]{0,1:T(8,128)} %reshape.269, f32[512]{0:T(512)S(1)} %fusion.53, f32[1024]{0:T(1024)S(1)} %get-tuple-element.7, pred[512]{0:T(512)(128)(4,1)S(1)} %fusion.54), kind=kLoop, calls=%fused_computation.29 | loop fusion | flops 3145728 | bytes 5249536 | tf_op jit(solution)/shard_map/convert_element_type | solution.py:84
  249.9 11.2 %all-gather.5.cloned.1.call-done = bf16[1024,2048]{0,1:T(8,128)(2,1)} async-done(((bf16[1024,128]{0,1:T(8,128)(2,1)}), bf16[1024,2048]{0,1:T(8,128)(2,1)}) %all-gather.5.cloned.1.call-update) | async-done | bytes 4194320 | tf_op jit(solution)/shard_map/all_gather | solution.py:88
  261.1 7.4 %reshape.272 = bf16[1024,2,64,8,2]{0,4,3,2,1:T(2,128)(2,1)} reshape(bf16[1024,2048]{0,1:T(8,128)(2,1)} %all-gather.5.cloned.1.call-done) | data formatting | bytes 8388608 | tf_op jit(solution)/shard_map/reshape | solution.py:89
  268.5 3.7 dynamic-slice_bitcast_fusion.3
  273.7 0.8 reshape_squeeze.28
  275.2 2.2 fusion.67
  277.4 1.1 fusion.68
  278.4 1.1 fusion.69
  279.5 1.1 fusion.70
  280.5 0.6 fusion.8
  281.2 0.9 fusion.21
  282.1 0.6 fusion.7
  282.7 0.9 fusion.23
  283.6 0.6 fusion.6
  284.2 1.1 fusion.25
  285.3 0.6 fusion.5
  286.0 0.9 fusion.27
  286.9 18.7 %fusion = f32[1024,8192]{1,0:T(8,128)} fusion(bf16[1,512,8192]{2,1,0:T(8,128)(2,1)} %param.11, bf16[1024,128]{0,1:T(8,128)(2,1)S(1)} %fusion.21, bf16[1024,128]{0,1:T(8,128)(2,1)S(1)} %fusion.23, bf16[1024,128]{0,1:T(8,128)(2,1)S(1)} %fusion.25, bf16[1024,128]{0,1:T(8,128)(2,1)S(1)} %fusion.27), kind=kOutput, calls=%fused_computation.2 | convolution fusion | flops 8594128896 | bytes 42991616 | tf_op jit(solution)/shard_map/dot_general | solution.py:106
  305.6 240.6 %reduce-scatter.2.cloned.1.call-done = f32[1024,512]{1,0:T(8,128)} async-done(((f32[1024,8192]{1,0:T(8,128)}), f32[1024,512]{1,0:T(8,128)}) %reduce-scatter.2.cloned.1.call-update) | async-done | bytes 2097168 | tf_op jit(solution)/shard_map/reduce_scatter | solution.py:107
  546.2 2.7 convert_element_type.72
  (44 shorter events, 4.2 us)
Async XLA Ops:
  6.5 186.0 %copy-start = (bf16[1,8192,128]{2,1,0:T(8,128)(2,1)S(1)}, bf16[1,8192,128]{2,1,0:T(8,128)(2,1)}, u32[]{:S(2)}) copy-start(bf16[1,8192,128]{2,1,0:T(8,128)(2,1)} %param.10) | copy-start | bytes 6291460
  9.7 24.0 %all-to-all-start = ((s32[8,1,1]{2,1,0:T(1,128)}), s32[8,1,1]{2,1,0:T(1,128)S(1)}, u32[]{:S(2)}, u32[]{:S(2)}) async-start(s32[8,1,1]{2,1,0:T(1,128)} %copy.9), calls=%async_computation | async-start | bytes 8192 | tf_op jit(solution)/shard_map/all_to_all | solution.py:68
  33.6 30.7 %all-to-all-start.1 = ((bf16[8,256,512]{2,1,0:T(8,128)(2,1)}), bf16[8,256,512]{2,1,0:T(8,128)(2,1)}, u32[]{:S(2)}, u32[]{:S(2)}) async-start(bf16[8,256,512]{2,1,0:T(8,128)(2,1)} %broadcast_select_fusion), calls=%async_computation.1 | async-start | bytes 4194304 | tf_op jit(solution)/shard_map/all_to_all | solution.py:67
  38.8 153.7 %all-gather.3.cloned.1.call-start = ((), (), s32[]{:S(2)}) async-start(), calls=%async_computation.3 | async-start | bytes 17825792 | tf_op jit(solution)/shard_map/all_gather | solution.py:78
  71.9 189.2 %all-gather.5.cloned.1.call-start = ((), (), s32[]{:S(2)}) async-start(), calls=%async_computation.4 | async-start | bytes 4456448 | tf_op jit(solution)/shard_map/all_gather | solution.py:88
  208.5 337.7 %reduce-scatter.2.cloned.1.call-start = ((), (), s32[]{:S(2)}) async-start(), calls=%async_computation.5 | async-start | bytes 35651584 | tf_op jit(solution)/shard_map/reduce_scatter | solution.py:107
  274.9 2.4 copy-start.2
  275.0 2.4 copy-start.3
  305.6 243.3 %copy-start.1 = (bf16[1,8192,128]{2,1,0:T(8,128)(2,1)S(1)}, bf16[1,8192,128]{2,1,0:T(8,128)(2,1)}, u32[]{:S(2)}) copy-start(bf16[1,8192,128]{2,1,0:T(8,128)(2,1)} %param.10) | copy-start | bytes 6291460
Sparse Core Ops, SparseCore 0:
  72.0 120.4 all-gather.2
  208.6 52.3 all-gather.4
  305.7 240.4 reduce-scatter.1
where the time goes:
time: 565 us; the launch traced here: 556 us
  waiting for transfers between devices  390 us (69%)
  matrix products  56.5 us (10%)
  local copies, waits for them, and re-layouts  42.7 us (8%)
  other arithmetic  40.4 us (7%)
  between operations  13.7 us (2%)
  starting transfers between devices  12.5 us (2%)
    reduce_scatter x1, waiting for transfers between devices, body(): summed = lax.psum_scatter(terms, 'tp', scatter_dimension=1, tiled=True)  241 us
    all_gather x1, waiting for transfers between devices, body(): piece = lax.all_gather(packed, 'tp', axis=1, tiled=True)  121 us
    dot_general x1, matrix products, body(): terms = jnp.dot(head_rows, w_out[0], preferred_element_type=jnp.float32)  18.7 us
    all_to_all x1, waiting for transfers between devices, body(): lax.all_to_all(outgoing, 'sec', split_axis=0, concat_axis=0, tiled=True)  17.4 us
    dot_general x1, matrix products, body(): jnp.dot(piece, query_weights, preferred_element_type=jnp.float32)  17.2 us
    dot_general x1, matrix products, body(): jnp.dot(piece, keyval_weights, preferred_element_type=jnp.float32)  11.4 us
  transfers between devices with their start and end apart: 5, of which 4 were waited for; matrix products, arithmetic and copies ran while one was open for 12% of the time, Pallas kernels for 0%

commit v1 on v0

v1 whole, which is shorter than its diff:
```python
import functools
import math

import jax
import jax.numpy as jnp
from jax import lax
from jax.experimental import pallas as pl
from jax.experimental.pallas import tpu as pltpu
from jax.sharding import PartitionSpec as P

HQ = 64
KVH = 8
HD = 128
CAP = 1024
SLOT = 256
ALIGN = 16
SENT = SLOT + ALIGN
TILE = 256
BLOCK = 512
rope_base = 500000.0
BF = jnp.bfloat16
F32 = jnp.float32


def params(mib):
    return pltpu.CompilerParams(vmem_limit_bytes=mib * 1024 * 1024)


def permutation(move):
    pairs = []
    for t in range(16):
        x, y, c = move(t // 8, t // 2 % 4, t % 2)
        pairs.append((t, x % 2 * 8 + y % 4 * 2 + c % 2))
    return pairs


TO_CORE = permutation(lambda x, y, c: (x, y, c + 1))
TO_X = permutation(lambda x, y, c: (x + 1, y, c))
TO_Y = permutation(lambda x, y, c: (x, y + 1 - 2 * c, c))


def send(value, pairs):
    return lax.ppermute(value, "tp", pairs)


def cut_kernel(start_ref, rollout_ref, first_ref, second_ref, sems):
    width = first_ref.shape[2]
    copies = []
    for part, out in enumerate((first_ref, second_ref)):
        for d in range(8):
            row = pl.multiple_of(start_ref[d], ALIGN)
            copies.append(
                pltpu.make_async_copy(
                    rollout_ref.at[pl.ds(row, SENT), pl.ds(part * width, width)],
                    out.at[d],
                    sems.at[part * 8 + d],
                )
            )
    for copy in copies:
        copy.start()
    for copy in copies:
        copy.wait()


def cut(rollout, starts):
    width = rollout.shape[1] // 2
    shape = jax.ShapeDtypeStruct((8, SENT, width), BF)
    return pl.pallas_call(
        cut_kernel,
        out_shape=(shape, shape),
        grid_spec=pltpu.PrefetchScalarGridSpec(
            num_scalar_prefetch=1,
            grid=(1,),
            in_specs=[pl.BlockSpec(memory_space=pl.ANY)],
            out_specs=[pl.BlockSpec(memory_space=pl.ANY)] * 2,
            scratch_shapes=[pltpu.SemaphoreType.DMA((16,))],
        ),
        cost_estimate=pl.CostEstimate(flops=0, bytes_accessed=8 << 20, transcendentals=0),
        name="cut",
    )(starts, rollout)


def pack_kernel(plan_ref, arrived_ref, packed_ref):
    rows = pl.program_id(0) * TILE + lax.broadcasted_iota(jnp.int32, (TILE, 1), 0)
    source = jnp.full((TILE, 1), -1, jnp.int32)
    for s in range(8):
        inside = (rows >= plan_ref[0, s]) & (rows < plan_ref[1, s])
        source = jnp.where(inside, rows + plan_ref[2, s], source)
    slots = lax.broadcasted_iota(jnp.int32, (TILE, arrived_ref.shape[0]), 1)
    picked = jnp.where(slots == source, 1.0, 0.0).astype(BF)
    packed_ref[...] = jnp.dot(
        picked, arrived_ref[...], preferred_element_type=F32
    ).astype(BF)


def pack(arrived, plan):
    slots, width = arrived.shape
    return pl.pallas_call(
        pack_kernel,
        out_shape=jax.ShapeDtypeStruct((CAP, width), BF),
        grid_spec=pltpu.PrefetchScalarGridSpec(
            num_scalar_prefetch=1,
            grid=(CAP // TILE,),
            in_specs=[pl.BlockSpec((slots, width), lambda i, p: (0, 0))],
            out_specs=pl.BlockSpec((TILE, width), lambda i, p: (i, 0)),
        ),
        compiler_params=params(32),
        cost_estimate=pl.CostEstimate(
            flops=2 * CAP * slots * width, bytes_accessed=2 << 20, transcendentals=0
        ),
        name="pack",
    )(plan, arrived)


def swap_members(values):
    lanes = lax.broadcasted_iota(jnp.int32, values.shape, 1)
    return jnp.where(
        lanes % 2 == 0, pltpu.roll(values, HD - 1, 1), pltpu.roll(values, 1, 1)
    )


def project_kernel(counts, has_total, last, *refs):
    refs = list(refs)
    refs.pop(0)
    pieces = [refs.pop(0) for _ in counts]
    n = sum(counts)
    query_w = [refs.pop(0) for _ in range(n)]
    keyval_w = [refs.pop(0) for _ in range(n)]
    total_refs = [refs.pop(0) for _ in range(2)] if has_total else None
    tables = [refs.pop(0) for _ in range(4)] if last else None
    query_out, keyval_out = refs
    query = total_refs[0][...] if has_total else None
    keyval = total_refs[1][...] if has_total else None
    k = 0
    for ref, count in zip(pieces, counts):
        for j in range(count):
            left = ref[j]
            q_term = jnp.dot(left, query_w[k][...], preferred_element_type=F32)
            kv_term = jnp.dot(left, keyval_w[k][...], preferred_element_type=F32)
            query = q_term if query is None else query + q_term
            keyval = kv_term if keyval is None else keyval + kv_term
            k += 1
    if not last:
        query_out[...] = query
        keyval_out[...] = keyval
        return
    q_cos, q_sin, kv_cos, kv_sin = [t[...] for t in tables]
    for head in range(query.shape[1] // HD):
        span = slice(head * HD, (head + 1) * HD)
        part = query[:, span]
        query_out[:, span] = (part * q_cos + swap_members(part) * q_sin).astype(BF)
    turned = (keyval * kv_cos + swap_members(keyval) * kv_sin).astype(BF)
    to = lax.broadcasted_iota(jnp.int32, (HD, HD), 0)
    came = lax.broadcasted_iota(jnp.int32, (HD, HD), 1)
    order = jnp.where(came == to % 16 // 2 * 16 + to // 16 * 2 + to % 2, 1.0, 0.0).astype(BF)
    keyval_out[...] = lax.dot_general(
        order, turned, (((1,), (1,)), ((), ())), preferred_element_type=F32
    ).astype(BF)


def project(pieces, index, w_query, w_keyval, total, tables, block):
    pieces = [p if p.ndim == 3 else p[None] for p in pieces]
    counts = tuple(p.shape[0] for p in pieces)
    n = sum(counts)
    rows, width = pieces[0].shape[1:]
    columns = w_query.shape[1]
    last = tables is not None
    skip = block * (BLOCK // TILE)
    in_specs = [
        pl.BlockSpec((c, TILE, width), lambda i, p: (0, i, 0)) for c in counts
    ]
    for cols in (columns, HD):
        in_specs += [
            pl.BlockSpec((width, cols), lambda i, p, k=k: (p[k], 0)) for k in range(n)
        ]
    operands = pieces + [w_query] * n + [w_keyval] * n
    if total is not None:
        in_specs += [
            pl.BlockSpec((TILE, columns), lambda i, p: (i + skip, 0)),
            pl.BlockSpec((TILE, HD), lambda i, p: (i + skip, 0)),
        ]
        operands += list(total)
    if last:
        in_specs += [pl.BlockSpec((TILE, HD), lambda i, p: (i + skip, 0))] * 4
        operands += list(tables)
        out_shape = (
            jax.ShapeDtypeStruct((rows, columns), BF),
            jax.ShapeDtypeStruct((HD, rows), BF),
        )
        kv_spec = pl.BlockSpec((HD, TILE), lambda i, p: (0, i))
    else:
        out_shape = (
            jax.ShapeDtypeStruct((rows, columns), F32),
            jax.ShapeDtypeStruct((rows, HD), F32),
        )
        kv_spec = pl.BlockSpec((TILE, HD), lambda i, p: (i, 0))
    return pl.pallas_call(
        functools.partial(project_kernel, counts, total is not None, last),
        out_shape=out_shape,
        grid_spec=pltpu.PrefetchScalarGridSpec(
            num_scalar_prefetch=1,
            grid=(rows // TILE,),
            in_specs=in_specs,
            out_specs=[pl.BlockSpec((TILE, columns), lambda i, p: (i, 0)), kv_spec],
        ),
        compiler_params=params(48),
        cost_estimate=pl.CostEstimate(
            flops=2 * rows * n * width * (columns + HD),
            bytes_accessed=n * width * (rows + columns + HD) * 2,
            transcendentals=0,
        ),
        name="project",
    )(index, *operands)


def attend_kernel(block, plan_ref, query_ref, *refs):
    heads_ref = refs[-1]
    keyvals = refs[:-1]
    scale = 1.0 / math.sqrt(HD)
    local_heads = query_ref.shape[1] // HD
    for tile in range(BLOCK // TILE):
        here = block * (BLOCK // TILE) + tile
        rows = here * TILE + lax.broadcasted_iota(jnp.int32, (TILE, 1), 0)
        begin = jnp.zeros((TILE, 1), jnp.int32)
        for s in range(8):
            begin = jnp.where(rows >= plan_ref[0, s], plan_ref[0, s], begin)
        filled = rows < plan_ref[1, 7]
        seen = []
        for there in range(max(here - 1, 0), here + 1):
            columns = there * TILE + lax.broadcasted_iota(jnp.int32, (TILE, TILE), 1)
            allowed = (columns >= begin) & (columns <= rows)
            source = keyvals[-1] if there * TILE >= block * BLOCK else keyvals[0]
            first = there * TILE % BLOCK
            seen.append((allowed, source, slice(first, first + TILE)))
        for head in range(local_heads):
            span = slice(head * HD, (head + 1) * HD)
            query = query_ref[tile * TILE : (tile + 1) * TILE, span]
            scores = []
            for allowed, source, at in seen:
                raw = jnp.dot(query, source[0:HD, at], preferred_element_type=F32)
                scores.append(jnp.where(allowed, raw * scale, -1e30))
            top = functools.reduce(
                jnp.maximum, [jnp.max(s, axis=1, keepdims=True) for s in scores]
            )
            shifted = [jnp.exp(s - top) for s in scores]
            norm = sum(jnp.sum(s, axis=1, keepdims=True) for s in shifted)
            result = jnp.zeros((TILE, HD), F32)
            for part, (_, source, at) in zip(shifted, seen):
                weights = (part / norm).astype(BF)
                result += lax.dot_general(
                    weights,
                    source[HD : 2 * HD, at],
                    (((1,), (1,)), ((), ())),
                    preferred_element_type=F32,
                )
            heads_ref[tile * TILE : (tile + 1) * TILE, span] = jnp.where(
                filled, result, 0.0
            ).astype(BF)


def attend(block, plan, query, keyvals):
    return pl.pallas_call(
        functools.partial(attend_kernel, block),
        out_shape=jax.ShapeDtypeStruct(query.shape, BF),
        in_specs=[pl.BlockSpec(memory_space=pltpu.SMEM)]
        + [pl.BlockSpec(memory_space=pltpu.VMEM)] * (1 + len(keyvals)),
        out_specs=pl.BlockSpec(memory_space=pltpu.VMEM),
        compiler_params=params(32),
        cost_estimate=pl.CostEstimate(
            flops=4 * BLOCK * 2 * TILE * query.shape[1],
            bytes_accessed=2 << 20,
            transcendentals=BLOCK * 2 * TILE * 4,
        ),
        name="attend",
    )(plan, query, *keyvals)


def chunks_kernel(adds, *refs):
    refs = list(refs)
    refs.pop(0)
    heads = refs.pop(0)[...]
    n = len(adds)
    weights = [refs.pop(0) for _ in range(n)]
    out_ref = refs.pop()
    for k in range(n):
        total = jnp.dot(heads, weights[k][...], preferred_element_type=F32)
        for _ in range(adds[k]):
            total += refs.pop(0)[0].astype(F32)
        out_ref[k] = total.astype(BF)


def chunks(heads, w_out, index, adds):
    rows, depth = heads.shape
    width = 512
    n = len(adds)
    in_specs = [pl.BlockSpec((TILE, depth), lambda i, p: (i, 0))]
    in_specs += [
        pl.BlockSpec((depth, width), lambda i, p, k=k: (0, p[k])) for k in range(n)
    ]
    operands = [heads] + [w_out] * n
    for terms in adds:
        for array, place in terms:
            in_specs.append(
                pl.BlockSpec((1, TILE, width), lambda i, p, at=place: (at, i, 0))
            )
            operands.append(array)
    return pl.pallas_call(
        functools.partial(chunks_kernel, tuple(len(a) for a in adds)),
        out_shape=jax.ShapeDtypeStruct((n, rows, width), BF),
        grid_spec=pltpu.PrefetchScalarGridSpec(
            num_scalar_prefetch=1,
            grid=(rows // TILE,),
            in_specs=in_specs,
            out_specs=pl.BlockSpec((n, TILE, width), lambda i, p: (0, i, 0)),
        ),
        compiler_params=params(32),
        cost_estimate=pl.CostEstimate(
            flops=2 * rows * depth * width * n,
            bytes_accessed=2 * n * width * (rows + depth) * 2,
            transcendentals=0,
        ),
        name="chunks",
    )(index, *operands)


def gather_chips(value):
    own = jnp.stack([value, send(value, TO_CORE)])
    across = send(value, TO_X)
    up = send(own, TO_Y)
    across = jnp.stack([across, send(across, TO_CORE)])
    far = send(up[:1], TO_Y)
    down = send(up, TO_CORE)
    across_up = send(across, TO_Y)
    far_other = send(far, TO_CORE)
    across_far = send(across_up[:1], TO_Y)
    across_down = send(across_up, TO_CORE)
    across_far_other = send(across_far, TO_CORE)
    return [
        own, up, down, far, far_other,
        across, across_up, across_down, across_far, across_far_other,
    ]


def gather_order(x, y, c):
    way = 1 - 2 * c
    order = []
    for side in (x, 1 - x):
        for row, core in (
            (y, c), (y, 1 - c), (y - way, c), (y - way, 1 - c),
            (y + way, 1 - c), (y + way, c), (y + 2, c), (y + 2, 1 - c),
        ):
            order.append(side * 8 + (row + 4) % 4 * 2 + core)
    return jnp.stack(order).astype(jnp.int32)


def scatter_sum(heads, w_out, x, y, c):
    way = 1 - 2 * c

    def at(*places):
        return jnp.stack(
            [side * 8 + (row + 4) % 4 * 2 + core for side, row, core in places]
        ).astype(jnp.int32)

    sides = (1 - x, x)
    for_core = []
    for side in sides:
        index = at((side, y + 2, 1 - c), (side, y - way, 1 - c), (side, y - way, c))
        for_core.append(send(chunks(heads, w_out, index, [[], [], []]), TO_CORE))
    far = []
    for side, other in zip(sides, for_core):
        far.append(send(chunks(heads, w_out, at((side, y + 2, c)), [[(other, 0)]]), TO_Y))
    near = []
    for side, other, passed in zip(sides, for_core, far):
        index = at((side, y + way, c), (side, y + way, 1 - c))
        adds = [[(other, 1), (passed, 0)], [(other, 2)]]
        near.append(send(chunks(heads, w_out, index, adds), TO_Y))
    crossed = None
    for side, came in zip(sides, near):
        shared = send(chunks(heads, w_out, at((side, y, 1 - c)), [[(came, 1)]]), TO_CORE)
        adds = [(came, 0), (shared, 0)]
        if crossed is not None:
            adds.append((crossed, 0))
        result = chunks(heads, w_out, at((side, y, c)), [adds])
        if crossed is None:
            crossed = send(result, TO_X)
    return result[0]


def rotary_tables(position, member):
    lanes = jnp.arange(HD, dtype=jnp.int32)
    sign = jnp.where(lanes % 2 == 0, -1.0, 1.0).astype(F32)

    def table(pairs):
        frequency = jnp.exp(pairs.astype(F32) * (-2.0 * math.log(rope_base) / HD))
        angles = position.astype(F32)[:, None] * frequency[None, :]
        return jnp.cos(angles), jnp.sin(angles) * sign[None, :]

    q_cos, q_sin = table(lanes // 2)
    columns = member * HD + lanes
    kv_cos, kv_sin = table(columns // (2 * KVH) % (HD // 2))
    keys = member < KVH
    return q_cos, q_sin, jnp.where(keys, kv_cos, 1.0), jnp.where(keys, kv_sin, 0.0)


def body(rollout, lengths, target, w_query, w_keyval, w_out):
    member = lax.axis_index("tp")
    x, y, c = member // 8, member // 2 % 4, member % 2
    section_ids = jnp.arange(8, dtype=jnp.int32)
    own_lengths = lengths[0]
    chosen = target[0][None, :] == section_ids[:, None]
    before = jnp.cumsum(own_lengths) - own_lengths
    count_to = jnp.sum(jnp.where(chosen, own_lengths[None, :], 0), axis=1)
    start_to = jnp.sum(jnp.where(chosen, before[None, :], 0), axis=1)
    sent_from = jnp.minimum(start_to // ALIGN * ALIGN, rollout.shape[0] - SENT)
    facts = jnp.stack([count_to, start_to - sent_from], axis=1)
    facts = lax.all_to_all(facts, "sec", split_axis=0, concat_axis=0, tiled=True)
    outgoing = cut(rollout, sent_from)
    arrived = [
        lax.all_to_all(o, "sec", split_axis=0, concat_axis=0, tiled=True).reshape(
            8 * SENT, o.shape[2]
        )
        for o in outgoing
    ]
    counts, shifts = facts[:, 0], facts[:, 1]
    ends = jnp.cumsum(counts)
    offsets = ends - counts
    plan = jnp.stack([offsets, ends, section_ids * SENT + shifts - offsets])
    row_ids = jnp.arange(CAP, dtype=jnp.int32)
    begin = jnp.max(
        jnp.where(row_ids[:, None] >= offsets[None, :], offsets[None, :], 0), axis=1
    )
    tables = rotary_tables(row_ids - begin, member)

    order = gather_order(x, y, c)
    first = pack(arrived[0], plan)
    second = pack(arrived[1], plan)
    total = project(gather_chips(first), order * 2, w_query[0], w_keyval[0], None, None, 0)
    keyvals = []
    results = []
    for block in range(CAP // BLOCK):
        rows = second[block * BLOCK : (block + 1) * BLOCK]
        query, keyval = project(
            gather_chips(rows), order * 2 + 1, w_query[0], w_keyval[0], total, tables, block
        )
        spread = jnp.repeat(keyval.reshape(KVH, 2 * KVH, BLOCK), 2, axis=0)
        spread = lax.all_to_all(spread, "tp", split_axis=0, concat_axis=0, tiled=True)
        keyvals.append(spread.reshape(2 * HD, BLOCK))
        heads = attend(block, plan, query, keyvals[-2:])
        results.append(scatter_sum(heads, w_out[0], x, y, c))
    return jnp.concatenate(results, axis=0)


def solution(mesh):
    placed = (
        P("sec", "tp"),
        P("sec", None),
        P("sec", None),
        P("sec", None, "tp"),
        P("sec", None, "tp"),
        P("sec", "tp", None),
    )
    return jax.shard_map(
        body, mesh=mesh, in_specs=placed, out_specs=P("sec", "tp"), check_vma=False
    )
```

time: 565 us -> 409 us (0.72)
  waiting for transfers between devices: 390 us -> 109 us
  Pallas kernels: 0 us -> 135 us
  starting transfers between devices: 12.5 us -> 111 us
  matrix products: 56.5 us -> 0 us
  other arithmetic: 40.4 us -> 11.4 us
  local copies, waits for them, and re-layouts: 42.7 us -> 17.9 us
  blocking collectives: 0 us -> 20.1 us
  between operations: 13.7 us -> 0.87 us
    reduce_scatter x1 -> x0, waiting for transfers between devices: 241 us -> none  [body(): summed = lax.psum_scatter(terms, 'tp', scatter_dimension=1, tiled=True)]
    pallas_call x0 -> x28, Pallas kernels: none -> 135 us  [the longest x1 69.4 us: cut(): pl.pallas_call(cut_kernel, out_shape=(shape, shape), grid_spec=pltpu.Pref...]
    all_gather x2 -> x0, waiting for transfers between devices: 132 us -> none  [the longest x1 121 us: body(): piece = lax.all_gather(packed, 'tp', axis=1, tiled=True)]
    ppermute x0 -> x51, waiting for transfers between devices: none -> 103 us  [send(): return lax.ppermute(value, 'tp', pairs)]
    ppermute x0 -> x51, starting transfers between devices: none -> 89.9 us  [send(): return lax.ppermute(value, 'tp', pairs)]
    dot_general x11 -> x0, matrix products: 56.5 us -> none  [the longest x1 18.7 us: body(): terms = jnp.dot(head_rows, w_out[0], preferred_element_type=jnp.float32)]
    all_to_all x0 -> x1, blocking collectives: none -> 20.1 us  [body(): lax.all_to_all(o, 'sec', split_axis=0, concat_axis=0, tiled=True)]
    gather x3 -> x0, local copies, waits for them, and re-layouts: 17.7 us -> none  [the longest x1 11.1 us: body(): jnp.take(padded, row_index.reshape(-1), axis=0)]
  transfers between devices with their start and end apart: 5 -> 55, of which waited for: 4 -> 20; matrix products, arithmetic and copies ran while one was open for 12% -> 4% of each run, Pallas kernels for 0% -> 33%
where the time goes in v1:
time: 409 us; the launch traced here: 405 us
  Pallas kernels  135 us (33%)
  starting transfers between devices  111 us (27%)
  waiting for transfers between devices  109 us (27%)
  blocking collectives  20.1 us (5%)
  local copies, waits for them, and re-layouts  17.9 us (4%)
  other arithmetic  11.4 us (3%)
    ppermute x51, waiting for transfers between devices, send(): return lax.ppermute(value, 'tp', pairs)  103 us
    ppermute x51, starting transfers between devices, send(): return lax.ppermute(value, 'tp', pairs)  89.9 us
    pallas_call x1, Pallas kernels, cut(): pl.pallas_call(cut_kernel, out_shape=(shape, shape), grid_spec=pltpu.Pref...  69.4 us
    pallas_call x3, Pallas kernels, project(): pl.pallas_call(functools.partial(project_kernel, counts, total is not Non...  30.2 us
    pallas_call x20, Pallas kernels, chunks(): pl.pallas_call(functools.partial(chunks_kernel, tuple((len(a) for a in ad...  23.6 us
    all_to_all x1, blocking collectives, body(): lax.all_to_all(o, 'sec', split_axis=0, concat_axis=0, tiled=True)  20.1 us
    all_to_all x2, starting transfers between devices, body(): lax.all_to_all(spread, 'tp', split_axis=0, concat_axis=0, tiled=True)  10.7 us
    unnamed x44, local copies, waits for them, and re-layouts  9.31 us
  transfers between devices with their start and end apart: 55, of which 20 were waited for; matrix products, arithmetic and copies ran while one was open for 4% of the time, Pallas kernels for 33%

profile of v1, /device:TPU:1, one launch (start us, length us, event | category | flops | bytes accessed | tf_op | source)
XLA Modules:
  0.0 404.6 jit_solution(13254532934790481895)
XLA Ops:
  3.0 6.8 %all-to-all-start = ((s32[8,1,2]{2,1,0:T(1,128)}), s32[8,1,2]{2,1,0:T(1,128)S(1)}, u32[]{:S(2)}, u32[]{:S(2)}) async-start(s32[8,1,2]{2,1,0:T(1,128)} %copy.9), calls=%async_computation | async-start | bytes 8192 | tf_op jit(solution)/shard_map/all_to_all | solution.py:416
  10.4 69.4 %cut.1 = (bf16[8,272,256]{2,1,0:T(8,128)(2,1)}, bf16[8,272,256]{2,1,0:T(8,128)(2,1)}) custom-call(s32[8]{0:T(128)} %multiply_minimum_fusion.start_ref, bf16[2048,512]{1,0:T(8,128)(2,1)} %rollout_ref.1), custom_call_target="tpu_custom_call" | custom-call | bytes 8388608 | tf_op jit(solution)/shard_map/cut/pallas_call | solution.py:68
  79.8 20.1 %all_to_all.32 = bf16[8,272,256]{2,1,0:T(8,128)(2,1)S(1)} all-to-all(bf16[8,272,256]{2,1,0:T(8,128)(2,1)} %get-tuple-element.14), channel_id=1, replica_groups=mesh['sec'=8,'tp'=16] {'sec'}, dimensions={0} | all-to-all | bytes 2228224 | tf_op jit(solution)/shard_map/all_to_all | solution.py:419
  99.9 3.6 all-to-all-start.1
  103.8 3.0 pack.3
  109.3 2.8 collective-permute-start.11
  112.1 5.2 %all-to-all-done.1 = bf16[8,272,256]{2,1,0:T(8,128)(2,1)S(1)} async-done(((bf16[8,272,256]{2,1,0:T(8,128)(2,1)}), bf16[8,272,256]{2,1,0:T(8,128)(2,1)S(1)}, u32[]{:S(2)}, u32[]{:S(2)}) %all-to-all-start.1) | async-done | bytes 1114144 | tf_op jit(solution)/shard_map/all_to_all | solution.py:419
  117.4 3.0 pack.2
  120.4 6.6 %collective-permute-start = (bf16[512,256]{1,0:T(8,128)(2,1)S(1)}, bf16[512,256]{1,0:T(8,128)(2,1)S(1)}, u32[]{:S(2)}, u32[]{:S(2)}) collective-permute-start(bf16[512,256]{1,0:T(8,128)(2,1)S(1)} %get-tuple-element.28), channel_id=1, source_target_pairs={{0,1},{1,0},{2,3},{3,2},{4,5},{5,4},{6,7},{7,6},{8,9},{9,8},{10,11... | collective-permute-start | bytes 786440 | tf_op jit(solution)/shard_map/ppermute | solution.py:43
  127.8 3.2 collective-permute-start.17
  134.5 5.8 %collective-permute-done.5 = bf16[512,256]{1,0:T(8,128)(2,1)S(1)} collective-permute-done((bf16[512,256]{1,0:T(8,128)(2,1)S(1)}, bf16[512,256]{1,0:T(8,128)(2,1)S(1)}, u32[]{:S(2)}, u32[]{:S(2)}) %collective-permute-start.5) | collective-permute-done | bytes 262176 | tf_op jit(solution)/shard_map/ppermute | solution.py:43
  140.4 2.7 collective-permute-start.1
  143.1 2.9 collective-permute-done.36
  146.9 2.8 collective-permute-start.12
  151.9 2.8 collective-permute-start.38
  154.8 23.5 %collective-permute-done.32.refs_2_ = bf16[2,512,256]{2,1,0:T(8,128)(2,1)} collective-permute-done((bf16[2,512,256]{2,1,0:T(8,128)(2,1)S(1)}, bf16[2,512,256]{2,1,0:T(8,128)(2,1)}, u32[]{:S(2)}, u32[]{:S(2)}) %collective-permute-start.32) | collective-permute-done | bytes 524320 | tf_op jit(solution)/shard_map/ppermute | solution.py:43
  178.3 3.2 collective-permute-start.3
  183.9 3.2 collective-permute-start.34
  188.8 3.5 collective-permute-done.3.refs_4_
  192.3 3.1 collective-permute-start.9
  203.1 2.6 collective-permute-start.19
  205.7 3.1 collective-permute-done.14.refs_4_
  211.4 3.1 collective-permute-done.20.refs_9_
  217.5 5.5 %fusion.3 = (f32[1024,128]{1,0:T(8,128)}, f32[1024,128]{1,0:T(8,128)}, f32[1024,128]{1,0:T(8,128)S(1)}, f32[1024,128]{1,0:T(8,128)}) fusion(f32[128]{0:T(128)S(1)} %fusion.9, f32[128]{0:T(128)S(1)} %get-tuple-element.35, f32[1024]{0:T(1024)S(1)} %subtract_convert_fusion, pred[]{:T(512)S(6)} %lt.136, f32[128]{0:T(128)S(1)} %get-tuple-element.36), kind=kLoop, calls=%fused_computation.10 | loop fusion | flops 786432 | bytes 2102785 | tf_op jit(solution)/shard_map/jit(_where)/select_n | solution.py:402
  225.0 12.8 %project.3 = (f32[1024,512]{1,0:T(8,128)}, f32[1024,128]{1,0:T(8,128)S(1)}) custom-call(s32[16]{0:T(128)S(1)} %get-tuple-element.33.refs_0_, bf16[2,1024,256]{2,1,0:T(8,128)(2,1)S(1)} %pad_maximum_fusion.refs_1_, bf16[2,1024,256]{2,1,0:T(8,128)(2,1)S(1)} %collective-permute-done.12.refs_2_, bf16[2,1024,256]{2,1,0:T(8,128)(2,1)S(1)} %collective-permute-done.13.refs_3_, ...), custom_call_target="tpu_custom_call" | custom-call | flops 5368709120 | bytes 13631488 | tf_op jit(solution)/shard_map/project/pallas_call | solution.py:197
  237.9 8.6 %project.4 = (bf16[512,512]{1,0:T(8,128)(2,1)S(1)}, bf16[128,512]{1,0:T(8,128)(2,1)S(1)}) custom-call(s32[16]{0:T(128)S(1)} %get-tuple-element.34.refs_0_, bf16[2,512,256]{2,1,0:T(8,128)(2,1)S(1)} %copy-done.4, bf16[2,512,256]{2,1,0:T(8,128)(2,1)S(1)} %copy-done.12, bf16[2,512,256]{2,1,0:T(8,128)(2,1)S(1)} %collective-permute-done.2.refs_3_, ...), custom_call_target="tpu_custom_call" | custom-call | flops 2684354560 | bytes 9437184 | tf_op jit(solution)/shard_map/project/pallas_call | solution.py:197
  247.2 3.4 all-to-all-start.3
  250.7 8.8 %project.5 = (bf16[512,512]{1,0:T(8,128)(2,1)S(1)}, bf16[128,512]{1,0:T(8,128)(2,1)S(1)}) custom-call(s32[16]{0:T(128)S(1)} %get-tuple-element.34.refs_0_, bf16[2,512,256]{2,1,0:T(8,128)(2,1)S(1)} %copy-done.6, bf16[2,512,256]{2,1,0:T(8,128)(2,1)} %collective-permute-done.32.refs_2_, bf16[2,512,256]{2,1,0:T(8,128)(2,1)} %collective-permute-done.33.refs_3_, ...), custom_call_target="tpu_custom_call" | custom-call | flops 2684354560 | bytes 9437184 | tf_op jit(solution)/shard_map/project/pallas_call | solution.py:197
  261.1 7.3 %all-to-all-start.4 = ((bf16[16,16,512]{2,1,0:T(8,128)(2,1)}), bf16[16,16,512]{2,1,0:T(8,128)(2,1)S(1)}, u32[]{:S(2)}, u32[]{:S(2)}) async-start(bf16[16,16,512]{2,1,0:T(8,128)(2,1)} %bitcast.49), calls=%async_computation.4 | async-start | bytes 524288 | tf_op jit(solution)/shard_map/all_to_all | solution.py:446
  268.4 2.6 attend.2.refs_1_
  271.0 3.4 copy-done
  274.4 2.8 chunks.24
  277.2 9.8 %collective-permute-start.26 = (bf16[3,512,512]{2,1,0:T(8,128)(2,1)}, bf16[3,512,512]{2,1,0:T(8,128)(2,1)S(1)}, u32[]{:S(2)}, u32[]{:S(2)}) collective-permute-start(bf16[3,512,512]{2,1,0:T(8,128)(2,1)} %chunks.24), channel_id=1, source_target_pairs={{0,1},{1,0},{2,3},{3,2},{4,5},{5,4},{6,7},{7,6},{8,9},{9,8},{10,11... | collective-permute-start | bytes 4718600 | tf_op jit(solution)/shard_map/ppermute | solution.py:43
  287.0 3.1 attend.3.refs_1_
  290.1 3.4 copy-done.1
  302.1 2.9 collective-permute-start.27
  308.3 2.9 collective-permute-done.27.refs_5_
  312.8 3.2 collective-permute-start.28
  318.4 3.2 collective-permute-start.48
  324.0 3.2 collective-permute-start.24
  329.7 3.2 collective-permute-start.44
  332.9 6.4 %collective-permute-done.28.refs_3_ = bf16[2,512,512]{2,1,0:T(8,128)(2,1)S(1)} collective-permute-done((bf16[2,512,512]{2,1,0:T(8,128)(2,1)S(1)}, bf16[2,512,512]{2,1,0:T(8,128)(2,1)S(1)}, u32[]{:S(2)}, u32[]{:S(2)}) %collective-permute-start.28) | collective-permute-done | bytes 1048608 | tf_op jit(solution)/shard_map/ppermute | solution.py:43
  341.8 8.7 %collective-permute-done.48.refs_3_ = bf16[2,512,512]{2,1,0:T(8,128)(2,1)S(1)} collective-permute-done((bf16[2,512,512]{2,1,0:T(8,128)(2,1)S(1)}, bf16[2,512,512]{2,1,0:T(8,128)(2,1)S(1)}, u32[]{:S(2)}, u32[]{:S(2)}) %collective-permute-start.48) | collective-permute-done | bytes 1048608 | tf_op jit(solution)/shard_map/ppermute | solution.py:43
  353.1 8.6 %collective-permute-done.24.refs_3_ = bf16[2,512,512]{2,1,0:T(8,128)(2,1)S(1)} collective-permute-done((bf16[2,512,512]{2,1,0:T(8,128)(2,1)S(1)}, bf16[2,512,512]{2,1,0:T(8,128)(2,1)S(1)}, u32[]{:S(2)}, u32[]{:S(2)}) %collective-permute-start.24) | collective-permute-done | bytes 1048608 | tf_op jit(solution)/shard_map/ppermute | solution.py:43
  364.3 8.7 %collective-permute-done.44.refs_3_ = bf16[2,512,512]{2,1,0:T(8,128)(2,1)S(1)} collective-permute-done((bf16[2,512,512]{2,1,0:T(8,128)(2,1)S(1)}, bf16[2,512,512]{2,1,0:T(8,128)(2,1)S(1)}, u32[]{:S(2)}, u32[]{:S(2)}) %collective-permute-start.44) | collective-permute-done | bytes 1048608 | tf_op jit(solution)/shard_map/ppermute | solution.py:43
  376.2 3.0 collective-permute-start.30
  380.1 11.2 %collective-permute-done.30.refs_5_ = bf16[1,512,512]{2,1,0:T(8,128)(2,1)S(1)} collective-permute-done((bf16[1,512,512]{2,1,0:T(8,128)(2,1)S(1)}, bf16[1,512,512]{2,1,0:T(8,128)(2,1)S(1)}, u32[]{:S(2)}, u32[]{:S(2)}) %collective-permute-start.30) | collective-permute-done | bytes 524320 | tf_op jit(solution)/shard_map/ppermute | solution.py:43
  392.1 10.4 %collective-permute-done.50.refs_5_ = bf16[1,512,512]{2,1,0:T(8,128)(2,1)S(1)} collective-permute-done((bf16[1,512,512]{2,1,0:T(8,128)(2,1)S(1)}, bf16[1,512,512]{2,1,0:T(8,128)(2,1)S(1)}, u32[]{:S(2)}, u32[]{:S(2)}) %collective-permute-start.50) | collective-permute-done | bytes 524320 | tf_op jit(solution)/shard_map/ppermute | solution.py:43
  (175 shorter events, 70.9 us)
Async XLA Ops:
  3.0 76.8 %all-to-all-start = ((s32[8,1,2]{2,1,0:T(1,128)}), s32[8,1,2]{2,1,0:T(1,128)S(1)}, u32[]{:S(2)}, u32[]{:S(2)}) async-start(s32[8,1,2]{2,1,0:T(1,128)} %copy.9), calls=%async_computation | async-start | bytes 8192 | tf_op jit(solution)/shard_map/all_to_all | solution.py:416
  99.9 17.5 %all-to-all-start.1 = ((bf16[8,272,256]{2,1,0:T(8,128)(2,1)}), bf16[8,272,256]{2,1,0:T(8,128)(2,1)S(1)}, u32[]{:S(2)}, u32[]{:S(2)}) async-start(bf16[8,272,256]{2,1,0:T(8,128)(2,1)} %get-tuple-element.13), calls=%async_computation.1 | async-start | bytes 2228224 | tf_op jit(solution)/shard_map/all_to_all | solution.py:419
  106.7 21.0 %collective-permute-start.16 = (bf16[1024,256]{1,0:T(8,128)(2,1)S(1)}, bf16[1024,256]{1,0:T(8,128)(2,1)S(1)}, u32[]{:S(2)}, u32[]{:S(2)}) collective-permute-start(bf16[1024,256]{1,0:T(8,128)(2,1)S(1)} %pack.3), channel_id=1, source_target_pairs={{0,8},{1,9},{2,10},{3,11},{4,12},{5,13},{6,14},{7,15},{8,0},{9,1},... | collective-permute-start | bytes 1572872 | tf_op jit(solution)/shard_map/ppermute | solution.py:43
  109.3 37.5 %collective-permute-start.11 = (bf16[1024,256]{1,0:T(8,128)(2,1)S(1)}, bf16[1024,256]{1,0:T(8,128)(2,1)S(1)}, u32[]{:S(2)}, u32[]{:S(2)}) collective-permute-start(bf16[1024,256]{1,0:T(8,128)(2,1)S(1)} %pack.3), channel_id=1, source_target_pairs={{0,1},{1,0},{2,3},{3,2},{4,5},{5,4},{6,7},{7,6},{8,9},{9,8},{10,11... | collective-permute-start | bytes 1572872 | tf_op jit(solution)/shard_map/ppermute | solution.py:43
  120.4 13.5 %collective-permute-start = (bf16[512,256]{1,0:T(8,128)(2,1)S(1)}, bf16[512,256]{1,0:T(8,128)(2,1)S(1)}, u32[]{:S(2)}, u32[]{:S(2)}) collective-permute-start(bf16[512,256]{1,0:T(8,128)(2,1)S(1)} %get-tuple-element.28), channel_id=1, source_target_pairs={{0,1},{1,0},{2,3},{3,2},{4,5},{5,4},{6,7},{7,6},{8,9},{9,8},{10,11... | collective-permute-start | bytes 786440 | tf_op jit(solution)/shard_map/ppermute | solution.py:43
  127.8 19.1 %collective-permute-start.17 = (bf16[1024,256]{1,0:T(8,128)(2,1)S(1)}, bf16[1024,256]{1,0:T(8,128)(2,1)S(1)}, u32[]{:S(2)}, u32[]{:S(2)}) collective-permute-start(bf16[1024,256]{1,0:T(8,128)(2,1)S(1)} %collective-permute-done.16), channel_id=1, source_target_pairs={{0,1},{1,0},{2,3},{3,2},{4,5},{5,4},{6,7},{7,6},{8,9},{9,8},{10,11... | collective-permute-start | bytes 1572872 | tf_op jit(solution)/shard_map/ppermute | solution.py:43
  130.9 9.4 %collective-permute-start.5 = (bf16[512,256]{1,0:T(8,128)(2,1)S(1)}, bf16[512,256]{1,0:T(8,128)(2,1)S(1)}, u32[]{:S(2)}, u32[]{:S(2)}) collective-permute-start(bf16[512,256]{1,0:T(8,128)(2,1)S(1)} %get-tuple-element.28), channel_id=1, source_target_pairs={{0,8},{1,9},{2,10},{3,11},{4,12},{5,13},{6,14},{7,15},{8,0},{9,1},... | collective-permute-start | bytes 786440 | tf_op jit(solution)/shard_map/ppermute | solution.py:43
  131.4 14.5 %collective-permute-start.36 = (bf16[512,256]{1,0:T(8,128)(2,1)S(1)}, bf16[512,256]{1,0:T(8,128)(2,1)S(1)}, u32[]{:S(2)}, u32[]{:S(2)}) collective-permute-start(bf16[512,256]{1,0:T(8,128)(2,1)S(1)} %get-tuple-element.27), channel_id=1, source_target_pairs={{0,8},{1,9},{2,10},{3,11},{4,12},{5,13},{6,14},{7,15},{8,0},{9,1},... | collective-permute-start | bytes 786440 | tf_op jit(solution)/shard_map/ppermute | solution.py:43
  133.9 16.9 %collective-permute-start.31 = (bf16[512,256]{1,0:T(8,128)(2,1)S(1)}, bf16[512,256]{1,0:T(8,128)(2,1)S(1)}, u32[]{:S(2)}, u32[]{:S(2)}) collective-permute-start(bf16[512,256]{1,0:T(8,128)(2,1)S(1)} %get-tuple-element.27), channel_id=1, source_target_pairs={{0,1},{1,0},{2,3},{3,2},{4,5},{5,4},{6,7},{7,6},{8,9},{9,8},{10,11... | collective-permute-start | bytes 786440 | tf_op jit(solution)/shard_map/ppermute | solution.py:43
  140.4 11.5 %collective-permute-start.1 = (bf16[2,512,256]{2,1,0:T(8,128)(2,1)S(1)}, bf16[2,512,256]{2,1,0:T(8,128)(2,1)S(1)}, u32[]{:S(2)}, u32[]{:S(2)}) collective-permute-start(bf16[2,512,256]{2,1,0:T(8,128)(2,1)S(1)} %pad_maximum_fusion.3.refs_1_), channel_id=1, source_target_pairs={{0,2},{1,7},{2,4},{3,1},{4,6},{5,3},{6,0},{7,5},{8,10},{9,15},{10,... | collective-permute-start | bytes 1572872 | tf_op jit(solution)/shard_map/ppermute | solution.py:43
  146.9 50.3 %collective-permute-start.12 = (bf16[2,1024,256]{2,1,0:T(8,128)(2,1)S(1)}, bf16[2,1024,256]{2,1,0:T(8,128)(2,1)S(1)}, u32[]{:S(2)}, u32[]{:S(2)}) collective-permute-start(bf16[2,1024,256]{2,1,0:T(8,128)(2,1)S(1)} %pad_maximum_fusion.refs_1_), channel_id=1, source_target_pairs={{0,2},{1,7},{2,4},{3,1},{4,6},{5,3},{6,0},{7,5},{8,10},{9,15},{10,... | collective-permute-start | bytes 3145736 | tf_op jit(solution)/shard_map/ppermute | solution.py:43
  150.8 48.5 %collective-permute-start.18 = (bf16[2,1024,256]{2,1,0:T(8,128)(2,1)}, bf16[2,1024,256]{2,1,0:T(8,128)(2,1)}, u32[]{:S(2)}, u32[]{:S(2)}) collective-permute-start(bf16[2,1024,256]{2,1,0:T(8,128)(2,1)} %pad_maximum_fusion.1.refs_6_), channel_id=1, source_target_pairs={{0,2},{1,7},{2,4},{3,1},{4,6},{5,3},{6,0},{7,5},{8,10},{9,15},{10,... | collective-permute-start | bytes 3145736 | tf_op jit(solution)/shard_map/ppermute | solution.py:43
  151.3 27.0 %collective-permute-start.32 = (bf16[2,512,256]{2,1,0:T(8,128)(2,1)S(1)}, bf16[2,512,256]{2,1,0:T(8,128)(2,1)}, u32[]{:S(2)}, u32[]{:S(2)}) collective-permute-start(bf16[2,512,256]{2,1,0:T(8,128)(2,1)S(1)} %pad_maximum_fusion.5.refs_1_), channel_id=1, source_target_pairs={{0,2},{1,7},{2,4},{3,1},{4,6},{5,3},{6,0},{7,5},{8,10},{9,15},{10,... | collective-permute-start | bytes 1572872 | tf_op jit(solution)/shard_map/ppermute | solution.py:43
  151.6 32.3 %collective-permute-start.7 = (bf16[2,512,256]{2,1,0:T(8,128)(2,1)S(1)}, bf16[2,512,256]{2,1,0:T(8,128)(2,1)}, u32[]{:S(2)}, u32[]{:S(2)}) collective-permute-start(bf16[2,512,256]{2,1,0:T(8,128)(2,1)S(1)} %pad_maximum_fusion.4.refs_6_), channel_id=1, source_target_pairs={{0,2},{1,7},{2,4},{3,1},{4,6},{5,3},{6,0},{7,5},{8,10},{9,15},{10,... | collective-permute-start | bytes 1572872 | tf_op jit(solution)/shard_map/ppermute | solution.py:43
  151.9 43.5 %collective-permute-start.38 = (bf16[2,512,256]{2,1,0:T(8,128)(2,1)S(1)}, bf16[2,512,256]{2,1,0:T(8,128)(2,1)}, u32[]{:S(2)}, u32[]{:S(2)}) collective-permute-start(bf16[2,512,256]{2,1,0:T(8,128)(2,1)S(1)} %pad_maximum_fusion.6.refs_6_), channel_id=1, source_target_pairs={{0,2},{1,7},{2,4},{3,1},{4,6},{5,3},{6,0},{7,5},{8,10},{9,15},{10,... | collective-permute-start | bytes 1572872 | tf_op jit(solution)/shard_map/ppermute | solution.py:43
  178.3 14.0 %collective-permute-start.3 = (bf16[1,512,256]{2,1,0:T(8,128)(2,1)S(1)}, bf16[1,512,256]{2,1,0:T(8,128)(2,1)S(1)}, u32[]{:S(2)}, u32[]{:S(2)}) collective-permute-start(bf16[1,512,256]{2,1,0:T(8,128)(2,1)S(1)} %slice.41), channel_id=1, source_target_pairs={{0,2},{1,7},{2,4},{3,1},{4,6},{5,3},{6,0},{7,5},{8,10},{9,15},{10,... | collective-permute-start | bytes 786440 | tf_op jit(solution)/shard_map/ppermute | solution.py:43
  183.9 16.5 %collective-permute-start.34 = (bf16[1,512,256]{2,1,0:T(8,128)(2,1)}, bf16[1,512,256]{2,1,0:T(8,128)(2,1)S(1)}, u32[]{:S(2)}, u32[]{:S(2)}) collective-permute-start(bf16[1,512,256]{2,1,0:T(8,128)(2,1)} %slice.46), channel_id=1, source_target_pairs={{0,2},{1,7},{2,4},{3,1},{4,6},{5,3},{6,0},{7,5},{8,10},{9,15},{10,... | collective-permute-start | bytes 786440 | tf_op jit(solution)/shard_map/ppermute | solution.py:43
  192.3 9.8 %collective-permute-start.9 = (bf16[1,512,256]{2,1,0:T(8,128)(2,1)}, bf16[1,512,256]{2,1,0:T(8,128)(2,1)S(1)}, u32[]{:S(2)}, u32[]{:S(2)}) collective-permute-start(bf16[1,512,256]{2,1,0:T(8,128)(2,1)} %slice.42), channel_id=1, source_target_pairs={{0,2},{1,7},{2,4},{3,1},{4,6},{5,3},{6,0},{7,5},{8,10},{9,15},{10,... | collective-permute-start | bytes 786440 | tf_op jit(solution)/shard_map/ppermute | solution.py:43
  200.5 8.4 %collective-permute-start.14 = (bf16[1,1024,256]{2,1,0:T(8,128)(2,1)S(1)}, bf16[1,1024,256]{2,1,0:T(8,128)(2,1)S(1)}, u32[]{:S(2)}, u32[]{:S(2)}) collective-permute-start(bf16[1,1024,256]{2,1,0:T(8,128)(2,1)S(1)} %slice.43), channel_id=1, source_target_pairs={{0,2},{1,7},{2,4},{3,1},{4,6},{5,3},{6,0},{7,5},{8,10},{9,15},{10,... | collective-permute-start | bytes 1572872 | tf_op jit(solution)/shard_map/ppermute | solution.py:43
  202.1 12.4 %collective-permute-start.20 = (bf16[1,1024,256]{2,1,0:T(8,128)(2,1)S(1)}, bf16[1,1024,256]{2,1,0:T(8,128)(2,1)S(1)}, u32[]{:S(2)}, u32[]{:S(2)}) collective-permute-start(bf16[1,1024,256]{2,1,0:T(8,128)(2,1)S(1)} %slice.44), channel_id=1, source_target_pairs={{0,2},{1,7},{2,4},{3,1},{4,6},{5,3},{6,0},{7,5},{8,10},{9,15},{10,... | collective-permute-start | bytes 1572872 | tf_op jit(solution)/shard_map/ppermute | solution.py:43
  202.3 21.2 %collective-permute-start.13 = (bf16[2,1024,256]{2,1,0:T(8,128)(2,1)S(1)}, bf16[2,1024,256]{2,1,0:T(8,128)(2,1)S(1)}, u32[]{:S(2)}, u32[]{:S(2)}) collective-permute-start(bf16[2,1024,256]{2,1,0:T(8,128)(2,1)S(1)} %collective-permute-done.12.refs_2_), channel_id=1, source_target_pairs={{0,1},{1,0},{2,3},{3,2},{4,5},{5,4},{6,7},{7,6},{8,9},{9,8},{10,11... | collective-permute-start | bytes 3145736 | tf_op jit(solution)/shard_map/ppermute | solution.py:43
  203.1 21.0 %collective-permute-start.19 = (bf16[2,1024,256]{2,1,0:T(8,128)(2,1)}, bf16[2,1024,256]{2,1,0:T(8,128)(2,1)S(1)}, u32[]{:S(2)}, u32[]{:S(2)}) collective-permute-start(bf16[2,1024,256]{2,1,0:T(8,128)(2,1)} %collective-permute-done.18.refs_7_), channel_id=1, source_target_pairs={{0,1},{1,0},{2,3},{3,2},{4,5},{5,4},{6,7},{7,6},{8,9},{9,8},{10,11... | collective-permute-start | bytes 3145736 | tf_op jit(solution)/shard_map/ppermute | solution.py:43
  205.7 11.5 %collective-permute-start.10 = (bf16[1,512,256]{2,1,0:T(8,128)(2,1)S(1)}, bf16[1,512,256]{2,1,0:T(8,128)(2,1)S(1)}, u32[]{:S(2)}, u32[]{:S(2)}) collective-permute-start(bf16[1,512,256]{2,1,0:T(8,128)(2,1)S(1)} %collective-permute-done.9.refs_9_), channel_id=1, source_target_pairs={{0,1},{1,0},{2,3},{3,2},{4,5},{5,4},{6,7},{7,6},{8,9},{9,8},{10,11... | collective-permute-start | bytes 786440 | tf_op jit(solution)/shard_map/ppermute | solution.py:43
  208.9 14.1 %collective-permute-start.15 = (bf16[1,1024,256]{2,1,0:T(8,128)(2,1)S(1)}, bf16[1,1024,256]{2,1,0:T(8,128)(2,1)S(1)}, u32[]{:S(2)}, u32[]{:S(2)}) collective-permute-start(bf16[1,1024,256]{2,1,0:T(8,128)(2,1)S(1)} %collective-permute-done.14.refs_4_), channel_id=1, source_target_pairs={{0,1},{1,0},{2,3},{3,2},{4,5},{5,4},{6,7},{7,6},{8,9},{9,8},{10,11... | collective-permute-start | bytes 1572872 | tf_op jit(solution)/shard_map/ppermute | solution.py:43
  214.5 9.1 %collective-permute-start.21 = (bf16[1,1024,256]{2,1,0:T(8,128)(2,1)S(1)}, bf16[1,1024,256]{2,1,0:T(8,128)(2,1)S(1)}, u32[]{:S(2)}, u32[]{:S(2)}) collective-permute-start(bf16[1,1024,256]{2,1,0:T(8,128)(2,1)S(1)} %collective-permute-done.20.refs_9_), channel_id=1, source_target_pairs={{0,1},{1,0},{2,3},{3,2},{4,5},{5,4},{6,7},{7,6},{8,9},{9,8},{10,11... | collective-permute-start | bytes 1572872 | tf_op jit(solution)/shard_map/ppermute | solution.py:43
  217.1 20.7 %collective-permute-start.8 = (bf16[2,512,256]{2,1,0:T(8,128)(2,1)}, bf16[2,512,256]{2,1,0:T(8,128)(2,1)S(1)}, u32[]{:S(2)}, u32[]{:S(2)}) collective-permute-start(bf16[2,512,256]{2,1,0:T(8,128)(2,1)} %collective-permute-done.7.refs_7_), channel_id=1, source_target_pairs={{0,1},{1,0},{2,3},{3,2},{4,5},{5,4},{6,7},{7,6},{8,9},{9,8},{10,11... | collective-permute-start | bytes 1572872 | tf_op jit(solution)/shard_map/ppermute | solution.py:43
  223.0 27.7 %collective-permute-start.33 = (bf16[2,512,256]{2,1,0:T(8,128)(2,1)}, bf16[2,512,256]{2,1,0:T(8,128)(2,1)}, u32[]{:S(2)}, u32[]{:S(2)}) collective-permute-start(bf16[2,512,256]{2,1,0:T(8,128)(2,1)} %collective-permute-done.32.refs_2_), channel_id=1, source_target_pairs={{0,1},{1,0},{2,3},{3,2},{4,5},{5,4},{6,7},{7,6},{8,9},{9,8},{10,11... | collective-permute-start | bytes 1572872 | tf_op jit(solution)/shard_map/ppermute | solution.py:43
  223.5 27.2 %collective-permute-start.39 = (bf16[2,512,256]{2,1,0:T(8,128)(2,1)}, bf16[2,512,256]{2,1,0:T(8,128)(2,1)}, u32[]{:S(2)}, u32[]{:S(2)}) collective-permute-start(bf16[2,512,256]{2,1,0:T(8,128)(2,1)} %collective-permute-done.38.refs_7_), channel_id=1, source_target_pairs={{0,1},{1,0},{2,3},{3,2},{4,5},{5,4},{6,7},{7,6},{8,9},{9,8},{10,11... | collective-permute-start | bytes 1572872 | tf_op jit(solution)/shard_map/ppermute | solution.py:43
  223.6 27.0 %collective-permute-start.35 = (bf16[1,512,256]{2,1,0:T(8,128)(2,1)S(1)}, bf16[1,512,256]{2,1,0:T(8,128)(2,1)}, u32[]{:S(2)}, u32[]{:S(2)}) collective-permute-start(bf16[1,512,256]{2,1,0:T(8,128)(2,1)S(1)} %collective-permute-done.34.refs_4_), channel_id=1, source_target_pairs={{0,1},{1,0},{2,3},{3,2},{4,5},{5,4},{6,7},{7,6},{8,9},{9,8},{10,11... | collective-permute-start | bytes 786440 | tf_op jit(solution)/shard_map/ppermute | solution.py:43
  224.0 26.6 %collective-permute-start.41 = (bf16[1,512,256]{2,1,0:T(8,128)(2,1)}, bf16[1,512,256]{2,1,0:T(8,128)(2,1)}, u32[]{:S(2)}, u32[]{:S(2)}) collective-permute-start(bf16[1,512,256]{2,1,0:T(8,128)(2,1)} %collective-permute-done.40.refs_9_), channel_id=1, source_target_pairs={{0,1},{1,0},{2,3},{3,2},{4,5},{5,4},{6,7},{7,6},{8,9},{9,8},{10,11... | collective-permute-start | bytes 786440 | tf_op jit(solution)/shard_map/ppermute | solution.py:43
  247.2 13.1 %all-to-all-start.3 = ((bf16[16,16,512]{2,1,0:T(8,128)(2,1)}), bf16[16,16,512]{2,1,0:T(8,128)(2,1)S(1)}, u32[]{:S(2)}, u32[]{:S(2)}) async-start(bf16[16,16,512]{2,1,0:T(8,128)(2,1)} %bitcast.40), calls=%async_computation.3 | async-start | bytes 524288 | tf_op jit(solution)/shard_map/all_to_all | solution.py:446
  261.1 25.9 %all-to-all-start.4 = ((bf16[16,16,512]{2,1,0:T(8,128)(2,1)}), bf16[16,16,512]{2,1,0:T(8,128)(2,1)S(1)}, u32[]{:S(2)}, u32[]{:S(2)}) async-start(bf16[16,16,512]{2,1,0:T(8,128)(2,1)} %bitcast.49), calls=%async_computation.4 | async-start | bytes 524288 | tf_op jit(solution)/shard_map/all_to_all | solution.py:446
  277.2 24.2 %collective-permute-start.26 = (bf16[3,512,512]{2,1,0:T(8,128)(2,1)}, bf16[3,512,512]{2,1,0:T(8,128)(2,1)S(1)}, u32[]{:S(2)}, u32[]{:S(2)}) collective-permute-start(bf16[3,512,512]{2,1,0:T(8,128)(2,1)} %chunks.24), channel_id=1, source_target_pairs={{0,1},{1,0},{2,3},{3,2},{4,5},{5,4},{6,7},{7,6},{8,9},{9,8},{10,11... | collective-permute-start | bytes 4718600 | tf_op jit(solution)/shard_map/ppermute | solution.py:43
  295.4 9.6 %collective-permute-start.46 = (bf16[3,512,512]{2,1,0:T(8,128)(2,1)S(1)}, bf16[3,512,512]{2,1,0:T(8,128)(2,1)S(1)}, u32[]{:S(2)}, u32[]{:S(2)}) collective-permute-start(bf16[3,512,512]{2,1,0:T(8,128)(2,1)S(1)} %chunks.34), channel_id=1, source_target_pairs={{0,1},{1,0},{2,3},{3,2},{4,5},{5,4},{6,7},{7,6},{8,9},{9,8},{10,11... | collective-permute-start | bytes 4718600 | tf_op jit(solution)/shard_map/ppermute | solution.py:43
  302.1 9.0 %collective-permute-start.27 = (bf16[1,512,512]{2,1,0:T(8,128)(2,1)S(1)}, bf16[1,512,512]{2,1,0:T(8,128)(2,1)S(1)}, u32[]{:S(2)}, u32[]{:S(2)}) collective-permute-start(bf16[1,512,512]{2,1,0:T(8,128)(2,1)S(1)} %chunks.25), channel_id=1, source_target_pairs={{0,2},{1,7},{2,4},{3,1},{4,6},{5,3},{6,0},{7,5},{8,10},{9,15},{10,... | collective-permute-start | bytes 1572872 | tf_op jit(solution)/shard_map/ppermute | solution.py:43
  305.7 11.1 %collective-permute-start.47 = (bf16[1,512,512]{2,1,0:T(8,128)(2,1)S(1)}, bf16[1,512,512]{2,1,0:T(8,128)(2,1)S(1)}, u32[]{:S(2)}, u32[]{:S(2)}) collective-permute-start(bf16[1,512,512]{2,1,0:T(8,128)(2,1)S(1)} %chunks.35), channel_id=1, source_target_pairs={{0,2},{1,7},{2,4},{3,1},{4,6},{5,3},{6,0},{7,5},{8,10},{9,15},{10,... | collective-permute-start | bytes 1572872 | tf_op jit(solution)/shard_map/ppermute | solution.py:43
  307.1 15.3 %collective-permute-start.23 = (bf16[1,512,512]{2,1,0:T(8,128)(2,1)S(1)}, bf16[1,512,512]{2,1,0:T(8,128)(2,1)S(1)}, u32[]{:S(2)}, u32[]{:S(2)}) collective-permute-start(bf16[1,512,512]{2,1,0:T(8,128)(2,1)S(1)} %chunks.21), channel_id=1, source_target_pairs={{0,2},{1,7},{2,4},{3,1},{4,6},{5,3},{6,0},{7,5},{8,10},{9,15},{10,... | collective-permute-start | bytes 1572872 | tf_op jit(solution)/shard_map/ppermute | solution.py:43
  308.2 19.9 %collective-permute-start.43 = (bf16[1,512,512]{2,1,0:T(8,128)(2,1)S(1)}, bf16[1,512,512]{2,1,0:T(8,128)(2,1)S(1)}, u32[]{:S(2)}, u32[]{:S(2)}) collective-permute-start(bf16[1,512,512]{2,1,0:T(8,128)(2,1)S(1)} %chunks.31), channel_id=1, source_target_pairs={{0,2},{1,7},{2,4},{3,1},{4,6},{5,3},{6,0},{7,5},{8,10},{9,15},{10,... | collective-permute-start | bytes 1572872 | tf_op jit(solution)/shard_map/ppermute | solution.py:43
  312.8 26.4 %collective-permute-start.28 = (bf16[2,512,512]{2,1,0:T(8,128)(2,1)S(1)}, bf16[2,512,512]{2,1,0:T(8,128)(2,1)S(1)}, u32[]{:S(2)}, u32[]{:S(2)}) collective-permute-start(bf16[2,512,512]{2,1,0:T(8,128)(2,1)S(1)} %chunks.26), channel_id=1, source_target_pairs={{0,2},{1,7},{2,4},{3,1},{4,6},{5,3},{6,0},{7,5},{8,10},{9,15},{10,... | collective-permute-start | bytes 3145736 | tf_op jit(solution)/shard_map/ppermute | solution.py:43
  318.4 32.0 %collective-permute-start.48 = (bf16[2,512,512]{2,1,0:T(8,128)(2,1)S(1)}, bf16[2,512,512]{2,1,0:T(8,128)(2,1)S(1)}, u32[]{:S(2)}, u32[]{:S(2)}) collective-permute-start(bf16[2,512,512]{2,1,0:T(8,128)(2,1)S(1)} %chunks.36), channel_id=1, source_target_pairs={{0,2},{1,7},{2,4},{3,1},{4,6},{5,3},{6,0},{7,5},{8,10},{9,15},{10,... | collective-permute-start | bytes 3145736 | tf_op jit(solution)/shard_map/ppermute | solution.py:43
  324.0 37.7 %collective-permute-start.24 = (bf16[2,512,512]{2,1,0:T(8,128)(2,1)S(1)}, bf16[2,512,512]{2,1,0:T(8,128)(2,1)S(1)}, u32[]{:S(2)}, u32[]{:S(2)}) collective-permute-start(bf16[2,512,512]{2,1,0:T(8,128)(2,1)S(1)} %chunks.22), channel_id=1, source_target_pairs={{0,2},{1,7},{2,4},{3,1},{4,6},{5,3},{6,0},{7,5},{8,10},{9,15},{10,... | collective-permute-start | bytes 3145736 | tf_op jit(solution)/shard_map/ppermute | solution.py:43
  329.7 43.3 %collective-permute-start.44 = (bf16[2,512,512]{2,1,0:T(8,128)(2,1)S(1)}, bf16[2,512,512]{2,1,0:T(8,128)(2,1)S(1)}, u32[]{:S(2)}, u32[]{:S(2)}) collective-permute-start(bf16[2,512,512]{2,1,0:T(8,128)(2,1)S(1)} %chunks.32), channel_id=1, source_target_pairs={{0,2},{1,7},{2,4},{3,1},{4,6},{5,3},{6,0},{7,5},{8,10},{9,15},{10,... | collective-permute-start | bytes 3145736 | tf_op jit(solution)/shard_map/ppermute | solution.py:43
  339.9 35.6 %collective-permute-start.29 = (bf16[1,512,512]{2,1,0:T(8,128)(2,1)S(1)}, bf16[1,512,512]{2,1,0:T(8,128)(2,1)S(1)}, u32[]{:S(2)}, u32[]{:S(2)}) collective-permute-start(bf16[1,512,512]{2,1,0:T(8,128)(2,1)S(1)} %chunks.27), channel_id=1, source_target_pairs={{0,1},{1,0},{2,3},{3,2},{4,5},{5,4},{6,7},{7,6},{8,9},{9,8},{10,11... | collective-permute-start | bytes 1572872 | tf_op jit(solution)/shard_map/ppermute | solution.py:43
  351.2 28.1 %collective-permute-start.49 = (bf16[1,512,512]{2,1,0:T(8,128)(2,1)S(1)}, bf16[1,512,512]{2,1,0:T(8,128)(2,1)S(1)}, u32[]{:S(2)}, u32[]{:S(2)}) collective-permute-start(bf16[1,512,512]{2,1,0:T(8,128)(2,1)S(1)} %chunks.37), channel_id=1, source_target_pairs={{0,1},{1,0},{2,3},{3,2},{4,5},{5,4},{6,7},{7,6},{8,9},{9,8},{10,11... | collective-permute-start | bytes 1572872 | tf_op jit(solution)/shard_map/ppermute | solution.py:43
  362.4 17.7 %collective-permute-start.25 = (bf16[1,512,512]{2,1,0:T(8,128)(2,1)S(1)}, bf16[1,512,512]{2,1,0:T(8,128)(2,1)S(1)}, u32[]{:S(2)}, u32[]{:S(2)}) collective-permute-start(bf16[1,512,512]{2,1,0:T(8,128)(2,1)S(1)} %chunks.23), channel_id=1, source_target_pairs={{0,1},{1,0},{2,3},{3,2},{4,5},{5,4},{6,7},{7,6},{8,9},{9,8},{10,11... | collective-permute-start | bytes 1572872 | tf_op jit(solution)/shard_map/ppermute | solution.py:43
  373.6 18.5 %collective-permute-start.45 = (bf16[1,512,512]{2,1,0:T(8,128)(2,1)S(1)}, bf16[1,512,512]{2,1,0:T(8,128)(2,1)S(1)}, u32[]{:S(2)}, u32[]{:S(2)}) collective-permute-start(bf16[1,512,512]{2,1,0:T(8,128)(2,1)S(1)} %chunks.33), channel_id=1, source_target_pairs={{0,1},{1,0},{2,3},{3,2},{4,5},{5,4},{6,7},{7,6},{8,9},{9,8},{10,11... | collective-permute-start | bytes 1572872 | tf_op jit(solution)/shard_map/ppermute | solution.py:43
  376.2 15.1 %collective-permute-start.30 = (bf16[1,512,512]{2,1,0:T(8,128)(2,1)S(1)}, bf16[1,512,512]{2,1,0:T(8,128)(2,1)S(1)}, u32[]{:S(2)}, u32[]{:S(2)}) collective-permute-start(bf16[1,512,512]{2,1,0:T(8,128)(2,1)S(1)} %chunks.28), channel_id=1, source_target_pairs={{0,8},{1,9},{2,10},{3,11},{4,12},{5,13},{6,14},{7,15},{8,0},{9,1},... | collective-permute-start | bytes 1572872 | tf_op jit(solution)/shard_map/ppermute | solution.py:43
  379.9 22.6 %collective-permute-start.50 = (bf16[1,512,512]{2,1,0:T(8,128)(2,1)S(1)}, bf16[1,512,512]{2,1,0:T(8,128)(2,1)S(1)}, u32[]{:S(2)}, u32[]{:S(2)}) collective-permute-start(bf16[1,512,512]{2,1,0:T(8,128)(2,1)S(1)} %chunks.38), channel_id=1, source_target_pairs={{0,8},{1,9},{2,10},{3,11},{4,12},{5,13},{6,14},{7,15},{8,0},{9,1},... | collective-permute-start | bytes 1572872 | tf_op jit(solution)/shard_map/ppermute | solution.py:43
  (29 other events, 427.8 us)

commit v2 on v1

v2 whole, which is shorter than its diff:
```python
import functools
import math

import jax
import jax.numpy as jnp
from jax import lax
from jax.experimental import pallas as pl
from jax.experimental.pallas import tpu as pltpu
from jax.sharding import PartitionSpec as P

HQ = 64
KVH = 8
HD = 128
CAP = 1024
SLOT = 256
ALIGN = 16
SENT = SLOT + ALIGN
TILE = 256
BLOCK = 512
rope_base = 500000.0
BF = jnp.bfloat16
F32 = jnp.float32


def params():
    return pltpu.CompilerParams(vmem_limit_bytes=14 << 20)


def permutation(move):
    pairs = []
    for t in range(16):
        x, y, c = move(t // 8, t // 2 % 4, t % 2)
        pairs.append((t, x % 2 * 8 + y % 4 * 2 + c % 2))
    return pairs


TO_CORE = permutation(lambda x, y, c: (x, y, c + 1))
TO_X = permutation(lambda x, y, c: (x + 1, y, c))
TO_Y = permutation(lambda x, y, c: (x, y + 1 - 2 * c, c))


def after(value, *others):
    return lax.optimization_barrier((value, *others))[0]


class Line:
    def __init__(self):
        self.last = None

    def next(self, value):
        return value if self.last is None else after(value, self.last)

    def add(self, result):
        self.last = jax.tree.leaves(result)[0]
        return result


def send(value, pairs):
    return lax.ppermute(value, "tp", pairs)


def in_hbm(array):
    return pltpu.with_memory_space_constraint(array, pltpu.HBM)


def cut_kernel(start_ref, rollout_ref, sent_ref):
    for d in range(8):
        row = pl.multiple_of(start_ref[d], ALIGN)
        sent_ref[d] = rollout_ref[pl.ds(row, SENT), :]


def cut(rollout, starts):
    return pl.pallas_call(
        cut_kernel,
        out_shape=jax.ShapeDtypeStruct((8, SENT, rollout.shape[1]), BF),
        in_specs=[
            pl.BlockSpec(memory_space=pltpu.SMEM),
            pl.BlockSpec(memory_space=pltpu.VMEM),
        ],
        out_specs=pl.BlockSpec(memory_space=pltpu.VMEM),
        compiler_params=params(),
        name="cut",
    )(starts, rollout)


def pack_kernel(plan_ref, arrived_ref, packed_ref, total_ref):
    first = pl.program_id(0) * TILE
    rows = first + lax.broadcasted_iota(jnp.int32, (TILE, 1), 0)
    slots = lax.broadcasted_iota(jnp.int32, (TILE, SENT), 1)
    total_ref[...] = jnp.zeros_like(total_ref)
    for s in range(8):
        begin, end = plan_ref[0, s], plan_ref[1, s]

        @pl.when((begin < first + TILE) & (end > first))
        def _():
            source = jnp.where(
                (rows >= begin) & (rows < end), rows + plan_ref[2, s], -1
            )
            picked = jnp.where(slots == source, 1.0, 0.0).astype(BF)
            total_ref[...] += jnp.dot(
                picked, arrived_ref[s], preferred_element_type=F32
            )

    packed_ref[...] = total_ref[...].astype(BF)


def pack(arrived, plan):
    width = arrived.shape[2]
    return pl.pallas_call(
        pack_kernel,
        out_shape=jax.ShapeDtypeStruct((CAP, width), BF),
        grid_spec=pltpu.PrefetchScalarGridSpec(
            num_scalar_prefetch=1,
            grid=(CAP // TILE,),
            in_specs=[pl.BlockSpec(memory_space=pltpu.VMEM)],
            out_specs=pl.BlockSpec((TILE, width), lambda i, p: (i, 0)),
            scratch_shapes=[pltpu.VMEM((TILE, width), F32)],
        ),
        compiler_params=params(),
        name="pack",
    )(plan, arrived)


def swap_members(values):
    lanes = lax.broadcasted_iota(jnp.int32, values.shape, 1)
    return jnp.where(
        lanes % 2 == 0, pltpu.roll(values, HD - 1, 1), pltpu.roll(values, 1, 1)
    )


def project_kernel(counts, has_total, last, index_ref, *refs):
    refs = list(refs)
    pieces = [refs.pop(0) for _ in counts]
    query_w, keyval_w = refs.pop(0), refs.pop(0)
    total_ref = refs.pop(0) if has_total else None
    tables = [refs.pop(0) for _ in range(4)] if last else None
    weights_ref, sems = refs[-2:]
    refs = refs[:-2]
    columns = query_w.shape[1]
    depth = pieces[0].shape[2]
    copies = []
    for k in range(sum(counts)):
        rows = pl.ds(pl.multiple_of(index_ref[k] * depth, depth), depth)
        copies.append((
            pltpu.make_async_copy(
                query_w.at[rows, :], weights_ref.at[k, :, pl.ds(0, columns)], sems.at[k, 0]
            ),
            pltpu.make_async_copy(
                keyval_w.at[rows, :], weights_ref.at[k, :, pl.ds(columns, HD)], sems.at[k, 1]
            ),
        ))

    @pl.when(pl.program_id(0) == 0)
    def _():
        for pair in copies:
            for copy in pair:
                copy.start()

    query = total_ref[:, :columns] if has_total else 0.0
    keyval = total_ref[:, columns:] if has_total else 0.0
    k = 0
    for ref, count in zip(pieces, counts):
        for j in range(count):

            @pl.when(pl.program_id(0) == 0)
            def _(k=k):
                for copy in copies[k]:
                    copy.wait()

            left = ref[j]
            query += jnp.dot(left, weights_ref[k, :, :columns], preferred_element_type=F32)
            keyval += jnp.dot(left, weights_ref[k, :, columns:], preferred_element_type=F32)
            k += 1
    if not last:
        refs[0][:, :columns] = query
        refs[0][:, columns:] = keyval
        return
    query_out, keyval_out = refs
    q_cos, q_sin, kv_cos, kv_sin = [t[...] for t in tables]
    for head in range(columns // HD):
        span = slice(head * HD, (head + 1) * HD)
        part = query[:, span]
        query_out[:, span] = (part * q_cos + swap_members(part) * q_sin).astype(BF)
    turned = (keyval * kv_cos + swap_members(keyval) * kv_sin).astype(BF)
    to = lax.broadcasted_iota(jnp.int32, (HD, HD), 0)
    came = lax.broadcasted_iota(jnp.int32, (HD, HD), 1)
    order = jnp.where(came == to % 16 // 2 * 16 + to // 16 * 2 + to % 2, 1.0, 0.0).astype(BF)
    turned = lax.dot_general(
        order, turned, (((1,), (1,)), ((), ())), preferred_element_type=F32
    ).astype(BF)
    for member in range(2 * KVH):
        keyval_out[member] = turned[member // 2 * 16 : member // 2 * 16 + 16]


def project(pieces, index, w_query, w_keyval, rows, total=None, tables=None, block=0):
    counts = tuple(p.shape[0] for p in pieces)
    n = sum(counts)
    width = pieces[0].shape[2]
    columns = w_query.shape[1]
    last = tables is not None

    def skip(array, axis):
        return block * (BLOCK // TILE) if array.shape[axis] > rows else 0

    in_specs = [
        pl.BlockSpec((p.shape[0], TILE, width), lambda i, _, at=skip(p, 1): (0, i + at, 0))
        for p in pieces
    ]
    in_specs += [pl.BlockSpec(memory_space=pltpu.HBM)] * 2
    operands = list(pieces) + [in_hbm(w_query), in_hbm(w_keyval)]
    if total is not None:
        at = skip(total, 0)
        in_specs.append(pl.BlockSpec((TILE, columns + HD), lambda i, _: (i + at, 0)))
        operands.append(in_hbm(total))
    if last:
        first = skip(tables[0], 0)
        in_specs += [pl.BlockSpec((TILE, HD), lambda i, _: (i + first, 0))] * 4
        operands += [in_hbm(t) for t in tables]
        out_shape = (
            jax.ShapeDtypeStruct((rows, columns), BF),
            jax.ShapeDtypeStruct((2 * KVH, 16, rows), BF),
        )
        out_specs = [
            pl.BlockSpec((TILE, columns), lambda i, _: (i, 0)),
            pl.BlockSpec((2 * KVH, 16, TILE), lambda i, _: (0, 0, i)),
        ]
    else:
        out_shape = jax.ShapeDtypeStruct((rows, columns + HD), F32)
        out_specs = pl.BlockSpec((TILE, columns + HD), lambda i, _: (i, 0))
    return pl.pallas_call(
        functools.partial(project_kernel, counts, total is not None, last),
        out_shape=out_shape,
        grid_spec=pltpu.PrefetchScalarGridSpec(
            num_scalar_prefetch=1,
            grid=(rows // TILE,),
            in_specs=in_specs,
            out_specs=out_specs,
            scratch_shapes=[
                pltpu.VMEM((n, width, columns + HD), BF),
                pltpu.SemaphoreType.DMA((n, 2)),
            ],
        ),
        compiler_params=params(),
        name="project",
    )(index, *operands)


def attend_kernel(block, plan_ref, query_ref, *refs):
    keyval_refs, heads_ref = refs[:-1], refs[-1]
    scale = 1.0 / math.sqrt(HD)
    local_heads = query_ref.shape[1] // HD

    def columns_of(there, member):
        part, first = there * TILE // BLOCK, there * TILE % BLOCK
        return keyval_refs[part][member * HD : (member + 1) * HD, first : first + TILE]

    for tile in range(BLOCK // TILE):
        here = block * (BLOCK // TILE) + tile
        rows = here * TILE + lax.broadcasted_iota(jnp.int32, (TILE, 1), 0)
        begin = jnp.zeros((TILE, 1), jnp.int32)
        for s in range(8):
            begin = jnp.where(rows >= plan_ref[0, s], plan_ref[0, s], begin)
        filled = rows < plan_ref[1, 7]
        seen = []
        for there in range(max(here - 1, 0), here + 1):
            columns = there * TILE + lax.broadcasted_iota(jnp.int32, (TILE, TILE), 1)
            allowed = (columns >= begin) & (columns <= rows)
            seen.append((allowed, columns_of(there, 0), columns_of(there, 1)))
        for head in range(local_heads):
            span = slice(head * HD, (head + 1) * HD)
            query = query_ref[tile * TILE : (tile + 1) * TILE, span]
            scores = []
            for allowed, key, _ in seen:
                raw = jnp.dot(query, key, preferred_element_type=F32)
                scores.append(jnp.where(allowed, raw * scale, -1e30))
            top = functools.reduce(
                jnp.maximum, [jnp.max(s, axis=1, keepdims=True) for s in scores]
            )
            shifted = [jnp.exp(s - top) for s in scores]
            norm = sum(jnp.sum(s, axis=1, keepdims=True) for s in shifted)
            result = jnp.zeros((TILE, HD), F32)
            for part, (_, _, value) in zip(shifted, seen):
                weights = (part / norm).astype(BF)
                result += lax.dot_general(
                    weights, value, (((1,), (1,)), ((), ())), preferred_element_type=F32
                )
            heads_ref[tile * TILE : (tile + 1) * TILE, span] = jnp.where(
                filled, result, 0.0
            ).astype(BF)


def attend(block, plan, query, keyvals):
    return pl.pallas_call(
        functools.partial(attend_kernel, block),
        out_shape=jax.ShapeDtypeStruct(query.shape, BF),
        in_specs=[
            pl.BlockSpec(memory_space=pltpu.SMEM),
            pl.BlockSpec(memory_space=pltpu.VMEM),
        ]
        + [pl.BlockSpec(memory_space=pltpu.VMEM)] * len(keyvals),
        out_specs=pl.BlockSpec(memory_space=pltpu.VMEM),
        compiler_params=params(),
        name="attend",
    )(plan, query, *keyvals)


def chunks_kernel(groups, adds, index_ref, heads_ref, w_out, *refs):
    n = len(adds)
    refs = list(refs)
    weights_ref, sems = refs[-2:]
    outs = refs[-2 - len(groups) : -2]
    width = weights_ref.shape[2]
    copies = []
    for k in range(n):
        columns = pl.ds(pl.multiple_of(index_ref[k] * width, width), width)
        copies.append(
            pltpu.make_async_copy(w_out.at[:, columns], weights_ref.at[k], sems.at[k])
        )

    @pl.when(pl.program_id(0) == 0)
    def _():
        for copy in copies:
            copy.start()

    k = 0
    for out, size in zip(outs, groups):
        for j in range(size):

            @pl.when(pl.program_id(0) == 0)
            def _(k=k):
                copies[k].wait()

            total = jnp.dot(heads_ref[...], weights_ref[k], preferred_element_type=F32)
            for _ in range(adds[k]):
                total += refs.pop(0)[0].astype(F32)
            out[j] = total.astype(BF)
            k += 1


def chunks(heads, w_out, index, groups, adds):
    rows, depth = heads.shape
    width = 512
    n = len(adds)
    in_specs = [
        pl.BlockSpec((TILE, depth), lambda i, p: (i, 0)),
        pl.BlockSpec(memory_space=pltpu.HBM),
    ]
    operands = [heads, in_hbm(w_out)]
    for terms in adds:
        for array, place in terms:
            in_specs.append(
                pl.BlockSpec((1, TILE, width), lambda i, p, at=place: (at, i, 0))
            )
            operands.append(array)
    return pl.pallas_call(
        functools.partial(chunks_kernel, groups, tuple(len(a) for a in adds)),
        out_shape=[jax.ShapeDtypeStruct((g, rows, width), BF) for g in groups],
        grid_spec=pltpu.PrefetchScalarGridSpec(
            num_scalar_prefetch=1,
            grid=(rows // TILE,),
            in_specs=in_specs,
            out_specs=[pl.BlockSpec((g, TILE, width), lambda i, p: (0, i, 0)) for g in groups],
            scratch_shapes=[
                pltpu.VMEM((n, depth, width), BF),
                pltpu.SemaphoreType.DMA((n,)),
            ],
        ),
        compiler_params=params(),
        name="chunks",
    )(index, *operands)


def gather_order(x, y, c):
    way = 1 - 2 * c
    places = [(x, y, c), (x, y, 1 - c), (x, y - way, c), (x, y - way, 1 - c)]
    places += [(x, y + way, 1 - c), (x, y + way, c)]
    places += [(1 - x, y, c), (1 - x, y, 1 - c), (x, y + 2, c), (x, y + 2, 1 - c)]
    places += [(1 - x, y - way, c), (1 - x, y - way, 1 - c)]
    places += [(1 - x, y + way, 1 - c), (1 - x, y + way, c)]
    places += [(1 - x, y + 2, c), (1 - x, y + 2, 1 - c)]
    return jnp.stack(
        [side * 8 + (row + 4) % 4 * 2 + core for side, row, core in places]
    ).astype(jnp.int32)


def rotary_tables(position, member):
    lanes = jnp.arange(HD, dtype=jnp.int32)
    sign = jnp.where(lanes % 2 == 0, -1.0, 1.0).astype(F32)

    def table(pairs):
        frequency = jnp.exp(pairs.astype(F32) * (-2.0 * math.log(rope_base) / HD))
        angles = position.astype(F32)[:, None] * frequency[None, :]
        return jnp.cos(angles), jnp.sin(angles) * sign[None, :]

    q_cos, q_sin = table(lanes // 2)
    columns = member * HD + lanes
    kv_cos, kv_sin = table(columns // (2 * KVH) % (HD // 2))
    keys = member < KVH
    return q_cos, q_sin, jnp.where(keys, kv_cos, 1.0), jnp.where(keys, kv_sin, 0.0)


def body(rollout, lengths, target, w_query, w_keyval, w_out):
    member = lax.axis_index("tp")
    x, y, c = member // 8, member // 2 % 4, member % 2
    section_ids = jnp.arange(8, dtype=jnp.int32)
    own_lengths = lengths[0]
    chosen = target[0][None, :] == section_ids[:, None]
    before = jnp.cumsum(own_lengths) - own_lengths
    start_to = jnp.sum(jnp.where(chosen, before[None, :], 0), axis=1)
    sent_from = jnp.minimum(start_to // ALIGN * ALIGN, rollout.shape[0] - SENT)
    count_to = jnp.sum(jnp.where(chosen, own_lengths[None, :], 0), axis=1)
    facts = jnp.stack([count_to, start_to - sent_from], axis=1)
    outgoing = cut(rollout, sent_from)
    arrived = lax.all_to_all(outgoing, "sec", split_axis=0, concat_axis=0, tiled=True)
    facts = lax.all_to_all(facts, "sec", split_axis=0, concat_axis=0, tiled=True)
    counts, shifts = facts[:, 0], facts[:, 1]
    ends = jnp.cumsum(counts)
    offsets = ends - counts
    plan = jnp.stack([offsets, ends, shifts - offsets])
    row_ids = jnp.arange(CAP, dtype=jnp.int32)
    begin = jnp.max(
        jnp.where(row_ids[:, None] >= offsets[None, :], offsets[None, :], 0), axis=1
    )
    order = gather_order(x, y, c)
    weights = w_query[0], w_keyval[0]
    w_out = w_out[0]
    line = Line()
    way = 1 - 2 * c
    sides = (1 - x, x)

    def at(*places):
        return jnp.stack(
            [side * 8 + (row + 4) % 4 * 2 + core for side, row, core in places]
        ).astype(jnp.int32)

    def move(value, pairs):
        return send(line.next(value), pairs)

    def stack(*arrays):
        return line.add(jnp.stack([line.next(arrays[0]), *arrays[1:]]))

    def part(value, *index):
        return line.add(line.next(value)[index])

    def projected(pieces, index, *more):
        return line.add(project(pieces, line.next(index), *weights, *more))

    def spread(keyval):
        keyval = lax.all_to_all(
            line.next(keyval), "tp", split_axis=0, concat_axis=0, tiled=True
        )
        return keyval.reshape(2 * HD, BLOCK)

    def attended(block, query, keyvals):
        return line.add(attend(block, line.next(plan), query, keyvals))

    def join(*arrays):
        *arrays, line.last = lax.optimization_barrier((*arrays, line.last))
        return arrays

    def summed(heads, places, groups, adds):
        index = line.next(at(*places))
        return line.add(chunks(heads, w_out, index, groups, adds))

    def for_core(heads, places):
        parts = summed(heads, places, (1,) * len(places), [[]] * len(places))
        return [send(p, TO_CORE) for p in parts]

    def far_for_core(heads):
        return for_core(heads, [(side, y + 2, 1 - c) for side in sides])

    def near_for_core(heads):
        places = []
        for side in sides:
            places += [(side, y - way, 1 - c), (side, y - way, c)]
        return for_core(heads, places)

    def far_sums(heads, passed):
        places = [(side, y + 2, c) for side in sides]
        adds = [[(p, 0)] for p in passed]
        return send(summed(heads, places, (2,), adds)[0], TO_Y)

    def near_sums(heads, passed, far, groups):
        places, adds = [], []
        for i, side in enumerate(sides):
            places += [(side, y + way, c), (side, y + way, 1 - c)]
            adds += [[(passed[2 * i], 0), (far, i)], [(passed[2 * i + 1], 0)]]
        return summed(heads, places, groups, adds)

    def last_sum(i, heads, near, place, *more):
        shared = summed(heads, [(sides[i], y, 1 - c)], (1,), [[(near, place + 1)]])[0]
        terms = [(near, place), (send(shared, TO_CORE), 0)] + [(t, 0) for t in more]
        return summed(heads, [(sides[i], y, c)], (1,), [terms])[0]


    value = line.add(pack(arrived, plan))
    across = send(value, TO_X)
    up = send(value, TO_Y)
    other = send(value, TO_CORE)
    up_other = send(other, TO_Y)
    position = line.next(row_ids) - begin
    tables = line.add(rotary_tables(position, member))
    total = projected([value[None], other[None]], order[:2], CAP)
    across, up, up_other = join(across, up, up_other)
    far = send(up, TO_Y)
    there_up1 = send(jnp.stack([up[BLOCK:], up_other[BLOCK:]]), TO_X)
    across_other = send(across, TO_CORE)
    there_up0 = send(jnp.stack([across[:BLOCK], across_other[:BLOCK]]), TO_Y)
    down, down_other = send(up, TO_CORE), send(up_other, TO_CORE)
    pieces = [up, up_other, down, down_other, across, across_other]
    total = projected([p[None] for p in pieces], order[2:8], CAP, total)
    far, *there_up = join(far, there_up0, there_up1)
    there_far = [send(there_up[0][:1], TO_Y), send(far[None, BLOCK:], TO_X)]
    there_down = [send(u, TO_CORE) for u in there_up]
    far_other = send(far, TO_CORE)
    pieces = [far[None], far_other[None], there_up[0], there_down[0]]
    total0 = projected(pieces, order[8:14], BLOCK, total, None, 0)
    there_far0, far = join(there_far[0], far)
    pieces = [there_far0, send(there_far0, TO_CORE)]
    query0, keyval0 = projected(pieces, order[14:], BLOCK, total0, tables, 0)
    keyval0 = spread(keyval0)
    pieces = [far[None], far_other[None], there_up[1], there_down[1]]
    there_far_other1 = send(there_far[1], TO_CORE)
    index = after(order[8:14], there_far_other1)
    total1 = projected(pieces, index, BLOCK, total, None, 1)
    heads0 = attended(0, query0, [keyval0])
    far0 = far_sums(heads0, far_for_core(heads0))
    passed = near_for_core(heads0)
    pieces = [there_far[1], there_far_other1]
    query1, keyval1 = projected(pieces, order[14:], BLOCK, total1, tables, 1)
    keyval1 = spread(keyval1)
    near0 = near_sums(heads0, passed, far0, (4,))[0]
    near0 = send(after(near0, keyval1), TO_Y)
    heads1 = attended(1, query1, [keyval0, keyval1])
    far1 = far_sums(heads1, far_for_core(heads1))
    passed = near_for_core(heads1)
    crossed0 = send(last_sum(0, after(heads0, *passed), near0, 0), TO_X)
    near1 = [send(t, TO_Y) for t in near_sums(heads1, passed, far1, (2, 2))]
    result0 = last_sum(1, heads0, near0, 2, crossed0)
    crossed1 = send(last_sum(0, heads1, near1[0], 0), TO_X)
    result1 = last_sum(1, heads1, near1[1], 0, crossed1)
    return jnp.concatenate([result0[0], result1[0]], axis=0)


def solution(mesh):
    placed = (
        P("sec", "tp"),
        P("sec", None),
        P("sec", None),
        P("sec", None, "tp"),
        P("sec", None, "tp"),
        P("sec", "tp", None),
    )
    return jax.shard_map(
        body, mesh=mesh, in_specs=placed, out_specs=P("sec", "tp"), check_vma=False
    )
```

time: 409 us -> 288 us (0.70)
  starting transfers between devices: 111 us -> 62.8 us
  Pallas kernels: 135 us -> 99.7 us
  blocking collectives: 20.1 us -> 0 us
  waiting for transfers between devices: 109 us -> 95.3 us
    ppermute x51 -> x40, starting transfers between devices: 89.9 us -> 42.8 us  [send(): return lax.ppermute(value, 'tp', pairs)]
    pallas_call x21 -> x17, Pallas kernels: 93 us -> 46.7 us  [the longest x16 44.6 us: chunks(): pl.pallas_call(functools.partial(chunks_kernel, groups, tuple((len(a) for...]
    ppermute x51 -> x40, waiting for transfers between devices: 103 us -> 66 us  [send(): return lax.ppermute(value, 'tp', pairs)]
    all_to_all x3, waiting for transfers between devices: 5.25 us -> 28.1 us  [the longest x1 26.4 us: body(): lax.all_to_all(outgoing, 'sec', split_axis=0, concat_axis=0, tiled=True)]
    all_to_all x1 -> x0, blocking collectives: 20.1 us -> none  [body(): lax.all_to_all(o, 'sec', split_axis=0, concat_axis=0, tiled=True)]
    pallas_call x3 -> x6, Pallas kernels: 30.2 us -> 43.9 us  [project(): pl.pallas_call(functools.partial(project_kernel, counts, total is not Non...]
    slice x6 -> x1, local copies, waits for them, and re-layouts: 6.16 us -> 1.92 us  [body(): there_far = [send(there_up[0][:1], TO_Y), send(far[None, BLOCK:], TO_X)]]
    unnamed x44 -> x30, local copies, waits for them, and re-layouts: 9.31 us -> 12.1 us
  transfers between devices with their start and end apart: 55 -> 44, of which waited for: 20 -> 20; matrix products, arithmetic and copies ran while one was open for 4% -> 4% of each run, Pallas kernels for 33% -> 28%
where the time goes in v2:
time: 288 us; the launch traced here: 287 us
  Pallas kernels  99.7 us (35%)
  waiting for transfers between devices  95.3 us (33%)
  starting transfers between devices  62.8 us (22%)
  local copies, waits for them, and re-layouts  17 us (6%)
  other arithmetic  11.7 us (4%)
    ppermute x40, waiting for transfers between devices, send(): return lax.ppermute(value, 'tp', pairs)  66 us
    pallas_call x16, Pallas kernels, chunks(): pl.pallas_call(functools.partial(chunks_kernel, groups, tuple((len(a) for...  44.6 us
    pallas_call x6, Pallas kernels, project(): pl.pallas_call(functools.partial(project_kernel, counts, total is not Non...  43.9 us
    ppermute x40, starting transfers between devices, send(): return lax.ppermute(value, 'tp', pairs)  42.8 us
    all_to_all x1, waiting for transfers between devices, body(): lax.all_to_all(outgoing, 'sec', split_axis=0, concat_axis=0, tiled=True)  26.4 us
    unnamed x30, local copies, waits for them, and re-layouts  12.1 us
    all_to_all x2, starting transfers between devices, spread(): lax.all_to_all(line.next(keyval), 'tp', split_axis=0, concat_axis=0, tile...  9.28 us
    all_to_all x1, starting transfers between devices, body(): lax.all_to_all(facts, 'sec', split_axis=0, concat_axis=0, tiled=True)  6.79 us
  transfers between devices with their start and end apart: 44, of which 20 were waited for; matrix products, arithmetic and copies ran while one was open for 4% of the time, Pallas kernels for 28%

profile of v2, /device:TPU:1, one launch (start us, length us, event | category | flops | bytes accessed | tf_op | source)
XLA Modules:
  0.0 286.9 jit_solution(819205209719147672)
XLA Ops:
  3.0 6.8 %all-to-all-start = ((s32[8,1,2]{2,1,0:T(1,128)}), s32[8,1,2]{2,1,0:T(1,128)S(1)}, u32[]{:S(2)}, u32[]{:S(2)}) async-start(s32[8,1,2]{2,1,0:T(1,128)} %copy.9), calls=%async_computation | async-start | bytes 8192 | tf_op jit(solution)/shard_map/all_to_all | solution.py:415
  11.4 2.1 cut.1
  14.7 3.9 %all-to-all-start.1 = ((bf16[8,272,512]{2,1,0:T(8,128)(2,1)}), bf16[8,272,512]{2,1,0:T(8,128)(2,1)S(1)}, u32[]{:S(2)}, u32[]{:S(2)}) async-start(bf16[8,272,512]{2,1,0:T(8,128)(2,1)} %cut.1), calls=%async_computation.1 | async-start | bytes 4456448 | tf_op jit(solution)/shard_map/all_to_all | solution.py:414
  18.9 26.4 %all-to-all-done.1.arrived_ref = bf16[8,272,512]{2,1,0:T(8,128)(2,1)S(1)} async-done(((bf16[8,272,512]{2,1,0:T(8,128)(2,1)}), bf16[8,272,512]{2,1,0:T(8,128)(2,1)S(1)}, u32[]{:S(2)}, u32[]{:S(2)}) %all-to-all-start.1) | async-done | bytes 2228256 | tf_op jit(solution)/shard_map/all_to_all | solution.py:414
  45.3 3.5 %pack.1 = bf16[1024,512]{1,0:T(8,128)(2,1)S(1)} custom-call(s32[3,8]{1,0:T(4,128)S(1)} %pad_add_fusion.plan_ref, bf16[8,272,512]{2,1,0:T(8,128)(2,1)S(1)} %all-to-all-done.1.arrived_ref), custom_call_target="tpu_custom_call" | custom-call | tf_op jit(solution)/shard_map/pack/pallas_call | solution.py:109
  48.8 2.8 collective-permute-start.2
  51.6 2.5 collective-permute-start
  54.1 2.7 collective-permute-start.1
  57.5 5.4 %fusion.3 = (f32[1024,128]{1,0:T(8,128)}, f32[1024,128]{1,0:T(8,128)}, f32[1024,128]{1,0:T(8,128)}, f32[1024,128]{1,0:T(8,128)}) fusion(f32[128]{0:T(128)S(1)} %fusion.9, f32[128]{0:T(128)S(1)} %get-tuple-element.119, f32[1024]{0:T(1024)S(1)} %subtract_convert_fusion, pred[]{:T(512)S(6)} %lt.136, f32[128]{0:T(128)S(1)} %get-tuple-element.120), kind=kLoop, calls=%fused_computation.10 | loop fusion | flops 786432 | bytes 2102785 | tf_op jit(solution)/shard_map/jit(_where)/select_n | solution.py:399
  63.0 4.4 %project.6.refs_8_ = f32[1024,640]{1,0:T(8,128)S(1)} custom-call(s32[2]{0:T(128)S(1)} %pad_add_fusion.6.index_ref, bf16[1,1024,512]{2,1,0:T(8,128)(2,1)S(1)} %bitcast.75, bf16[1,1024,512]{2,1,0:T(8,128)(2,1)S(1)} %bitcast.85, bf16[8192,512]{1,0:T(8,128)(2,1)} %bitcast.103, bf16[8192,128]{1,0:T(8,128)(2,1)} %bitcast.109), custom_call_target="tpu_custom_call" | custom-call | tf_op jit(solution)/shard_map/project/pallas_call | solution.py:230
  67.4 10.5 %collective-permute-done = bf16[1024,512]{1,0:T(8,128)(2,1)S(1)} collective-permute-done((bf16[1024,512]{1,0:T(8,128)(2,1)S(1)}, bf16[1024,512]{1,0:T(8,128)(2,1)S(1)}, u32[]{:S(2)}, u32[]{:S(2)}) %collective-permute-start) | collective-permute-done | bytes 1048608 | tf_op jit(solution)/shard_map/ppermute | solution.py:59
  77.9 1.9 collective-permute-done.3
  79.9 2.0 collective-permute-start.5
  81.8 1.8 collective-permute-start.4
  91.5 12.4 %project.7.refs_6_ = f32[1024,640]{1,0:T(8,128)S(1)} custom-call(s32[6]{0:T(128)S(1)} %stack.168.index_ref, bf16[1,1024,512]{2,1,0:T(8,128)(2,1)S(1)} %bitcast.78, bf16[1,1024,512]{2,1,0:T(8,128)(2,1)} %bitcast.36.refs_1_, bf16[1,1024,512]{2,1,0:T(8,128)(2,1)} %bitcast.37.refs_2_, bf16[1,1024,512]{2,1,0:T(8,128)(2,1)} %bitcast.38.refs_3_, ...), custom_call_target="tpu_custom_call" | custom-call | tf_op jit(solution)/shard_map/project/pallas_call | solution.py:230
  105.3 6.5 %collective-permute-done.7.refs_2_ = bf16[2,512,512]{2,1,0:T(8,128)(2,1)} collective-permute-done((bf16[2,512,512]{2,1,0:T(8,128)(2,1)}, bf16[2,512,512]{2,1,0:T(8,128)(2,1)}, u32[]{:S(2)}, u32[]{:S(2)}) %collective-permute-start.7) | collective-permute-done | bytes 1048608 | tf_op jit(solution)/shard_map/ppermute | solution.py:59
  113.3 1.9 slice.41
  115.2 1.7 collective-permute-start.12
  118.3 7.9 %project.8.refs_4_ = f32[512,640]{1,0:T(8,128)S(1)} custom-call(s32[6]{0:T(128)S(1)} %stack.160.index_ref, bf16[1,1024,512]{2,1,0:T(8,128)(2,1)S(1)} %bitcast.73, bf16[1,1024,512]{2,1,0:T(8,128)(2,1)S(1)} %bitcast.76, bf16[2,512,512]{2,1,0:T(8,128)(2,1)} %collective-permute-done.6.refs_2_, bf16[2,512,512]{2,1,0:T(8,128)(2,1)} %collective-permute-done.14.refs_3_, ...), custom_call_target="tpu_custom_call" | custom-call | tf_op jit(solution)/shard_map/project/pallas_call | solution.py:230
  127.8 5.4 %collective-permute-done.10.refs_0_ = bf16[1,512,512]{2,1,0:T(8,128)(2,1)} collective-permute-done((bf16[1,512,512]{2,1,0:T(8,128)(2,1)}, bf16[1,512,512]{2,1,0:T(8,128)(2,1)}, u32[]{:S(2)}, u32[]{:S(2)}) %collective-permute-start.10) | collective-permute-done | bytes 524320 | tf_op jit(solution)/shard_map/ppermute | solution.py:59
  133.7 5.4 %project.9 = (bf16[512,512]{1,0:T(8,128)(2,1)S(1)}, bf16[16,16,512]{2,1,0:T(8,128)(2,1)S(1)}) custom-call(s32[2]{0:T(128)S(1)} %pad_add_fusion.5.index_ref, bf16[1,512,512]{2,1,0:T(8,128)(2,1)} %collective-permute-done.12.refs_0_, bf16[1,512,512]{2,1,0:T(8,128)(2,1)} %collective-permute-done.15.refs_1_, bf16[8192,512]{1,0:T(8,128)(2,1)} %bitcast.106, ...), custom_call_target="tpu_custom_call" | custom-call | tf_op jit(solution)/shard_map/project/pallas_call | solution.py:230
  140.7 3.4 %all-to-all-start.2 = ((bf16[16,16,512]{2,1,0:T(8,128)(2,1)}), bf16[16,16,512]{2,1,0:T(8,128)(2,1)S(1)}, u32[]{:S(2)}, u32[]{:S(2)}) async-start(bf16[16,16,512]{2,1,0:T(8,128)(2,1)} %copy-done.14), calls=%async_computation.2 | async-start | bytes 524288 | tf_op jit(solution)/shard_map/all_to_all | solution.py:449
  144.2 7.7 %project.10.refs_4_ = f32[512,640]{1,0:T(8,128)S(1)} custom-call(s32[6]{0:T(128)S(1)} %stack.160.index_ref, bf16[1,1024,512]{2,1,0:T(8,128)(2,1)S(1)} %bitcast.74, bf16[1,1024,512]{2,1,0:T(8,128)(2,1)S(1)} %bitcast.77, bf16[2,512,512]{2,1,0:T(8,128)(2,1)} %collective-permute-done.7.refs_2_, bf16[2,512,512]{2,1,0:T(8,128)(2,1)S(1)} %collective-permute-done.16.refs_3_, ...), custom_call_target="tpu_custom_call" | custom-call | tf_op jit(solution)/shard_map/project/pallas_call | solution.py:230
  154.0 2.6 attend.2.heads_ref
  156.6 2.8 chunks.16
  162.7 3.7 %chunks.17 = bf16[2,512,512]{2,1,0:T(8,128)(2,1)} custom-call(s32[2]{0:T(128)S(1)} %pad_add_fusion.3.index_ref, bf16[512,512]{1,0:T(8,128)(2,1)S(1)} %attend.2.heads_ref, bf16[512,8192]{1,0:T(8,128)(2,1)} %bitcast.88, bf16[1,512,512]{2,1,0:T(8,128)(2,1)S(1)} %collective-permute-done.17.refs_0_, bf16[1,512,512]{2,1,0:T(8,128)(2,1)S(1)} %collective-permute-done.18.refs_1_), custom_call_target="tpu_custom_call" | custom-call | tf_op jit(solution)/shard_map/chunks/pallas_call | solution.py:355
  166.4 2.2 collective-permute-start.20
  168.7 4.8 %chunks.18 = (bf16[1,512,512]{2,1,0:T(8,128)(2,1)}, bf16[1,512,512]{2,1,0:T(8,128)(2,1)}, bf16[1,512,512]{2,1,0:T(8,128)(2,1)}, bf16[1,512,512]{2,1,0:T(8,128)(2,1)}) custom-call(s32[4]{0:T(128)S(1)} %pad_add_fusion.2.index_ref, bf16[512,512]{1,0:T(8,128)(2,1)S(1)} %attend.2.heads_ref, bf16[512,8192]{1,0:T(8,128)(2,1)} %bitcast.89), custom_call_target="tpu_custom_call" | custom-call | tf_op jit(solution)/shard_map/chunks/pallas_call | solution.py:355
  174.6 6.1 %project.11 = (bf16[512,512]{1,0:T(8,128)(2,1)S(1)}, bf16[16,16,512]{2,1,0:T(8,128)(2,1)}) custom-call(s32[2]{0:T(128)S(1)} %pad_add_fusion.5.index_ref, bf16[1,512,512]{2,1,0:T(8,128)(2,1)} %collective-permute-done.10.refs_0_, bf16[1,512,512]{2,1,0:T(8,128)(2,1)} %collective-permute-done.11.refs_1_, bf16[8192,512]{1,0:T(8,128)(2,1)} %bitcast.108, ...), custom_call_target="tpu_custom_call" | custom-call | tf_op jit(solution)/shard_map/project/pallas_call | solution.py:230
  181.5 5.8 %all-to-all-start.3 = ((bf16[16,16,512]{2,1,0:T(8,128)(2,1)}), bf16[16,16,512]{2,1,0:T(8,128)(2,1)S(1)}, u32[]{:S(2)}, u32[]{:S(2)}) async-start(bf16[16,16,512]{2,1,0:T(8,128)(2,1)} %get-tuple-element.88), calls=%async_computation.3 | async-start | bytes 524288 | tf_op jit(solution)/shard_map/all_to_all | solution.py:449
  187.5 5.5 %chunks.19 = bf16[4,512,512]{2,1,0:T(8,128)(2,1)S(1)} custom-call(s32[4]{0:T(128)S(1)} %pad_add_fusion.1.index_ref, bf16[512,512]{1,0:T(8,128)(2,1)S(1)} %attend.2.heads_ref, bf16[512,8192]{1,0:T(8,128)(2,1)} %bitcast.90, bf16[1,512,512]{2,1,0:T(8,128)(2,1)S(1)} %collective-permute-done.19.refs_0_, ...), custom_call_target="tpu_custom_call" | custom-call | tf_op jit(solution)/shard_map/chunks/pallas_call | solution.py:355
  194.3 1.7 all-to-all-done.3
  197.5 3.0 %attend.3.heads_ref = bf16[512,512]{1,0:T(8,128)(2,1)S(1)} custom-call(s32[3,8]{1,0:T(4,128)S(1)} %pad_add_fusion.plan_ref, bf16[512,512]{1,0:T(8,128)(2,1)S(1)} %copy-done.13, bf16[256,512]{1,0:T(8,128)(2,1)S(1)} %bitcast.82, bf16[256,512]{1,0:T(8,128)(2,1)S(1)} %bitcast.86), custom_call_target="tpu_custom_call" | custom-call | tf_op jit(solution)/shard_map/attend/pallas_call | solution.py:293
  200.6 2.8 chunks.20
  206.2 2.9 %chunks.21 = bf16[2,512,512]{2,1,0:T(8,128)(2,1)S(1)} custom-call(s32[2]{0:T(128)S(1)} %pad_add_fusion.3.index_ref, bf16[512,512]{1,0:T(8,128)(2,1)S(1)} %attend.3.heads_ref, bf16[512,8192]{1,0:T(8,128)(2,1)} %bitcast.92, bf16[1,512,512]{2,1,0:T(8,128)(2,1)S(1)} %collective-permute-done.24.refs_0_, bf16[1,512,512]{2,1,0:T(8,128)(2,1)S(1)} %collective-permute-done.25.refs_1_), custom_call_target="tpu_custom_call" | custom-call | tf_op jit(solution)/shard_map/chunks/pallas_call | solution.py:355
  209.1 4.1 %chunks.22 = (bf16[1,512,512]{2,1,0:T(8,128)(2,1)S(1)}, bf16[1,512,512]{2,1,0:T(8,128)(2,1)S(1)}, bf16[1,512,512]{2,1,0:T(8,128)(2,1)S(1)}, bf16[1,512,512]{2,1,0:T(8,128)(2,1)S(1)}) custom-call(s32[4]{0:T(128)S(1)} %pad_add_fusion.2.index_ref, bf16[512,512]{1,0:T(8,128)(2,1)S(1)} %attend.3.heads_ref, bf16[512,8192]{1,0:T(8,128)(2,1)} %bitcast.93), custom_call_target="tpu_custom_call" | custom-call | tf_op jit(solution)/shard_map/chunks/pallas_call | solution.py:355
  215.2 2.1 collective-permute-start.32
  217.4 4.0 %collective-permute-done.30.refs_0_ = bf16[4,512,512]{2,1,0:T(8,128)(2,1)S(1)} collective-permute-done((bf16[4,512,512]{2,1,0:T(8,128)(2,1)}, bf16[4,512,512]{2,1,0:T(8,128)(2,1)S(1)}, u32[]{:S(2)}, u32[]{:S(2)}) %collective-permute-start.30) | collective-permute-done | bytes 2097184 | tf_op jit(solution)/shard_map/ppermute | solution.py:59
  223.1 3.1 %collective-permute-start.31 = (bf16[1,512,512]{2,1,0:T(8,128)(2,1)S(1)}, bf16[1,512,512]{2,1,0:T(8,128)(2,1)S(1)}, u32[]{:S(2)}, u32[]{:S(2)}) collective-permute-start(bf16[1,512,512]{2,1,0:T(8,128)(2,1)S(1)} %chunks.23), channel_id=1, source_target_pairs={{0,1},{1,0},{2,3},{3,2},{4,5},{5,4},{6,7},{7,6},{8,9},{9,8},{10,11... | collective-permute-start | bytes 1572872 | tf_op jit(solution)/shard_map/ppermute | solution.py:59
  229.5 3.2 %collective-permute-done.32.refs_1_.refs_4_ = bf16[2,512,512]{2,1,0:T(8,128)(2,1)S(1)} collective-permute-done((bf16[2,512,512]{2,1,0:T(8,128)(2,1)S(1)}, bf16[2,512,512]{2,1,0:T(8,128)(2,1)S(1)}, u32[]{:S(2)}, u32[]{:S(2)}) %collective-permute-start.32) | collective-permute-done | bytes 1048608 | tf_op jit(solution)/shard_map/ppermute | solution.py:59
  232.7 4.3 %chunks.25 = (bf16[2,512,512]{2,1,0:T(8,128)(2,1)S(1)}, bf16[2,512,512]{2,1,0:T(8,128)(2,1)S(1)}) custom-call(s32[4]{0:T(128)S(1)} %pad_add_fusion.1.index_ref, bf16[512,512]{1,0:T(8,128)(2,1)S(1)} %attend.3.heads_ref, bf16[512,8192]{1,0:T(8,128)(2,1)} %bitcast.96, bf16[1,512,512]{2,1,0:T(8,128)(2,1)S(1)} %collective-permute-done.26.refs_0_, ...), custom_call_target="tpu_custom_call" | custom-call | tf_op jit(solution)/shard_map/chunks/pallas_call | solution.py:355
  237.0 2.5 collective-permute-start.35
  243.4 2.0 collective-permute-start.37
  245.4 11.5 %collective-permute-done.34.refs_2_ = bf16[1,512,512]{2,1,0:T(8,128)(2,1)S(1)} collective-permute-done((bf16[1,512,512]{2,1,0:T(8,128)(2,1)S(1)}, bf16[1,512,512]{2,1,0:T(8,128)(2,1)S(1)}, u32[]{:S(2)}, u32[]{:S(2)}) %collective-permute-start.34) | collective-permute-done | bytes 524320 | tf_op jit(solution)/shard_map/ppermute | solution.py:59
  256.9 1.8 chunks.27
  266.3 2.8 collective-permute-start.38
  270.6 13.4 %collective-permute-done.39.refs_2_ = bf16[1,512,512]{2,1,0:T(8,128)(2,1)S(1)} collective-permute-done((bf16[1,512,512]{2,1,0:T(8,128)(2,1)S(1)}, bf16[1,512,512]{2,1,0:T(8,128)(2,1)S(1)}, u32[]{:S(2)}, u32[]{:S(2)}) %collective-permute-start.39) | collective-permute-done | bytes 524320 | tf_op jit(solution)/shard_map/ppermute | solution.py:59
  284.1 1.8 chunks.31
  (132 shorter events, 56.7 us)
Async XLA Ops:
  3.0 11.7 %all-to-all-start = ((s32[8,1,2]{2,1,0:T(1,128)}), s32[8,1,2]{2,1,0:T(1,128)S(1)}, u32[]{:S(2)}, u32[]{:S(2)}) async-start(s32[8,1,2]{2,1,0:T(1,128)} %copy.9), calls=%async_computation | async-start | bytes 8192 | tf_op jit(solution)/shard_map/all_to_all | solution.py:415
  14.7 30.5 %all-to-all-start.1 = ((bf16[8,272,512]{2,1,0:T(8,128)(2,1)}), bf16[8,272,512]{2,1,0:T(8,128)(2,1)S(1)}, u32[]{:S(2)}, u32[]{:S(2)}) async-start(bf16[8,272,512]{2,1,0:T(8,128)(2,1)} %cut.1), calls=%async_computation.1 | async-start | bytes 4456448 | tf_op jit(solution)/shard_map/all_to_all | solution.py:414
  48.8 8.1 %collective-permute-start.2 = (bf16[1024,512]{1,0:T(8,128)(2,1)S(1)}, bf16[1024,512]{1,0:T(8,128)(2,1)S(1)}, u32[]{:S(2)}, u32[]{:S(2)}) collective-permute-start(bf16[1024,512]{1,0:T(8,128)(2,1)S(1)} %pack.1), channel_id=1, source_target_pairs={{0,1},{1,0},{2,3},{3,2},{4,5},{5,4},{6,7},{7,6},{8,9},{9,8},{10,11... | collective-permute-start | bytes 3145736 | tf_op jit(solution)/shard_map/ppermute | solution.py:59
  51.6 26.3 %collective-permute-start = (bf16[1024,512]{1,0:T(8,128)(2,1)S(1)}, bf16[1024,512]{1,0:T(8,128)(2,1)S(1)}, u32[]{:S(2)}, u32[]{:S(2)}) collective-permute-start(bf16[1024,512]{1,0:T(8,128)(2,1)S(1)} %pack.1), channel_id=1, source_target_pairs={{0,8},{1,9},{2,10},{3,11},{4,12},{5,13},{6,14},{7,15},{8,0},{9,1},... | collective-permute-start | bytes 3145736 | tf_op jit(solution)/shard_map/ppermute | solution.py:59
  54.1 23.8 %collective-permute-start.1 = (bf16[1024,512]{1,0:T(8,128)(2,1)S(1)}, bf16[1024,512]{1,0:T(8,128)(2,1)S(1)}, u32[]{:S(2)}, u32[]{:S(2)}) collective-permute-start(bf16[1024,512]{1,0:T(8,128)(2,1)S(1)} %pack.1), channel_id=1, source_target_pairs={{0,2},{1,7},{2,4},{3,1},{4,6},{5,3},{6,0},{7,5},{8,10},{9,15},{10,... | collective-permute-start | bytes 3145736 | tf_op jit(solution)/shard_map/ppermute | solution.py:59
  56.9 23.0 %collective-permute-start.3 = (bf16[1024,512]{1,0:T(8,128)(2,1)S(1)}, bf16[1024,512]{1,0:T(8,128)(2,1)}, u32[]{:S(2)}, u32[]{:S(2)}) collective-permute-start(bf16[1024,512]{1,0:T(8,128)(2,1)S(1)} %collective-permute-done.2), channel_id=1, source_target_pairs={{0,2},{1,7},{2,4},{3,1},{4,6},{5,3},{6,0},{7,5},{8,10},{9,15},{10,... | collective-permute-start | bytes 3145736 | tf_op jit(solution)/shard_map/ppermute | solution.py:59
  67.4 18.4 %copy-start.1 = (f32[1024,640]{1,0:T(8,128)}, f32[1024,640]{1,0:T(8,128)S(1)}, u32[]{:S(2)}) copy-start(f32[1024,640]{1,0:T(8,128)S(1)} %project.6.refs_8_) | copy-start | bytes 7864324
  77.9 8.4 %copy-start.4 = (bf16[1024,512]{1,0:T(8,128)(2,1)}, bf16[1024,512]{1,0:T(8,128)(2,1)S(1)}, u32[]{:S(2)}) copy-start(bf16[1024,512]{1,0:T(8,128)(2,1)S(1)} %collective-permute-done) | copy-start | bytes 3145732
  79.9 6.5 %collective-permute-start.5 = (bf16[1024,512]{1,0:T(8,128)(2,1)S(1)}, bf16[1024,512]{1,0:T(8,128)(2,1)S(1)}, u32[]{:S(2)}, u32[]{:S(2)}) collective-permute-start(bf16[1024,512]{1,0:T(8,128)(2,1)S(1)} %collective-permute-done), channel_id=1, source_target_pairs={{0,1},{1,0},{2,3},{3,2},{4,5},{5,4},{6,7},{7,6},{8,9},{9,8},{10,11... | collective-permute-start | bytes 3145736 | tf_op jit(solution)/shard_map/ppermute | solution.py:59
  81.8 8.4 %collective-permute-start.8 = (bf16[1024,512]{1,0:T(8,128)(2,1)S(1)}, bf16[1024,512]{1,0:T(8,128)(2,1)}, u32[]{:S(2)}, u32[]{:S(2)}) collective-permute-start(bf16[1024,512]{1,0:T(8,128)(2,1)S(1)} %collective-permute-done.1), channel_id=1, source_target_pairs={{0,1},{1,0},{2,3},{3,2},{4,5},{5,4},{6,7},{7,6},{8,9},{9,8},{10,11... | collective-permute-start | bytes 3145736 | tf_op jit(solution)/shard_map/ppermute | solution.py:59
  81.8 30.0 %collective-permute-start.4 = (bf16[1024,512]{1,0:T(8,128)(2,1)S(1)}, bf16[1024,512]{1,0:T(8,128)(2,1)S(1)}, u32[]{:S(2)}, u32[]{:S(2)}) collective-permute-start(bf16[1024,512]{1,0:T(8,128)(2,1)S(1)} %collective-permute-done.1), channel_id=1, source_target_pairs={{0,2},{1,7},{2,4},{3,1},{4,6},{5,3},{6,0},{7,5},{8,10},{9,15},{10,... | collective-permute-start | bytes 3145736 | tf_op jit(solution)/shard_map/ppermute | solution.py:59
  83.6 6.6 %collective-permute-start.9 = (bf16[1024,512]{1,0:T(8,128)(2,1)}, bf16[1024,512]{1,0:T(8,128)(2,1)}, u32[]{:S(2)}, u32[]{:S(2)}) collective-permute-start(bf16[1024,512]{1,0:T(8,128)(2,1)} %collective-permute-done.3), channel_id=1, source_target_pairs={{0,1},{1,0},{2,3},{3,2},{4,5},{5,4},{6,7},{7,6},{8,9},{9,8},{10,11... | collective-permute-start | bytes 3145736 | tf_op jit(solution)/shard_map/ppermute | solution.py:59
  85.8 26.0 %collective-permute-start.7 = (bf16[2,512,512]{2,1,0:T(8,128)(2,1)}, bf16[2,512,512]{2,1,0:T(8,128)(2,1)}, u32[]{:S(2)}, u32[]{:S(2)}) collective-permute-start(bf16[2,512,512]{2,1,0:T(8,128)(2,1)} %pad_maximum_fusion.1), channel_id=1, source_target_pairs={{0,8},{1,9},{2,10},{3,11},{4,12},{5,13},{6,14},{7,15},{8,0},{9,1},... | collective-permute-start | bytes 3145736 | tf_op jit(solution)/shard_map/ppermute | solution.py:59
  86.4 3.9 %copy-start.5 = (bf16[1024,512]{1,0:T(8,128)(2,1)S(1)}, bf16[1024,512]{1,0:T(8,128)(2,1)}, u32[]{:S(2)}) copy-start(bf16[1024,512]{1,0:T(8,128)(2,1)} %copy-done.4) | copy-start | bytes 3145732
  88.5 23.4 %collective-permute-start.6 = (bf16[2,512,512]{2,1,0:T(8,128)(2,1)}, bf16[2,512,512]{2,1,0:T(8,128)(2,1)}, u32[]{:S(2)}, u32[]{:S(2)}) collective-permute-start(bf16[2,512,512]{2,1,0:T(8,128)(2,1)} %pad_maximum_fusion), channel_id=1, source_target_pairs={{0,2},{1,7},{2,4},{3,1},{4,6},{5,3},{6,0},{7,5},{8,10},{9,15},{10,... | collective-permute-start | bytes 3145736 | tf_op jit(solution)/shard_map/ppermute | solution.py:59
  111.8 6.5 %collective-permute-start.13 = (bf16[1024,512]{1,0:T(8,128)(2,1)S(1)}, bf16[1024,512]{1,0:T(8,128)(2,1)S(1)}, u32[]{:S(2)}, u32[]{:S(2)}) collective-permute-start(bf16[1024,512]{1,0:T(8,128)(2,1)S(1)} %collective-permute-done.4), channel_id=1, source_target_pairs={{0,1},{1,0},{2,3},{3,2},{4,5},{5,4},{6,7},{7,6},{8,9},{9,8},{10,11... | collective-permute-start | bytes 3145736 | tf_op jit(solution)/shard_map/ppermute | solution.py:59
  113.2 5.2 %collective-permute-start.14 = (bf16[2,512,512]{2,1,0:T(8,128)(2,1)}, bf16[2,512,512]{2,1,0:T(8,128)(2,1)}, u32[]{:S(2)}, u32[]{:S(2)}) collective-permute-start(bf16[2,512,512]{2,1,0:T(8,128)(2,1)} %collective-permute-done.6.refs_2_), channel_id=1, source_target_pairs={{0,1},{1,0},{2,3},{3,2},{4,5},{5,4},{6,7},{7,6},{8,9},{9,8},{10,11... | collective-permute-start | bytes 3145736 | tf_op jit(solution)/shard_map/ppermute | solution.py:59
  115.2 12.1 %collective-permute-start.12 = (bf16[1,512,512]{2,1,0:T(8,128)(2,1)}, bf16[1,512,512]{2,1,0:T(8,128)(2,1)}, u32[]{:S(2)}, u32[]{:S(2)}) collective-permute-start(bf16[1,512,512]{2,1,0:T(8,128)(2,1)} %slice.41), channel_id=1, source_target_pairs={{0,2},{1,7},{2,4},{3,1},{4,6},{5,3},{6,0},{7,5},{8,10},{9,15},{10,... | collective-permute-start | bytes 1572872 | tf_op jit(solution)/shard_map/ppermute | solution.py:59
  117.7 15.5 %collective-permute-start.10 = (bf16[1,512,512]{2,1,0:T(8,128)(2,1)}, bf16[1,512,512]{2,1,0:T(8,128)(2,1)}, u32[]{:S(2)}, u32[]{:S(2)}) collective-permute-start(bf16[1,512,512]{2,1,0:T(8,128)(2,1)} %slice_bitcast_fusion.1), channel_id=1, source_target_pairs={{0,8},{1,9},{2,10},{3,11},{4,12},{5,13},{6,14},{7,15},{8,0},{9,1},... | collective-permute-start | bytes 1572872 | tf_op jit(solution)/shard_map/ppermute | solution.py:59
  118.2 25.9 %collective-permute-start.16 = (bf16[2,512,512]{2,1,0:T(8,128)(2,1)}, bf16[2,512,512]{2,1,0:T(8,128)(2,1)S(1)}, u32[]{:S(2)}, u32[]{:S(2)}) collective-permute-start(bf16[2,512,512]{2,1,0:T(8,128)(2,1)} %collective-permute-done.7.refs_2_), channel_id=1, source_target_pairs={{0,1},{1,0},{2,3},{3,2},{4,5},{5,4},{6,7},{7,6},{8,9},{9,8},{10,11... | collective-permute-start | bytes 3145736 | tf_op jit(solution)/shard_map/ppermute | solution.py:59
  127.3 6.4 %collective-permute-start.15 = (bf16[1,512,512]{2,1,0:T(8,128)(2,1)}, bf16[1,512,512]{2,1,0:T(8,128)(2,1)}, u32[]{:S(2)}, u32[]{:S(2)}) collective-permute-start(bf16[1,512,512]{2,1,0:T(8,128)(2,1)} %collective-permute-done.12.refs_0_), channel_id=1, source_target_pairs={{0,1},{1,0},{2,3},{3,2},{4,5},{5,4},{6,7},{7,6},{8,9},{9,8},{10,11... | collective-permute-start | bytes 1572872 | tf_op jit(solution)/shard_map/ppermute | solution.py:59
  133.2 10.9 %collective-permute-start.11 = (bf16[1,512,512]{2,1,0:T(8,128)(2,1)}, bf16[1,512,512]{2,1,0:T(8,128)(2,1)}, u32[]{:S(2)}, u32[]{:S(2)}) collective-permute-start(bf16[1,512,512]{2,1,0:T(8,128)(2,1)} %collective-permute-done.10.refs_0_), channel_id=1, source_target_pairs={{0,1},{1,0},{2,3},{3,2},{4,5},{5,4},{6,7},{7,6},{8,9},{9,8},{10,11... | collective-permute-start | bytes 1572872 | tf_op jit(solution)/shard_map/ppermute | solution.py:59
  140.7 12.3 %all-to-all-start.2 = ((bf16[16,16,512]{2,1,0:T(8,128)(2,1)}), bf16[16,16,512]{2,1,0:T(8,128)(2,1)S(1)}, u32[]{:S(2)}, u32[]{:S(2)}) async-start(bf16[16,16,512]{2,1,0:T(8,128)(2,1)} %copy-done.14), calls=%async_computation.2 | async-start | bytes 524288 | tf_op jit(solution)/shard_map/all_to_all | solution.py:449
  159.5 2.5 collective-permute-start.17
  160.4 2.3 collective-permute-start.18
  166.4 21.1 %collective-permute-start.20 = (bf16[2,512,512]{2,1,0:T(8,128)(2,1)}, bf16[2,512,512]{2,1,0:T(8,128)(2,1)S(1)}, u32[]{:S(2)}, u32[]{:S(2)}) collective-permute-start(bf16[2,512,512]{2,1,0:T(8,128)(2,1)} %chunks.17), channel_id=1, source_target_pairs={{0,2},{1,7},{2,4},{3,1},{4,6},{5,3},{6,0},{7,5},{8,10},{9,15},{10,... | collective-permute-start | bytes 3145736 | tf_op jit(solution)/shard_map/ppermute | solution.py:59
  173.5 13.9 %collective-permute-start.19 = (bf16[1,512,512]{2,1,0:T(8,128)(2,1)}, bf16[1,512,512]{2,1,0:T(8,128)(2,1)S(1)}, u32[]{:S(2)}, u32[]{:S(2)}) collective-permute-start(bf16[1,512,512]{2,1,0:T(8,128)(2,1)} %get-tuple-element.79), channel_id=1, source_target_pairs={{0,1},{1,0},{2,3},{3,2},{4,5},{5,4},{6,7},{7,6},{8,9},{9,8},{10,11... | collective-permute-start | bytes 1572872 | tf_op jit(solution)/shard_map/ppermute | solution.py:59
  173.6 13.9 %collective-permute-start.21 = (bf16[1,512,512]{2,1,0:T(8,128)(2,1)}, bf16[1,512,512]{2,1,0:T(8,128)(2,1)}, u32[]{:S(2)}, u32[]{:S(2)}) collective-permute-start(bf16[1,512,512]{2,1,0:T(8,128)(2,1)} %get-tuple-element.83), channel_id=1, source_target_pairs={{0,1},{1,0},{2,3},{3,2},{4,5},{5,4},{6,7},{7,6},{8,9},{9,8},{10,11... | collective-permute-start | bytes 1572872 | tf_op jit(solution)/shard_map/ppermute | solution.py:59
  174.1 13.4 %collective-permute-start.22 = (bf16[1,512,512]{2,1,0:T(8,128)(2,1)}, bf16[1,512,512]{2,1,0:T(8,128)(2,1)}, u32[]{:S(2)}, u32[]{:S(2)}) collective-permute-start(bf16[1,512,512]{2,1,0:T(8,128)(2,1)} %get-tuple-element.84), channel_id=1, source_target_pairs={{0,1},{1,0},{2,3},{3,2},{4,5},{5,4},{6,7},{7,6},{8,9},{9,8},{10,11... | collective-permute-start | bytes 1572872 | tf_op jit(solution)/shard_map/ppermute | solution.py:59
  174.2 13.3 %collective-permute-start.23 = (bf16[1,512,512]{2,1,0:T(8,128)(2,1)}, bf16[1,512,512]{2,1,0:T(8,128)(2,1)}, u32[]{:S(2)}, u32[]{:S(2)}) collective-permute-start(bf16[1,512,512]{2,1,0:T(8,128)(2,1)} %get-tuple-element.85), channel_id=1, source_target_pairs={{0,1},{1,0},{2,3},{3,2},{4,5},{5,4},{6,7},{7,6},{8,9},{9,8},{10,11... | collective-permute-start | bytes 1572872 | tf_op jit(solution)/shard_map/ppermute | solution.py:59
  181.5 14.5 %all-to-all-start.3 = ((bf16[16,16,512]{2,1,0:T(8,128)(2,1)}), bf16[16,16,512]{2,1,0:T(8,128)(2,1)S(1)}, u32[]{:S(2)}, u32[]{:S(2)}) async-start(bf16[16,16,512]{2,1,0:T(8,128)(2,1)} %get-tuple-element.88), calls=%async_computation.3 | async-start | bytes 524288 | tf_op jit(solution)/shard_map/all_to_all | solution.py:449
  187.4 10.1 %copy-start.13 = (bf16[512,512]{1,0:T(8,128)(2,1)S(1)}, bf16[512,512]{1,0:T(8,128)(2,1)}, u32[]{:S(2)}) copy-start(bf16[512,512]{1,0:T(8,128)(2,1)} %copy-done.12) | copy-start | bytes 1572868
  196.0 25.4 %collective-permute-start.30 = (bf16[4,512,512]{2,1,0:T(8,128)(2,1)}, bf16[4,512,512]{2,1,0:T(8,128)(2,1)S(1)}, u32[]{:S(2)}, u32[]{:S(2)}) collective-permute-start(bf16[4,512,512]{2,1,0:T(8,128)(2,1)} %copy-done.9), channel_id=1, source_target_pairs={{0,2},{1,7},{2,4},{3,1},{4,6},{5,3},{6,0},{7,5},{8,10},{9,15},{10,... | collective-permute-start | bytes 6291464 | tf_op jit(solution)/shard_map/ppermute | solution.py:59
  203.4 2.0 collective-permute-start.24
  203.5 2.6 collective-permute-start.25
  213.2 2.0 collective-permute-start.26
  213.4 3.9 %collective-permute-start.27 = (bf16[1,512,512]{2,1,0:T(8,128)(2,1)S(1)}, bf16[1,512,512]{2,1,0:T(8,128)(2,1)S(1)}, u32[]{:S(2)}, u32[]{:S(2)}) collective-permute-start(bf16[1,512,512]{2,1,0:T(8,128)(2,1)S(1)} %get-tuple-element.96), channel_id=1, source_target_pairs={{0,1},{1,0},{2,3},{3,2},{4,5},{5,4},{6,7},{7,6},{8,9},{9,8},{10,11... | collective-permute-start | bytes 1572872 | tf_op jit(solution)/shard_map/ppermute | solution.py:59
  213.8 3.5 %collective-permute-start.28 = (bf16[1,512,512]{2,1,0:T(8,128)(2,1)S(1)}, bf16[1,512,512]{2,1,0:T(8,128)(2,1)S(1)}, u32[]{:S(2)}, u32[]{:S(2)}) collective-permute-start(bf16[1,512,512]{2,1,0:T(8,128)(2,1)S(1)} %get-tuple-element.97), channel_id=1, source_target_pairs={{0,1},{1,0},{2,3},{3,2},{4,5},{5,4},{6,7},{7,6},{8,9},{9,8},{10,11... | collective-permute-start | bytes 1572872 | tf_op jit(solution)/shard_map/ppermute | solution.py:59
  213.9 3.5 %collective-permute-start.29 = (bf16[1,512,512]{2,1,0:T(8,128)(2,1)S(1)}, bf16[1,512,512]{2,1,0:T(8,128)(2,1)S(1)}, u32[]{:S(2)}, u32[]{:S(2)}) collective-permute-start(bf16[1,512,512]{2,1,0:T(8,128)(2,1)S(1)} %get-tuple-element.98), channel_id=1, source_target_pairs={{0,1},{1,0},{2,3},{3,2},{4,5},{5,4},{6,7},{7,6},{8,9},{9,8},{10,11... | collective-permute-start | bytes 1572872 | tf_op jit(solution)/shard_map/ppermute | solution.py:59
  215.2 17.5 %collective-permute-start.32 = (bf16[2,512,512]{2,1,0:T(8,128)(2,1)S(1)}, bf16[2,512,512]{2,1,0:T(8,128)(2,1)S(1)}, u32[]{:S(2)}, u32[]{:S(2)}) collective-permute-start(bf16[2,512,512]{2,1,0:T(8,128)(2,1)S(1)} %chunks.21), channel_id=1, source_target_pairs={{0,2},{1,7},{2,4},{3,1},{4,6},{5,3},{6,0},{7,5},{8,10},{9,15},{10,... | collective-permute-start | bytes 3145736 | tf_op jit(solution)/shard_map/ppermute | solution.py:59
  223.1 4.7 %collective-permute-start.31 = (bf16[1,512,512]{2,1,0:T(8,128)(2,1)S(1)}, bf16[1,512,512]{2,1,0:T(8,128)(2,1)S(1)}, u32[]{:S(2)}, u32[]{:S(2)}) collective-permute-start(bf16[1,512,512]{2,1,0:T(8,128)(2,1)S(1)} %chunks.23), channel_id=1, source_target_pairs={{0,1},{1,0},{2,3},{3,2},{4,5},{5,4},{6,7},{7,6},{8,9},{9,8},{10,11... | collective-permute-start | bytes 1572872 | tf_op jit(solution)/shard_map/ppermute | solution.py:59
  237.0 21.7 %collective-permute-start.35 = (bf16[2,512,512]{2,1,0:T(8,128)(2,1)S(1)}, bf16[2,512,512]{2,1,0:T(8,128)(2,1)S(1)}, u32[]{:S(2)}, u32[]{:S(2)}) collective-permute-start(bf16[2,512,512]{2,1,0:T(8,128)(2,1)S(1)} %get-tuple-element.103), channel_id=1, source_target_pairs={{0,2},{1,7},{2,4},{3,1},{4,6},{5,3},{6,0},{7,5},{8,10},{9,15},{10,... | collective-permute-start | bytes 3145736 | tf_op jit(solution)/shard_map/ppermute | solution.py:59
  241.1 4.3 %collective-permute-start.33 = (bf16[1,512,512]{2,1,0:T(8,128)(2,1)S(1)}, bf16[1,512,512]{2,1,0:T(8,128)(2,1)S(1)}, u32[]{:S(2)}, u32[]{:S(2)}) collective-permute-start(bf16[1,512,512]{2,1,0:T(8,128)(2,1)S(1)} %chunks.26), channel_id=1, source_target_pairs={{0,1},{1,0},{2,3},{3,2},{4,5},{5,4},{6,7},{7,6},{8,9},{9,8},{10,11... | collective-permute-start | bytes 1572872 | tf_op jit(solution)/shard_map/ppermute | solution.py:59
  241.9 15.0 %collective-permute-start.34 = (bf16[1,512,512]{2,1,0:T(8,128)(2,1)S(1)}, bf16[1,512,512]{2,1,0:T(8,128)(2,1)S(1)}, u32[]{:S(2)}, u32[]{:S(2)}) collective-permute-start(bf16[1,512,512]{2,1,0:T(8,128)(2,1)S(1)} %chunks.24), channel_id=1, source_target_pairs={{0,8},{1,9},{2,10},{3,11},{4,12},{5,13},{6,14},{7,15},{8,0},{9,1},... | collective-permute-start | bytes 1572872 | tf_op jit(solution)/shard_map/ppermute | solution.py:59
  243.4 21.2 %collective-permute-start.37 = (bf16[2,512,512]{2,1,0:T(8,128)(2,1)S(1)}, bf16[2,512,512]{2,1,0:T(8,128)(2,1)S(1)}, u32[]{:S(2)}, u32[]{:S(2)}) collective-permute-start(bf16[2,512,512]{2,1,0:T(8,128)(2,1)S(1)} %get-tuple-element.109), channel_id=1, source_target_pairs={{0,2},{1,7},{2,4},{3,1},{4,6},{5,3},{6,0},{7,5},{8,10},{9,15},{10,... | collective-permute-start | bytes 3145736 | tf_op jit(solution)/shard_map/ppermute | solution.py:59
  260.4 2.5 collective-permute-start.36
  266.3 4.4 %collective-permute-start.38 = (bf16[1,512,512]{2,1,0:T(8,128)(2,1)S(1)}, bf16[1,512,512]{2,1,0:T(8,128)(2,1)S(1)}, u32[]{:S(2)}, u32[]{:S(2)}) collective-permute-start(bf16[1,512,512]{2,1,0:T(8,128)(2,1)S(1)} %chunks.30), channel_id=1, source_target_pairs={{0,1},{1,0},{2,3},{3,2},{4,5},{5,4},{6,7},{7,6},{8,9},{9,8},{10,11... | collective-permute-start | bytes 1572872 | tf_op jit(solution)/shard_map/ppermute | solution.py:59
  269.1 15.0 %collective-permute-start.39 = (bf16[1,512,512]{2,1,0:T(8,128)(2,1)S(1)}, bf16[1,512,512]{2,1,0:T(8,128)(2,1)S(1)}, u32[]{:S(2)}, u32[]{:S(2)}) collective-permute-start(bf16[1,512,512]{2,1,0:T(8,128)(2,1)S(1)} %chunks.29), channel_id=1, source_target_pairs={{0,8},{1,9},{2,10},{3,11},{4,12},{5,13},{6,14},{7,15},{8,0},{9,1},... | collective-permute-start | bytes 1572872 | tf_op jit(solution)/shard_map/ppermute | solution.py:59
  (11 other events, 12.1 us)

commit v3 on v2

--- a/solution.py
+++ b/solution.py
@@ -443,6 +443,7 @@
         return line.add(line.next(value)[index])
 
     def projected(pieces, index, *more):
+        pieces = [p[None] for p in pieces]
         return line.add(project(pieces, line.next(index), *weights, *more))
 
     def spread(keyval):
@@ -500,44 +501,43 @@
     up_other = send(other, TO_Y)
     position = line.next(row_ids) - begin
     tables = line.add(rotary_tables(position, member))
-    total = projected([value[None], other[None]], order[:2], CAP)
+    total = projected([value, other], order[:2], CAP)
     across, up, up_other = join(across, up, up_other)
+    there_up1 = [send(u[BLOCK:], TO_X) for u in (up, up_other)]
     far = send(up, TO_Y)
-    there_up1 = send(jnp.stack([up[BLOCK:], up_other[BLOCK:]]), TO_X)
     across_other = send(across, TO_CORE)
-    there_up0 = send(jnp.stack([across[:BLOCK], across_other[:BLOCK]]), TO_Y)
+    there_up0 = [send(a[:BLOCK], TO_Y) for a in (across, across_other)]
     down, down_other = send(up, TO_CORE), send(up_other, TO_CORE)
     pieces = [up, up_other, down, down_other, across, across_other]
-    total = projected([p[None] for p in pieces], order[2:8], CAP, total)
-    far, *there_up = join(far, there_up0, there_up1)
-    there_far = [send(there_up[0][:1], TO_Y), send(far[None, BLOCK:], TO_X)]
+    total = projected(pieces, order[2:8], CAP, total)
+    far, *there_up = join(far, *there_up0, *there_up1)
+    there_far0 = send(there_up[0], TO_Y)
+    there_far1 = send(far[BLOCK:], TO_X)
+    far_other = send(far, TO_CORE)
     there_down = [send(u, TO_CORE) for u in there_up]
-    far_other = send(far, TO_CORE)
-    pieces = [far[None], far_other[None], there_up[0], there_down[0]]
+    pieces = [far, far_other, *there_up[:2], *there_down[:2]]
     total0 = projected(pieces, order[8:14], BLOCK, total, None, 0)
-    there_far0, far = join(there_far[0], far)
+    there_far0, far = join(there_far0, far)
     pieces = [there_far0, send(there_far0, TO_CORE)]
-    query0, keyval0 = projected(pieces, order[14:], BLOCK, total0, tables, 0)
+    index = after(order[14:], there_far1)
+    query0, keyval0 = projected(pieces, index, BLOCK, total0, tables, 0)
     keyval0 = spread(keyval0)
-    pieces = [far[None], far_other[None], there_up[1], there_down[1]]
-    there_far_other1 = send(there_far[1], TO_CORE)
-    index = after(order[8:14], there_far_other1)
-    total1 = projected(pieces, index, BLOCK, total, None, 1)
+    pieces = [far, far_other, *there_up[2:], *there_down[2:]]
+    pieces += [there_far1, move(there_far1, TO_CORE)]
+    query1, keyval1 = projected(pieces, order[8:], BLOCK, total, tables, 1)
+    keyval1 = spread(keyval1)
+
     heads0 = attended(0, query0, [keyval0])
     far0 = far_sums(heads0, far_for_core(heads0))
-    passed = near_for_core(heads0)
-    pieces = [there_far[1], there_far_other1]
-    query1, keyval1 = projected(pieces, order[14:], BLOCK, total1, tables, 1)
-    keyval1 = spread(keyval1)
-    near0 = near_sums(heads0, passed, far0, (4,))[0]
-    near0 = send(after(near0, keyval1), TO_Y)
     heads1 = attended(1, query1, [keyval0, keyval1])
     far1 = far_sums(heads1, far_for_core(heads1))
+    passed = near_for_core(heads0)
+    near0 = [send(t, TO_Y) for t in near_sums(heads0, passed, far0, (2, 2))]
     passed = near_for_core(heads1)
-    crossed0 = send(last_sum(0, after(heads0, *passed), near0, 0), TO_X)
     near1 = [send(t, TO_Y) for t in near_sums(heads1, passed, far1, (2, 2))]
-    result0 = last_sum(1, heads0, near0, 2, crossed0)
+    crossed0 = send(last_sum(0, heads0, near0[0], 0), TO_X)
     crossed1 = send(last_sum(0, heads1, near1[0], 0), TO_X)
+    result0 = last_sum(1, heads0, near0[1], 0, crossed0)
     result1 = last_sum(1, heads1, near1[1], 0, crossed1)
     return jnp.concatenate([result0[0], result1[0]], axis=0)
 

time: 288 us -> 269 us (0.934)
  waiting for transfers between devices: 95.3 us -> 76.9 us
  Pallas kernels: 99.7 us -> 94.5 us
  local copies, waits for them, and re-layouts: 17 us -> 21.4 us
    ppermute x40 -> x45, waiting for transfers between devices: 66 us -> 46.3 us  [send(): return lax.ppermute(value, 'tp', pairs)]
    unnamed x30 -> x32, local copies, waits for them, and re-layouts: 12.1 us -> 16.2 us
    pallas_call x6 -> x5, Pallas kernels: 43.9 us -> 41.4 us  [project(): pl.pallas_call(functools.partial(project_kernel, counts, total is not Non...]
    ppermute x40 -> x45, starting transfers between devices: 42.8 us -> 42.3 us  [send(): return lax.ppermute(value, 'tp', pairs)]
  transfers between devices with their start and end apart: 44 -> 49, of which waited for: 20 -> 25; matrix products, arithmetic and copies ran while one was open for 4% -> 4% of each run, Pallas kernels for 28% -> 31%
where the time goes in v3:
time: 269 us; the launch traced here: 267 us
  Pallas kernels  94.5 us (35%)
  waiting for transfers between devices  76.9 us (29%)
  starting transfers between devices  64.4 us (24%)
  local copies, waits for them, and re-layouts  21.4 us (8%)
  other arithmetic  9.64 us (4%)
    ppermute x45, waiting for transfers between devices, send(): return lax.ppermute(value, 'tp', pairs)  46.3 us
    ppermute x45, starting transfers between devices, send(): return lax.ppermute(value, 'tp', pairs)  42.3 us
    pallas_call x16, Pallas kernels, chunks(): pl.pallas_call(functools.partial(chunks_kernel, groups, tuple((len(a) for...  41.9 us
    pallas_call x5, Pallas kernels, project(): pl.pallas_call(functools.partial(project_kernel, counts, total is not Non...  41.4 us
    all_to_all x1, waiting for transfers between devices, body(): lax.all_to_all(outgoing, 'sec', split_axis=0, concat_axis=0, tiled=True)  26.3 us
    unnamed x32, local copies, waits for them, and re-layouts  16.2 us
    all_to_all x2, starting transfers between devices, spread(): lax.all_to_all(line.next(keyval), 'tp', split_axis=0, concat_axis=0, tile...  11.5 us
    all_to_all x1, starting transfers between devices, body(): lax.all_to_all(facts, 'sec', split_axis=0, concat_axis=0, tiled=True)  6.79 us
  transfers between devices with their start and end apart: 49, of which 25 were waited for; matrix products, arithmetic and copies ran while one was open for 4% of the time, Pallas kernels for 31%

profile of v3, /device:TPU:1, one launch (start us, length us, event | category | flops | bytes accessed | tf_op | source)
XLA Modules:
  0.0 267.3 jit_solution(9221750388846906180)
XLA Ops:
  3.0 6.8 %all-to-all-start = ((s32[8,1,2]{2,1,0:T(1,128)}), s32[8,1,2]{2,1,0:T(1,128)S(1)}, u32[]{:S(2)}, u32[]{:S(2)}) async-start(s32[8,1,2]{2,1,0:T(1,128)} %copy.9), calls=%async_computation | async-start | bytes 8192 | tf_op jit(solution)/shard_map/all_to_all | solution.py:415
  11.4 2.0 cut.1
  14.7 3.9 %all-to-all-start.1 = ((bf16[8,272,512]{2,1,0:T(8,128)(2,1)}), bf16[8,272,512]{2,1,0:T(8,128)(2,1)S(1)}, u32[]{:S(2)}, u32[]{:S(2)}) async-start(bf16[8,272,512]{2,1,0:T(8,128)(2,1)} %cut.1), calls=%async_computation.1 | async-start | bytes 4456448 | tf_op jit(solution)/shard_map/all_to_all | solution.py:414
  18.9 26.3 %all-to-all-done.1.arrived_ref = bf16[8,272,512]{2,1,0:T(8,128)(2,1)S(1)} async-done(((bf16[8,272,512]{2,1,0:T(8,128)(2,1)}), bf16[8,272,512]{2,1,0:T(8,128)(2,1)S(1)}, u32[]{:S(2)}, u32[]{:S(2)}) %all-to-all-start.1) | async-done | bytes 2228256 | tf_op jit(solution)/shard_map/all_to_all | solution.py:414
  45.2 3.5 %pack.1 = bf16[1024,512]{1,0:T(8,128)(2,1)S(1)} custom-call(s32[3,8]{1,0:T(4,128)S(1)} %pad_add_fusion.plan_ref, bf16[8,272,512]{2,1,0:T(8,128)(2,1)S(1)} %all-to-all-done.1.arrived_ref), custom_call_target="tpu_custom_call" | custom-call | tf_op jit(solution)/shard_map/pack/pallas_call | solution.py:109
  48.8 2.8 %collective-permute-start.2 = (bf16[1024,512]{1,0:T(8,128)(2,1)S(1)}, bf16[1024,512]{1,0:T(8,128)(2,1)S(1)}, u32[]{:S(2)}, u32[]{:S(2)}) collective-permute-start(bf16[1024,512]{1,0:T(8,128)(2,1)S(1)} %pack.1), channel_id=1, source_target_pairs={{0,1},{1,0},{2,3},{3,2},{4,5},{5,4},{6,7},{7,6},{8,9},{9,8},{10,11... | collective-permute-start | bytes 3145736 | tf_op jit(solution)/shard_map/ppermute | solution.py:59
  51.6 2.5 collective-permute-start
  54.1 2.8 %collective-permute-start.1 = (bf16[1024,512]{1,0:T(8,128)(2,1)S(1)}, bf16[1024,512]{1,0:T(8,128)(2,1)S(1)}, u32[]{:S(2)}, u32[]{:S(2)}) collective-permute-start(bf16[1024,512]{1,0:T(8,128)(2,1)S(1)} %pack.1), channel_id=1, source_target_pairs={{0,2},{1,7},{2,4},{3,1},{4,6},{5,3},{6,0},{7,5},{8,10},{9,15},{10,... | collective-permute-start | bytes 3145736 | tf_op jit(solution)/shard_map/ppermute | solution.py:59
  57.5 5.5 %fusion.3 = (f32[1024,128]{1,0:T(8,128)}, f32[1024,128]{1,0:T(8,128)}, f32[1024,128]{1,0:T(8,128)}, f32[1024,128]{1,0:T(8,128)}) fusion(f32[128]{0:T(128)S(1)} %fusion.9, f32[128]{0:T(128)S(1)} %get-tuple-element.123, f32[1024]{0:T(1024)S(1)} %subtract_convert_fusion, pred[]{:T(512)S(6)} %lt.136, f32[128]{0:T(128)S(1)} %get-tuple-element.124), kind=kLoop, calls=%fused_computation.8 | loop fusion | flops 786432 | bytes 2102785 | tf_op jit(solution)/shard_map/jit(_where)/select_n | solution.py:399
  63.0 4.4 %project.5.refs_8_ = f32[1024,640]{1,0:T(8,128)S(1)} custom-call(s32[2]{0:T(128)S(1)} %pad_add_fusion.6.index_ref, bf16[1,1024,512]{2,1,0:T(8,128)(2,1)S(1)} %bitcast.77, bf16[1,1024,512]{2,1,0:T(8,128)(2,1)S(1)} %bitcast.88, bf16[8192,512]{1,0:T(8,128)(2,1)} %bitcast.110, bf16[8192,128]{1,0:T(8,128)(2,1)} %bitcast.115), custom_call_target="tpu_custom_call" | custom-call | tf_op jit(solution)/shard_map/project/pallas_call | solution.py:230
  68.9 9.0 %collective-permute-done = bf16[1024,512]{1,0:T(8,128)(2,1)S(1)} collective-permute-done((bf16[1024,512]{1,0:T(8,128)(2,1)S(1)}, bf16[1024,512]{1,0:T(8,128)(2,1)S(1)}, u32[]{:S(2)}, u32[]{:S(2)}) %collective-permute-start) | collective-permute-done | bytes 1048608 | tf_op jit(solution)/shard_map/ppermute | solution.py:59
  77.9 1.9 collective-permute-done.3
  79.8 1.9 collective-permute-start.6
  89.4 2.2 collective-permute-start.9
  97.7 12.2 %project.6.refs_8_.refs_10_ = f32[1024,640]{1,0:T(8,128)S(1)} custom-call(s32[6]{0:T(128)S(1)} %stack.146.index_ref, bf16[1,1024,512]{2,1,0:T(8,128)(2,1)S(1)} %bitcast.80, bf16[1,1024,512]{2,1,0:T(8,128)(2,1)S(1)} %bitcast.82, bf16[1,1024,512]{2,1,0:T(8,128)(2,1)S(1)} %bitcast.89, bf16[1,1024,512]{2,1,0:T(8,128)(2,1)S(1)} %bitcast.90, ...), custom_call_target="tpu_custom_call" | custom-call | tf_op jit(solution)/shard_map/project/pallas_call | solution.py:230
  111.4 2.0 collective-permute-done.9
  118.3 7.9 %project.7.refs_4_ = f32[512,640]{1,0:T(8,128)S(1)} custom-call(s32[6]{0:T(128)S(1)} %stack.147.index_ref, bf16[1,1024,512]{2,1,0:T(8,128)(2,1)S(1)} %bitcast.75, bf16[1,1024,512]{2,1,0:T(8,128)(2,1)S(1)} %bitcast.78, bf16[1,512,512]{2,1,0:T(8,128)(2,1)} %bitcast.39.refs_2_, bf16[1,512,512]{2,1,0:T(8,128)(2,1)} %bitcast.40.refs_3_, ...), custom_call_target="tpu_custom_call" | custom-call | tf_op jit(solution)/shard_map/project/pallas_call | solution.py:230
  128.4 2.4 collective-permute-done.12
  130.8 5.9 %project.8 = (bf16[512,512]{1,0:T(8,128)(2,1)S(1)}, bf16[16,16,512]{2,1,0:T(8,128)(2,1)}) custom-call(s32[2]{0:T(128)S(1)} %pad_add_fusion.5.index_ref, bf16[1,512,512]{2,1,0:T(8,128)(2,1)S(1)} %bitcast.92, bf16[1,512,512]{2,1,0:T(8,128)(2,1)} %bitcast.44.refs_1_, bf16[8192,512]{1,0:T(8,128)(2,1)} %bitcast.113, bf16[8192,128]{1,0:T(8,128)(2,1)} %bitcast.118, ...), custom_call_target="tpu_custom_call" | custom-call | tf_op jit(solution)/shard_map/project/pallas_call | solution.py:230
  139.1 4.3 %all-to-all-start.2 = ((bf16[16,16,512]{2,1,0:T(8,128)(2,1)}), bf16[16,16,512]{2,1,0:T(8,128)(2,1)S(1)}, u32[]{:S(2)}, u32[]{:S(2)}) async-start(bf16[16,16,512]{2,1,0:T(8,128)(2,1)} %get-tuple-element.79), calls=%async_computation.2 | async-start | bytes 524288 | tf_op jit(solution)/shard_map/all_to_all | solution.py:450
  143.5 11.0 %project.9 = (bf16[512,512]{1,0:T(8,128)(2,1)S(1)}, bf16[16,16,512]{2,1,0:T(8,128)(2,1)}) custom-call(s32[8]{0:T(128)S(1)} %stack.143.index_ref, bf16[1,1024,512]{2,1,0:T(8,128)(2,1)S(1)} %bitcast.76, bf16[1,1024,512]{2,1,0:T(8,128)(2,1)S(1)} %bitcast.79, bf16[1,512,512]{2,1,0:T(8,128)(2,1)} %bitcast.46.refs_2_, bf16[1,512,512]{2,1,0:T(8,128)(2,1)} %bitcast.47.refs_3_, ...), custom_call_target="tpu_custom_call" | custom-call | tf_op jit(solution)/shard_map/project/pallas_call | solution.py:230
  156.4 2.6 attend.2.heads_ref
  159.0 2.8 %chunks.16 = (bf16[1,512,512]{2,1,0:T(8,128)(2,1)S(1)}, bf16[1,512,512]{2,1,0:T(8,128)(2,1)S(1)}) custom-call(s32[2]{0:T(128)S(1)} %pad_add_fusion.4.index_ref, bf16[512,512]{1,0:T(8,128)(2,1)S(1)} %attend.2.heads_ref, bf16[512,8192]{1,0:T(8,128)(2,1)} %bitcast.94), custom_call_target="tpu_custom_call" | custom-call | tf_op jit(solution)/shard_map/chunks/pallas_call | solution.py:355
  162.4 7.2 %all-to-all-start.3 = ((bf16[16,16,512]{2,1,0:T(8,128)(2,1)}), bf16[16,16,512]{2,1,0:T(8,128)(2,1)S(1)}, u32[]{:S(2)}, u32[]{:S(2)}) async-start(bf16[16,16,512]{2,1,0:T(8,128)(2,1)} %get-tuple-element.86), calls=%async_computation.3 | async-start | bytes 524288 | tf_op jit(solution)/shard_map/all_to_all | solution.py:450
  169.7 2.9 %chunks.17 = bf16[2,512,512]{2,1,0:T(8,128)(2,1)S(1)} custom-call(s32[2]{0:T(128)S(1)} %pad_add_fusion.3.index_ref, bf16[512,512]{1,0:T(8,128)(2,1)S(1)} %attend.2.heads_ref, bf16[512,8192]{1,0:T(8,128)(2,1)} %bitcast.95, bf16[1,512,512]{2,1,0:T(8,128)(2,1)S(1)} %collective-permute-done.21.refs_0_, bf16[1,512,512]{2,1,0:T(8,128)(2,1)S(1)} %collective-permute-done.22.refs_1_), custom_call_target="tpu_custom_call" | custom-call | tf_op jit(solution)/shard_map/chunks/pallas_call | solution.py:355
  172.6 2.7 collective-permute-start.26
  175.3 3.0 %all-to-all-done.3 = bf16[16,16,512]{2,1,0:T(8,128)(2,1)S(1)} async-done(((bf16[16,16,512]{2,1,0:T(8,128)(2,1)}), bf16[16,16,512]{2,1,0:T(8,128)(2,1)S(1)}, u32[]{:S(2)}, u32[]{:S(2)}) %all-to-all-start.3) | async-done | bytes 262176 | tf_op jit(solution)/shard_map/all_to_all | solution.py:450
  179.4 3.1 %attend.3.heads_ref = bf16[512,512]{1,0:T(8,128)(2,1)S(1)} custom-call(s32[3,8]{1,0:T(4,128)S(1)} %pad_add_fusion.plan_ref, bf16[512,512]{1,0:T(8,128)(2,1)S(1)} %copy-done.15, bf16[256,512]{1,0:T(8,128)(2,1)S(1)} %bitcast.85, bf16[256,512]{1,0:T(8,128)(2,1)S(1)} %bitcast.91), custom_call_target="tpu_custom_call" | custom-call | tf_op jit(solution)/shard_map/attend/pallas_call | solution.py:293
  182.4 2.9 %chunks.18 = (bf16[1,512,512]{2,1,0:T(8,128)(2,1)S(1)}, bf16[1,512,512]{2,1,0:T(8,128)(2,1)S(1)}) custom-call(s32[2]{0:T(128)S(1)} %pad_add_fusion.4.index_ref, bf16[512,512]{1,0:T(8,128)(2,1)S(1)} %attend.3.heads_ref, bf16[512,8192]{1,0:T(8,128)(2,1)} %bitcast.96), custom_call_target="tpu_custom_call" | custom-call | tf_op jit(solution)/shard_map/chunks/pallas_call | solution.py:355
  188.7 2.9 %chunks.19 = bf16[2,512,512]{2,1,0:T(8,128)(2,1)S(1)} custom-call(s32[2]{0:T(128)S(1)} %pad_add_fusion.3.index_ref, bf16[512,512]{1,0:T(8,128)(2,1)S(1)} %attend.3.heads_ref, bf16[512,8192]{1,0:T(8,128)(2,1)} %bitcast.97, bf16[1,512,512]{2,1,0:T(8,128)(2,1)S(1)} %collective-permute-done.23.refs_0_, bf16[1,512,512]{2,1,0:T(8,128)(2,1)S(1)} %collective-permute-done.24.refs_1_), custom_call_target="tpu_custom_call" | custom-call | tf_op jit(solution)/shard_map/chunks/pallas_call | solution.py:355
  192.8 4.1 %chunks.20 = (bf16[1,512,512]{2,1,0:T(8,128)(2,1)S(1)}, bf16[1,512,512]{2,1,0:T(8,128)(2,1)S(1)}, bf16[1,512,512]{2,1,0:T(8,128)(2,1)S(1)}, bf16[1,512,512]{2,1,0:T(8,128)(2,1)S(1)}) custom-call(s32[4]{0:T(128)S(1)} %pad_add_fusion.2.index_ref, bf16[512,512]{1,0:T(8,128)(2,1)S(1)} %attend.2.heads_ref, bf16[512,8192]{1,0:T(8,128)(2,1)} %bitcast.98), custom_call_target="tpu_custom_call" | custom-call | tf_op jit(solution)/shard_map/chunks/pallas_call | solution.py:355
  201.1 4.3 %chunks.21 = (bf16[2,512,512]{2,1,0:T(8,128)(2,1)S(1)}, bf16[2,512,512]{2,1,0:T(8,128)(2,1)S(1)}) custom-call(s32[4]{0:T(128)S(1)} %pad_add_fusion.1.index_ref, bf16[512,512]{1,0:T(8,128)(2,1)S(1)} %attend.2.heads_ref, bf16[512,8192]{1,0:T(8,128)(2,1)} %bitcast.99, bf16[1,512,512]{2,1,0:T(8,128)(2,1)S(1)} %collective-permute-done.25.refs_0_, ...), custom_call_target="tpu_custom_call" | custom-call | tf_op jit(solution)/shard_map/chunks/pallas_call | solution.py:355
  205.4 2.2 collective-permute-start.35
  207.6 4.1 %chunks.22 = (bf16[1,512,512]{2,1,0:T(8,128)(2,1)S(1)}, bf16[1,512,512]{2,1,0:T(8,128)(2,1)S(1)}, bf16[1,512,512]{2,1,0:T(8,128)(2,1)S(1)}, bf16[1,512,512]{2,1,0:T(8,128)(2,1)S(1)}) custom-call(s32[4]{0:T(128)S(1)} %pad_add_fusion.2.index_ref, bf16[512,512]{1,0:T(8,128)(2,1)S(1)} %attend.3.heads_ref, bf16[512,8192]{1,0:T(8,128)(2,1)} %bitcast.100), custom_call_target="tpu_custom_call" | custom-call | tf_op jit(solution)/shard_map/chunks/pallas_call | solution.py:355
  215.9 4.3 %chunks.23 = (bf16[2,512,512]{2,1,0:T(8,128)(2,1)S(1)}, bf16[2,512,512]{2,1,0:T(8,128)(2,1)S(1)}) custom-call(s32[4]{0:T(128)S(1)} %pad_add_fusion.1.index_ref, bf16[512,512]{1,0:T(8,128)(2,1)S(1)} %attend.3.heads_ref, bf16[512,8192]{1,0:T(8,128)(2,1)} %bitcast.101, bf16[1,512,512]{2,1,0:T(8,128)(2,1)S(1)} %collective-permute-done.30.refs_0_, ...), custom_call_target="tpu_custom_call" | custom-call | tf_op jit(solution)/shard_map/chunks/pallas_call | solution.py:355
  223.4 1.8 collective-permute-start.39
  225.2 1.7 chunks.25
  226.9 7.4 %collective-permute-done.37.refs_0_ = bf16[2,512,512]{2,1,0:T(8,128)(2,1)S(1)} collective-permute-done((bf16[2,512,512]{2,1,0:T(8,128)(2,1)S(1)}, bf16[2,512,512]{2,1,0:T(8,128)(2,1)S(1)}, u32[]{:S(2)}, u32[]{:S(2)}) %collective-permute-start.37) | collective-permute-done | bytes 1048608 | tf_op jit(solution)/shard_map/ppermute | solution.py:59
  235.9 2.3 collective-permute-start.38
  239.8 1.7 chunks.27
  241.5 4.0 %collective-permute-done.39.refs_0_ = bf16[2,512,512]{2,1,0:T(8,128)(2,1)S(1)} collective-permute-done((bf16[2,512,512]{2,1,0:T(8,128)(2,1)S(1)}, bf16[2,512,512]{2,1,0:T(8,128)(2,1)S(1)}, u32[]{:S(2)}, u32[]{:S(2)}) %collective-permute-start.39) | collective-permute-done | bytes 1048608 | tf_op jit(solution)/shard_map/ppermute | solution.py:59
  247.2 2.3 collective-permute-start.40
  249.8 3.2 %collective-permute-done.41.refs_2_ = bf16[1,512,512]{2,1,0:T(8,128)(2,1)S(1)} collective-permute-done((bf16[1,512,512]{2,1,0:T(8,128)(2,1)S(1)}, bf16[1,512,512]{2,1,0:T(8,128)(2,1)S(1)}, u32[]{:S(2)}, u32[]{:S(2)}) %collective-permute-start.41) | collective-permute-done | bytes 524320 | tf_op jit(solution)/shard_map/ppermute | solution.py:59
  253.1 1.8 chunks.29
  254.9 1.8 collective-permute-done.42.refs_0_
  258.4 2.3 collective-permute-start.43
  260.7 3.7 %collective-permute-done.44.refs_2_ = bf16[1,512,512]{2,1,0:T(8,128)(2,1)S(1)} collective-permute-done((bf16[1,512,512]{2,1,0:T(8,128)(2,1)S(1)}, bf16[1,512,512]{2,1,0:T(8,128)(2,1)S(1)}, u32[]{:S(2)}, u32[]{:S(2)}) %collective-permute-start.44) | collective-permute-done | bytes 524320 | tf_op jit(solution)/shard_map/ppermute | solution.py:59
  264.4 1.8 chunks.31
  (141 shorter events, 60.9 us)
Async XLA Ops:
  3.0 11.7 %all-to-all-start = ((s32[8,1,2]{2,1,0:T(1,128)}), s32[8,1,2]{2,1,0:T(1,128)S(1)}, u32[]{:S(2)}, u32[]{:S(2)}) async-start(s32[8,1,2]{2,1,0:T(1,128)} %copy.9), calls=%async_computation | async-start | bytes 8192 | tf_op jit(solution)/shard_map/all_to_all | solution.py:415
  14.7 30.5 %all-to-all-start.1 = ((bf16[8,272,512]{2,1,0:T(8,128)(2,1)}), bf16[8,272,512]{2,1,0:T(8,128)(2,1)S(1)}, u32[]{:S(2)}, u32[]{:S(2)}) async-start(bf16[8,272,512]{2,1,0:T(8,128)(2,1)} %cut.1), calls=%async_computation.1 | async-start | bytes 4456448 | tf_op jit(solution)/shard_map/all_to_all | solution.py:414
  48.8 8.1 %collective-permute-start.2 = (bf16[1024,512]{1,0:T(8,128)(2,1)S(1)}, bf16[1024,512]{1,0:T(8,128)(2,1)S(1)}, u32[]{:S(2)}, u32[]{:S(2)}) collective-permute-start(bf16[1024,512]{1,0:T(8,128)(2,1)S(1)} %pack.1), channel_id=1, source_target_pairs={{0,1},{1,0},{2,3},{3,2},{4,5},{5,4},{6,7},{7,6},{8,9},{9,8},{10,11... | collective-permute-start | bytes 3145736 | tf_op jit(solution)/shard_map/ppermute | solution.py:59
  51.6 26.3 %collective-permute-start = (bf16[1024,512]{1,0:T(8,128)(2,1)S(1)}, bf16[1024,512]{1,0:T(8,128)(2,1)S(1)}, u32[]{:S(2)}, u32[]{:S(2)}) collective-permute-start(bf16[1024,512]{1,0:T(8,128)(2,1)S(1)} %pack.1), channel_id=1, source_target_pairs={{0,8},{1,9},{2,10},{3,11},{4,12},{5,13},{6,14},{7,15},{8,0},{9,1},... | collective-permute-start | bytes 3145736 | tf_op jit(solution)/shard_map/ppermute | solution.py:59
  54.1 23.8 %collective-permute-start.1 = (bf16[1024,512]{1,0:T(8,128)(2,1)S(1)}, bf16[1024,512]{1,0:T(8,128)(2,1)S(1)}, u32[]{:S(2)}, u32[]{:S(2)}) collective-permute-start(bf16[1024,512]{1,0:T(8,128)(2,1)S(1)} %pack.1), channel_id=1, source_target_pairs={{0,2},{1,7},{2,4},{3,1},{4,6},{5,3},{6,0},{7,5},{8,10},{9,15},{10,... | collective-permute-start | bytes 3145736 | tf_op jit(solution)/shard_map/ppermute | solution.py:59
  56.9 23.0 %collective-permute-start.3 = (bf16[1024,512]{1,0:T(8,128)(2,1)S(1)}, bf16[1024,512]{1,0:T(8,128)(2,1)S(1)}, u32[]{:S(2)}, u32[]{:S(2)}) collective-permute-start(bf16[1024,512]{1,0:T(8,128)(2,1)S(1)} %collective-permute-done.2), channel_id=1, source_target_pairs={{0,2},{1,7},{2,4},{3,1},{4,6},{5,3},{6,0},{7,5},{8,10},{9,15},{10,... | collective-permute-start | bytes 3145736 | tf_op jit(solution)/shard_map/ppermute | solution.py:59
  79.8 6.9 %collective-permute-start.6 = (bf16[1024,512]{1,0:T(8,128)(2,1)S(1)}, bf16[1024,512]{1,0:T(8,128)(2,1)S(1)}, u32[]{:S(2)}, u32[]{:S(2)}) collective-permute-start(bf16[1024,512]{1,0:T(8,128)(2,1)S(1)} %collective-permute-done), channel_id=1, source_target_pairs={{0,1},{1,0},{2,3},{3,2},{4,5},{5,4},{6,7},{7,6},{8,9},{9,8},{10,11... | collective-permute-start | bytes 3145736 | tf_op jit(solution)/shard_map/ppermute | solution.py:59
  81.7 6.7 %collective-permute-start.10 = (bf16[1024,512]{1,0:T(8,128)(2,1)S(1)}, bf16[1024,512]{1,0:T(8,128)(2,1)S(1)}, u32[]{:S(2)}, u32[]{:S(2)}) collective-permute-start(bf16[1024,512]{1,0:T(8,128)(2,1)S(1)} %collective-permute-done.1), channel_id=1, source_target_pairs={{0,1},{1,0},{2,3},{3,2},{4,5},{5,4},{6,7},{7,6},{8,9},{9,8},{10,11... | collective-permute-start | bytes 3145736 | tf_op jit(solution)/shard_map/ppermute | solution.py:59
  81.7 9.9 %collective-permute-start.11 = (bf16[1024,512]{1,0:T(8,128)(2,1)S(1)}, bf16[1024,512]{1,0:T(8,128)(2,1)S(1)}, u32[]{:S(2)}, u32[]{:S(2)}) collective-permute-start(bf16[1024,512]{1,0:T(8,128)(2,1)S(1)} %collective-permute-done.3), channel_id=1, source_target_pairs={{0,1},{1,0},{2,3},{3,2},{4,5},{5,4},{6,7},{7,6},{8,9},{9,8},{10,11... | collective-permute-start | bytes 3145736 | tf_op jit(solution)/shard_map/ppermute | solution.py:59
  82.2 31.2 %collective-permute-start.4 = (bf16[1024,512]{1,0:T(8,128)(2,1)S(1)}, bf16[1024,512]{1,0:T(8,128)(2,1)S(1)}, u32[]{:S(2)}, u32[]{:S(2)}) collective-permute-start(bf16[1024,512]{1,0:T(8,128)(2,1)S(1)} %collective-permute-done.1), channel_id=1, source_target_pairs={{0,2},{1,7},{2,4},{3,1},{4,6},{5,3},{6,0},{7,5},{8,10},{9,15},{10,... | collective-permute-start | bytes 3145736 | tf_op jit(solution)/shard_map/ppermute | solution.py:59
  86.3 25.1 %collective-permute-start.5 = (bf16[512,512]{1,0:T(8,128)(2,1)}, bf16[512,512]{1,0:T(8,128)(2,1)}, u32[]{:S(2)}, u32[]{:S(2)}) collective-permute-start(bf16[512,512]{1,0:T(8,128)(2,1)} %slice.33), channel_id=1, source_target_pairs={{0,2},{1,7},{2,4},{3,1},{4,6},{5,3},{6,0},{7,5},{8,10},{9,15},{10,... | collective-permute-start | bytes 1572872 | tf_op jit(solution)/shard_map/ppermute | solution.py:59
  86.7 24.7 %collective-permute-start.8 = (bf16[512,512]{1,0:T(8,128)(2,1)}, bf16[512,512]{1,0:T(8,128)(2,1)}, u32[]{:S(2)}, u32[]{:S(2)}) collective-permute-start(bf16[512,512]{1,0:T(8,128)(2,1)} %slice.35), channel_id=1, source_target_pairs={{0,8},{1,9},{2,10},{3,11},{4,12},{5,13},{6,14},{7,15},{8,0},{9,1},... | collective-permute-start | bytes 1572872 | tf_op jit(solution)/shard_map/ppermute | solution.py:59
  89.4 24.0 %collective-permute-start.9 = (bf16[512,512]{1,0:T(8,128)(2,1)}, bf16[512,512]{1,0:T(8,128)(2,1)}, u32[]{:S(2)}, u32[]{:S(2)}) collective-permute-start(bf16[512,512]{1,0:T(8,128)(2,1)} %slice.36), channel_id=1, source_target_pairs={{0,8},{1,9},{2,10},{3,11},{4,12},{5,13},{6,14},{7,15},{8,0},{9,1},... | collective-permute-start | bytes 1572872 | tf_op jit(solution)/shard_map/ppermute | solution.py:59
  92.6 20.8 %collective-permute-start.7 = (bf16[512,512]{1,0:T(8,128)(2,1)}, bf16[512,512]{1,0:T(8,128)(2,1)}, u32[]{:S(2)}, u32[]{:S(2)}) collective-permute-start(bf16[512,512]{1,0:T(8,128)(2,1)} %slice.38), channel_id=1, source_target_pairs={{0,2},{1,7},{2,4},{3,1},{4,6},{5,3},{6,0},{7,5},{8,10},{9,15},{10,... | collective-permute-start | bytes 1572872 | tf_op jit(solution)/shard_map/ppermute | solution.py:59
  113.4 4.9 %collective-permute-start.14 = (bf16[1024,512]{1,0:T(8,128)(2,1)S(1)}, bf16[1024,512]{1,0:T(8,128)(2,1)S(1)}, u32[]{:S(2)}, u32[]{:S(2)}) collective-permute-start(bf16[1024,512]{1,0:T(8,128)(2,1)S(1)} %collective-permute-done.4), channel_id=1, source_target_pairs={{0,1},{1,0},{2,3},{3,2},{4,5},{5,4},{6,7},{7,6},{8,9},{9,8},{10,11... | collective-permute-start | bytes 3145736 | tf_op jit(solution)/shard_map/ppermute | solution.py:59
  114.1 3.4 %collective-permute-start.15 = (bf16[512,512]{1,0:T(8,128)(2,1)}, bf16[512,512]{1,0:T(8,128)(2,1)}, u32[]{:S(2)}, u32[]{:S(2)}) collective-permute-start(bf16[512,512]{1,0:T(8,128)(2,1)} %collective-permute-done.5), channel_id=1, source_target_pairs={{0,1},{1,0},{2,3},{3,2},{4,5},{5,4},{6,7},{7,6},{8,9},{9,8},{10,11... | collective-permute-start | bytes 1572872 | tf_op jit(solution)/shard_map/ppermute | solution.py:59
  114.2 4.0 %collective-permute-start.16 = (bf16[512,512]{1,0:T(8,128)(2,1)}, bf16[512,512]{1,0:T(8,128)(2,1)}, u32[]{:S(2)}, u32[]{:S(2)}) collective-permute-start(bf16[512,512]{1,0:T(8,128)(2,1)} %collective-permute-done.7), channel_id=1, source_target_pairs={{0,1},{1,0},{2,3},{3,2},{4,5},{5,4},{6,7},{7,6},{8,9},{9,8},{10,11... | collective-permute-start | bytes 1572872 | tf_op jit(solution)/shard_map/ppermute | solution.py:59
  114.6 12.6 %collective-permute-start.13 = (bf16[512,512]{1,0:T(8,128)(2,1)}, bf16[512,512]{1,0:T(8,128)(2,1)S(1)}, u32[]{:S(2)}, u32[]{:S(2)}) collective-permute-start(bf16[512,512]{1,0:T(8,128)(2,1)} %collective-permute-done.5), channel_id=1, source_target_pairs={{0,2},{1,7},{2,4},{3,1},{4,6},{5,3},{6,0},{7,5},{8,10},{9,15},{10,... | collective-permute-start | bytes 1572872 | tf_op jit(solution)/shard_map/ppermute | solution.py:59
  116.3 14.5 %collective-permute-start.12 = (bf16[512,512]{1,0:T(8,128)(2,1)}, bf16[512,512]{1,0:T(8,128)(2,1)S(1)}, u32[]{:S(2)}, u32[]{:S(2)}) collective-permute-start(bf16[512,512]{1,0:T(8,128)(2,1)} %slice.37), channel_id=1, source_target_pairs={{0,8},{1,9},{2,10},{3,11},{4,12},{5,13},{6,14},{7,15},{8,0},{9,1},... | collective-permute-start | bytes 1572872 | tf_op jit(solution)/shard_map/ppermute | solution.py:59
  127.2 3.6 %collective-permute-start.17 = (bf16[512,512]{1,0:T(8,128)(2,1)S(1)}, bf16[512,512]{1,0:T(8,128)(2,1)}, u32[]{:S(2)}, u32[]{:S(2)}) collective-permute-start(bf16[512,512]{1,0:T(8,128)(2,1)S(1)} %collective-permute-done.13), channel_id=1, source_target_pairs={{0,1},{1,0},{2,3},{3,2},{4,5},{5,4},{6,7},{7,6},{8,9},{9,8},{10,11... | collective-permute-start | bytes 1572872 | tf_op jit(solution)/shard_map/ppermute | solution.py:59
  127.7 15.9 %collective-permute-start.18 = (bf16[512,512]{1,0:T(8,128)(2,1)}, bf16[512,512]{1,0:T(8,128)(2,1)}, u32[]{:S(2)}, u32[]{:S(2)}) collective-permute-start(bf16[512,512]{1,0:T(8,128)(2,1)} %collective-permute-done.8), channel_id=1, source_target_pairs={{0,1},{1,0},{2,3},{3,2},{4,5},{5,4},{6,7},{7,6},{8,9},{9,8},{10,11... | collective-permute-start | bytes 1572872 | tf_op jit(solution)/shard_map/ppermute | solution.py:59
  128.0 15.5 %collective-permute-start.19 = (bf16[512,512]{1,0:T(8,128)(2,1)}, bf16[512,512]{1,0:T(8,128)(2,1)}, u32[]{:S(2)}, u32[]{:S(2)}) collective-permute-start(bf16[512,512]{1,0:T(8,128)(2,1)} %collective-permute-done.9), channel_id=1, source_target_pairs={{0,1},{1,0},{2,3},{3,2},{4,5},{5,4},{6,7},{7,6},{8,9},{9,8},{10,11... | collective-permute-start | bytes 1572872 | tf_op jit(solution)/shard_map/ppermute | solution.py:59
  137.5 6.0 %collective-permute-start.20 = (bf16[512,512]{1,0:T(8,128)(2,1)S(1)}, bf16[512,512]{1,0:T(8,128)(2,1)}, u32[]{:S(2)}, u32[]{:S(2)}) collective-permute-start(bf16[512,512]{1,0:T(8,128)(2,1)S(1)} %collective-permute-done.12), channel_id=1, source_target_pairs={{0,1},{1,0},{2,3},{3,2},{4,5},{5,4},{6,7},{7,6},{8,9},{9,8},{10,11... | collective-permute-start | bytes 1572872 | tf_op jit(solution)/shard_map/ppermute | solution.py:59
  139.1 16.3 %all-to-all-start.2 = ((bf16[16,16,512]{2,1,0:T(8,128)(2,1)}), bf16[16,16,512]{2,1,0:T(8,128)(2,1)S(1)}, u32[]{:S(2)}, u32[]{:S(2)}) async-start(bf16[16,16,512]{2,1,0:T(8,128)(2,1)} %get-tuple-element.79), calls=%async_computation.2 | async-start | bytes 524288 | tf_op jit(solution)/shard_map/all_to_all | solution.py:450
  161.8 7.9 %collective-permute-start.21 = (bf16[1,512,512]{2,1,0:T(8,128)(2,1)S(1)}, bf16[1,512,512]{2,1,0:T(8,128)(2,1)S(1)}, u32[]{:S(2)}, u32[]{:S(2)}) collective-permute-start(bf16[1,512,512]{2,1,0:T(8,128)(2,1)S(1)} %get-tuple-element.81), channel_id=1, source_target_pairs={{0,1},{1,0},{2,3},{3,2},{4,5},{5,4},{6,7},{7,6},{8,9},{9,8},{10,11... | collective-permute-start | bytes 1572872 | tf_op jit(solution)/shard_map/ppermute | solution.py:59
  162.0 7.7 %collective-permute-start.22 = (bf16[1,512,512]{2,1,0:T(8,128)(2,1)S(1)}, bf16[1,512,512]{2,1,0:T(8,128)(2,1)S(1)}, u32[]{:S(2)}, u32[]{:S(2)}) collective-permute-start(bf16[1,512,512]{2,1,0:T(8,128)(2,1)S(1)} %get-tuple-element.83), channel_id=1, source_target_pairs={{0,1},{1,0},{2,3},{3,2},{4,5},{5,4},{6,7},{7,6},{8,9},{9,8},{10,11... | collective-permute-start | bytes 1572872 | tf_op jit(solution)/shard_map/ppermute | solution.py:59
  162.4 15.9 %all-to-all-start.3 = ((bf16[16,16,512]{2,1,0:T(8,128)(2,1)}), bf16[16,16,512]{2,1,0:T(8,128)(2,1)S(1)}, u32[]{:S(2)}, u32[]{:S(2)}) async-start(bf16[16,16,512]{2,1,0:T(8,128)(2,1)} %get-tuple-element.86), calls=%async_computation.3 | async-start | bytes 524288 | tf_op jit(solution)/shard_map/all_to_all | solution.py:450
  172.6 24.9 %collective-permute-start.26 = (bf16[2,512,512]{2,1,0:T(8,128)(2,1)S(1)}, bf16[2,512,512]{2,1,0:T(8,128)(2,1)S(1)}, u32[]{:S(2)}, u32[]{:S(2)}) collective-permute-start(bf16[2,512,512]{2,1,0:T(8,128)(2,1)S(1)} %chunks.17), channel_id=1, source_target_pairs={{0,2},{1,7},{2,4},{3,1},{4,6},{5,3},{6,0},{7,5},{8,10},{9,15},{10,... | collective-permute-start | bytes 3145736 | tf_op jit(solution)/shard_map/ppermute | solution.py:59
  185.3 2.6 collective-permute-start.23
  186.4 2.3 collective-permute-start.24
  191.6 20.8 %collective-permute-start.31 = (bf16[2,512,512]{2,1,0:T(8,128)(2,1)S(1)}, bf16[2,512,512]{2,1,0:T(8,128)(2,1)S(1)}, u32[]{:S(2)}, u32[]{:S(2)}) collective-permute-start(bf16[2,512,512]{2,1,0:T(8,128)(2,1)S(1)} %chunks.19), channel_id=1, source_target_pairs={{0,2},{1,7},{2,4},{3,1},{4,6},{5,3},{6,0},{7,5},{8,10},{9,15},{10,... | collective-permute-start | bytes 3145736 | tf_op jit(solution)/shard_map/ppermute | solution.py:59
  196.9 2.0 collective-permute-start.25
  197.0 2.6 collective-permute-start.27
  197.5 2.9 %collective-permute-start.28 = (bf16[1,512,512]{2,1,0:T(8,128)(2,1)S(1)}, bf16[1,512,512]{2,1,0:T(8,128)(2,1)S(1)}, u32[]{:S(2)}, u32[]{:S(2)}) collective-permute-start(bf16[1,512,512]{2,1,0:T(8,128)(2,1)S(1)} %get-tuple-element.95), channel_id=1, source_target_pairs={{0,1},{1,0},{2,3},{3,2},{4,5},{5,4},{6,7},{7,6},{8,9},{9,8},{10,11... | collective-permute-start | bytes 1572872 | tf_op jit(solution)/shard_map/ppermute | solution.py:59
  197.6 3.6 %collective-permute-start.29 = (bf16[1,512,512]{2,1,0:T(8,128)(2,1)S(1)}, bf16[1,512,512]{2,1,0:T(8,128)(2,1)S(1)}, u32[]{:S(2)}, u32[]{:S(2)}) collective-permute-start(bf16[1,512,512]{2,1,0:T(8,128)(2,1)S(1)} %get-tuple-element.96), channel_id=1, source_target_pairs={{0,1},{1,0},{2,3},{3,2},{4,5},{5,4},{6,7},{7,6},{8,9},{9,8},{10,11... | collective-permute-start | bytes 1572872 | tf_op jit(solution)/shard_map/ppermute | solution.py:59
  205.4 15.5 %collective-permute-start.35 = (bf16[2,512,512]{2,1,0:T(8,128)(2,1)S(1)}, bf16[2,512,512]{2,1,0:T(8,128)(2,1)S(1)}, u32[]{:S(2)}, u32[]{:S(2)}) collective-permute-start(bf16[2,512,512]{2,1,0:T(8,128)(2,1)S(1)} %get-tuple-element.97), channel_id=1, source_target_pairs={{0,2},{1,7},{2,4},{3,1},{4,6},{5,3},{6,0},{7,5},{8,10},{9,15},{10,... | collective-permute-start | bytes 3145736 | tf_op jit(solution)/shard_map/ppermute | solution.py:59
  211.8 2.6 collective-permute-start.32
  212.3 2.9 %collective-permute-start.33 = (bf16[1,512,512]{2,1,0:T(8,128)(2,1)S(1)}, bf16[1,512,512]{2,1,0:T(8,128)(2,1)S(1)}, u32[]{:S(2)}, u32[]{:S(2)}) collective-permute-start(bf16[1,512,512]{2,1,0:T(8,128)(2,1)S(1)} %get-tuple-element.102), channel_id=1, source_target_pairs={{0,1},{1,0},{2,3},{3,2},{4,5},{5,4},{6,7},{7,6},{8,9},{9,8},{10,11... | collective-permute-start | bytes 1572872 | tf_op jit(solution)/shard_map/ppermute | solution.py:59
  212.4 3.6 %collective-permute-start.34 = (bf16[1,512,512]{2,1,0:T(8,128)(2,1)S(1)}, bf16[1,512,512]{2,1,0:T(8,128)(2,1)S(1)}, u32[]{:S(2)}, u32[]{:S(2)}) collective-permute-start(bf16[1,512,512]{2,1,0:T(8,128)(2,1)S(1)} %get-tuple-element.103), channel_id=1, source_target_pairs={{0,1},{1,0},{2,3},{3,2},{4,5},{5,4},{6,7},{7,6},{8,9},{9,8},{10,11... | collective-permute-start | bytes 1572872 | tf_op jit(solution)/shard_map/ppermute | solution.py:59
  220.2 14.0 %collective-permute-start.37 = (bf16[2,512,512]{2,1,0:T(8,128)(2,1)S(1)}, bf16[2,512,512]{2,1,0:T(8,128)(2,1)S(1)}, u32[]{:S(2)}, u32[]{:S(2)}) collective-permute-start(bf16[2,512,512]{2,1,0:T(8,128)(2,1)S(1)} %get-tuple-element.104), channel_id=1, source_target_pairs={{0,2},{1,7},{2,4},{3,1},{4,6},{5,3},{6,0},{7,5},{8,10},{9,15},{10,... | collective-permute-start | bytes 3145736 | tf_op jit(solution)/shard_map/ppermute | solution.py:59
  222.6 2.5 collective-permute-start.36
  223.4 22.1 %collective-permute-start.39 = (bf16[2,512,512]{2,1,0:T(8,128)(2,1)S(1)}, bf16[2,512,512]{2,1,0:T(8,128)(2,1)S(1)}, u32[]{:S(2)}, u32[]{:S(2)}) collective-permute-start(bf16[2,512,512]{2,1,0:T(8,128)(2,1)S(1)} %get-tuple-element.110), channel_id=1, source_target_pairs={{0,2},{1,7},{2,4},{3,1},{4,6},{5,3},{6,0},{7,5},{8,10},{9,15},{10,... | collective-permute-start | bytes 3145736 | tf_op jit(solution)/shard_map/ppermute | solution.py:59
  235.9 3.8 %collective-permute-start.38 = (bf16[1,512,512]{2,1,0:T(8,128)(2,1)S(1)}, bf16[1,512,512]{2,1,0:T(8,128)(2,1)S(1)}, u32[]{:S(2)}, u32[]{:S(2)}) collective-permute-start(bf16[1,512,512]{2,1,0:T(8,128)(2,1)S(1)} %chunks.26), channel_id=1, source_target_pairs={{0,1},{1,0},{2,3},{3,2},{4,5},{5,4},{6,7},{7,6},{8,9},{9,8},{10,11... | collective-permute-start | bytes 1572872 | tf_op jit(solution)/shard_map/ppermute | solution.py:59
  238.2 18.5 %collective-permute-start.42 = (bf16[2,512,512]{2,1,0:T(8,128)(2,1)S(1)}, bf16[2,512,512]{2,1,0:T(8,128)(2,1)S(1)}, u32[]{:S(2)}, u32[]{:S(2)}) collective-permute-start(bf16[2,512,512]{2,1,0:T(8,128)(2,1)S(1)} %get-tuple-element.113), channel_id=1, source_target_pairs={{0,2},{1,7},{2,4},{3,1},{4,6},{5,3},{6,0},{7,5},{8,10},{9,15},{10,... | collective-permute-start | bytes 3145736 | tf_op jit(solution)/shard_map/ppermute | solution.py:59
  238.2 14.9 %collective-permute-start.41 = (bf16[1,512,512]{2,1,0:T(8,128)(2,1)S(1)}, bf16[1,512,512]{2,1,0:T(8,128)(2,1)S(1)}, u32[]{:S(2)}, u32[]{:S(2)}) collective-permute-start(bf16[1,512,512]{2,1,0:T(8,128)(2,1)S(1)} %chunks.25), channel_id=1, source_target_pairs={{0,8},{1,9},{2,10},{3,11},{4,12},{5,13},{6,14},{7,15},{8,0},{9,1},... | collective-permute-start | bytes 1572872 | tf_op jit(solution)/shard_map/ppermute | solution.py:59
  247.2 5.9 %collective-permute-start.40 = (bf16[1,512,512]{2,1,0:T(8,128)(2,1)S(1)}, bf16[1,512,512]{2,1,0:T(8,128)(2,1)S(1)}, u32[]{:S(2)}, u32[]{:S(2)}) collective-permute-start(bf16[1,512,512]{2,1,0:T(8,128)(2,1)S(1)} %chunks.28), channel_id=1, source_target_pairs={{0,1},{1,0},{2,3},{3,2},{4,5},{5,4},{6,7},{7,6},{8,9},{9,8},{10,11... | collective-permute-start | bytes 1572872 | tf_op jit(solution)/shard_map/ppermute | solution.py:59
  249.4 15.0 %collective-permute-start.44 = (bf16[1,512,512]{2,1,0:T(8,128)(2,1)S(1)}, bf16[1,512,512]{2,1,0:T(8,128)(2,1)S(1)}, u32[]{:S(2)}, u32[]{:S(2)}) collective-permute-start(bf16[1,512,512]{2,1,0:T(8,128)(2,1)S(1)} %chunks.27), channel_id=1, source_target_pairs={{0,8},{1,9},{2,10},{3,11},{4,12},{5,13},{6,14},{7,15},{8,0},{9,1},... | collective-permute-start | bytes 1572872 | tf_op jit(solution)/shard_map/ppermute | solution.py:59
  258.4 6.0 %collective-permute-start.43 = (bf16[1,512,512]{2,1,0:T(8,128)(2,1)S(1)}, bf16[1,512,512]{2,1,0:T(8,128)(2,1)S(1)}, u32[]{:S(2)}, u32[]{:S(2)}) collective-permute-start(bf16[1,512,512]{2,1,0:T(8,128)(2,1)S(1)} %chunks.30), channel_id=1, source_target_pairs={{0,1},{1,0},{2,3},{3,2},{4,5},{5,4},{6,7},{7,6},{8,9},{9,8},{10,11... | collective-permute-start | bytes 1572872 | tf_op jit(solution)/shard_map/ppermute | solution.py:59
  (17 other events, 40.4 us)
